TPU v7x, 256 devices: a whole 4x4x8 slice. The times are simulated.
256 devices in a mesh: outer: 16 (over z, y_lo), dev: 16 (over x, y_hi, core).
Axes of the slice: x: 4, y: 4 (y_hi: 2, y_lo: 2; y = y_hi * 2 + y_lo), z: 8, core: 2. Of those that a mesh axis runs over, the one named last changes fastest.
Arguments:
- partials: bfloat16 [256, 8192, 256], P(('outer', 'dev')), may hold values from -6 to 6
- p_old: bfloat16 [8192, 1024], P('dev'), may hold values from -0.0625 to 0.0625
- p_new: bfloat16 [8192, 1024], P('dev'), may hold values from -0.0625 to 0.0625
- weight: float32 [8192, 256], P('dev'), may hold values from -4 to 4
- m_old: float32 [1024, 256], P('dev'), may hold values from -96 to 96
- v_old: float32 [1024, 256], P('dev'), may hold values from 32 to 1280
Outputs:
- new_weight: float32 [8192, 256], P('dev')
- m_new: float32 [1024, 256], P('dev')
- v_new: float32 [1024, 256], P('dev')
All inputs are finite; a program needn't handle non-finite values.
Results may differ from a plain program's by a relative error of at most 0.0012.
Values may be sent and summed in bfloat16 or wider, within the bound.
No kernel may reach another device: no remote copies, remote signals or barrier semaphores. Data moves between devices by JAX's collectives and lax.ppermute only.
A program may use at most 128 MiB of HBM per device.

v0:
```python
import jax
import jax.numpy as jnp
from jax import lax
from jax.sharding import PartitionSpec as P

beta_mean = 0.9
beta_square = 0.95
bias_mean = 0.9999734386011124
bias_square = 0.9940794707796659
adam_epsilon = 1e-08
step_scale = 0.5


def on_device(partials, p_old, p_new, weight, m_old, v_old):
    local_grad = partials[0].astype(jnp.float32)
    grad_cols = lax.psum_scatter(local_grad, "dev", scatter_dimension=1, tiled=True)
    proj_cols = jnp.dot(
        lax.all_gather(p_new, "dev", axis=0, tiled=True).astype(jnp.float32).T,
        grad_cols,
        precision=lax.Precision.HIGHEST,
    )
    proj_cols = lax.psum(proj_cols, "outer")
    projected = lax.all_to_all(proj_cols, "dev", split_axis=0, concat_axis=1, tiled=True)
    columns = p_new
    margin_rows = lax.psum_scatter(
        jnp.dot(columns.T, p_old, preferred_element_type=jnp.float32),
        "dev",
        scatter_dimension=0,
        tiled=True,
    )
    first_piece = lax.all_gather(m_old, "dev", axis=0, tiled=True)
    second_piece = lax.all_gather(v_old, "dev", axis=0, tiled=True)
    first = jnp.dot(margin_rows, first_piece, precision=lax.Precision.HIGHEST)
    second = jnp.dot(margin_rows * margin_rows, second_piece, precision=lax.Precision.HIGHEST)
    m_new = beta_mean * first + (1.0 - beta_mean) * projected
    v_new = beta_square * second + (1.0 - beta_square) * projected * projected
    direction = (m_new / bias_mean / (jnp.sqrt(v_new / bias_square) + adam_epsilon)).astype(
        jnp.bfloat16
    )
    columns = p_new
    update = jnp.dot(
        columns,
        lax.all_gather(direction, "dev", axis=0, tiled=True),
        preferred_element_type=jnp.float32,
    )
    new_weight = weight - step_scale * update
    return (new_weight, m_new, v_new)


def solution(mesh):
    in_specs = (
        P(("outer", "dev"), None, None),
        P("dev", None),
        P("dev", None),
        P("dev", None),
        P("dev", None),
        P("dev", None),
    )
    out_specs = (P("dev", None), P("dev", None), P("dev", None))
    return jax.shard_map(
        on_device, mesh=mesh, in_specs=in_specs, out_specs=out_specs, check_vma=False
    )
```

profile of v0, /device:TPU:1, one launch (start us, length us, event | category | flops | bytes accessed | tf_op | source)
XLA Modules:
  0.0 627.6 jit_solution(10560370040956481151)
XLA Ops:
  7.2 0.0 copy-start
  7.2 0.0 reduce-scatter.7.cloned.1.call-start
  7.2 6.2 bitcast_convert_fusion
  13.4 8.9 %copy.24 = f32[8192,256]{0,1:T(8,128)} copy(f32[8192,256]{1,0:T(8,128)} %bitcast_convert_fusion) | data formatting | bytes 16777216
  22.3 0.0 reduce-scatter.7.cloned.1.call-update
  22.3 0.0 all-gather.6.cloned.1.call-start
  22.4 0.7 all-gather.6.cloned.1.call-update
  23.1 0.0 copy-start.1
  23.1 0.0 all-reduce.2.cloned.1.call-start
  23.1 112.1 %reduce-scatter.7.cloned.1.call-done = f32[16,8192]{1,0:T(8,128)} async-done(((f32[256,8192]{1,0:T(8,128)}), f32[16,8192]{1,0:T(8,128)}) %reduce-scatter.7.cloned.1.call-update) | async-done | bytes 524304
  135.2 118.6 %all-gather.6.cloned.1.call-done = bf16[8192,1024]{1,0:T(8,128)(2,1)} async-done(((bf16[512,1024]{1,0:T(8,128)(2,1)}), bf16[8192,1024]{1,0:T(8,128)(2,1)}) %all-gather.6.cloned.1.call-update) | async-done | bytes 16777232 | tf_op jit(solution)/shard_map/all_gather | solution.py:18
  253.8 10.2 %fusion.4 = f32[1024,16]{0,1:T(8,128)S(1)} fusion(bf16[8192,1024]{1,0:T(8,128)(2,1)} %all-gather.6.cloned.1.call-done, f32[16,8192]{1,0:T(8,128)} %reduce-scatter.7.cloned.1.call-done), kind=kOutput, calls=%fused_computation.8 | convolution fusion | flops 1610612736 | bytes 17367040 | tf_op jit(solution)/shard_map/dot_general | solution.py:17
  264.1 0.0 copy-start.2
  264.1 0.1 all_to_all.14
  264.1 0.7 copy.18
  264.9 0.0 all-reduce.2.cloned.1.call-update
  264.9 0.0 all-gather.4.cloned.1.call-start
  264.9 0.5 all-gather.4.cloned.1.call-update
  265.5 0.0 reduce-scatter.5.cloned.1.call-start
  265.5 0.0 copy-done
  265.5 0.0 copy-done.1
  265.5 3.2 fusion.7
  268.8 0.0 reduce-scatter.5.cloned.1.call-update
  268.8 0.0 all-gather.8.cloned.1.call-start
  268.8 0.5 all-gather.8.cloned.1.call-update
  269.4 118.0 %all-reduce.2.cloned.1.call-done = f32[16,64,16]{1,2,0:T(8,128)} async-done(((f32[16,64,16]{1,2,0:T(8,128)}), f32[16,64,16]{1,2,0:T(8,128)}) %all-reduce.2.cloned.1.call-update) | async-done | bytes 65552 | tf_op jit(solution)/shard_map/psum | solution.py:22
  387.4 1.7 reshape.14
  389.0 17.0 %all-to-all-start = ((f32[16,1,1024]{2,1,0:T(1,128)}), f32[16,1,1024]{2,1,0:T(1,128)S(1)}, u32[]{:S(2)}, u32[]{:S(2)}) async-start(f32[16,1,1024]{2,1,0:T(1,128)} %reshape.14), calls=%async_computation.1 | async-start | bytes 131072 | tf_op jit(solution)/shard_map/all_to_all | solution.py:23
  406.0 0.0 copy-done.2
  406.0 0.2 copy.22
  406.2 7.2 %all-to-all-done = f32[16,1,1024]{2,1,0:T(1,128)S(1)} async-done(((f32[16,1,1024]{2,1,0:T(1,128)}), f32[16,1,1024]{2,1,0:T(1,128)S(1)}, u32[]{:S(2)}, u32[]{:S(2)}) %all-to-all-start) | async-done | bytes 65568 | tf_op jit(solution)/shard_map/all_to_all | solution.py:23
  413.4 0.5 broadcast.4
  413.9 0.8 reduce
  414.7 0.1 reshape.15
  414.8 0.1 copy.19
  414.9 35.6 %all-gather.4.cloned.1.call-done = f32[1024,256]{1,0:T(8,128)} async-done(((f32[64,256]{1,0:T(8,128)}), f32[1024,256]{1,0:T(8,128)}) %all-gather.4.cloned.1.call-update) | async-done | bytes 1048592 | tf_op jit(solution)/shard_map/all_gather | solution.py:31
  450.5 89.9 %reduce-scatter.5.cloned.1.call-done = f32[64,1024]{1,0:T(8,128)} async-done(((f32[1024,1024]{1,0:T(8,128)}), f32[64,1024]{1,0:T(8,128)}) %reduce-scatter.5.cloned.1.call-update) | async-done | bytes 262160 | tf_op jit(solution)/shard_map/reduce_scatter | solution.py:25
  540.3 1.9 fusion.3
  542.3 0.0 copy-start.3
  542.3 51.5 %all-gather.8.cloned.1.call-done = f32[1024,256]{1,0:T(8,128)} async-done(((f32[64,256]{1,0:T(8,128)}), f32[1024,256]{1,0:T(8,128)}) %all-gather.8.cloned.1.call-update) | async-done | bytes 1048592 | tf_op jit(solution)/shard_map/all_gather | solution.py:32
  593.8 2.6 divide_convert_fusion
  596.4 22.9 %all_gather.15 = bf16[1024,256]{1,0:T(8,128)(2,1)S(1)} all-gather(bf16[64,256]{1,0:T(8,128)(2,1)S(1)} %get-tuple-element.12), channel_id=1, replica_groups=mesh['outer'=16,'dev'=16] {'dev'}, dimensions={0}, use_global_device_ids=true | all-gather | bytes 557056 | tf_op jit(solution)/shard_map/all_gather | solution.py:43
  619.3 0.5 fusion.1
  619.8 1.0 copy.23
  620.8 0.0 copy-done.3
Async XLA Ops:
  7.2 258.3 %copy-start = (bf16[512,1024]{1,0:T(8,128)(2,1)S(1)}, bf16[512,1024]{1,0:T(8,128)(2,1)}, u32[]{:S(2)}) copy-start(bf16[512,1024]{1,0:T(8,128)(2,1)} %param.7) | copy-start | bytes 3145732
  7.2 128.1 %reduce-scatter.7.cloned.1.call-start = ((), (), s32[]{:S(2)}) async-start(), calls=%async_computation.8 | async-start | bytes 8912896
  22.3 231.5 %all-gather.6.cloned.1.call-start = ((), (), s32[]{:S(2)}) async-start(), calls=%async_computation.5 | async-start | bytes 17825792 | tf_op jit(solution)/shard_map/all_gather | solution.py:18
  23.1 242.4 %copy-start.1 = (bf16[512,1024]{1,0:T(8,128)(2,1)S(1)}, bf16[512,1024]{1,0:T(8,128)(2,1)}, u32[]{:S(2)}) copy-start(bf16[512,1024]{1,0:T(8,128)(2,1)} %param.8) | copy-start | bytes 3145732
  23.1 364.3 %all-reduce.2.cloned.1.call-start = ((), (), s32[]{:S(2)}) async-start(), calls=%async_computation.6 | async-start | bytes 262144 | tf_op jit(solution)/shard_map/psum | solution.py:22
  264.1 142.0 %copy-start.2 = (f32[512,256]{1,0:T(8,128)S(1)}, f32[512,256]{1,0:T(8,128)}, u32[]{:S(2)}) copy-start(f32[512,256]{1,0:T(8,128)} %param.9) | copy-start | bytes 1572868
  264.9 185.6 %all-gather.4.cloned.1.call-start = ((), (), s32[]{:S(2)}) async-start(), calls=%async_computation.4 | async-start | bytes 1114112 | tf_op jit(solution)/shard_map/all_gather | solution.py:31
  265.5 274.9 %reduce-scatter.5.cloned.1.call-start = ((), (), s32[]{:S(2)}) async-start(), calls=%async_computation.3 | async-start | bytes 4456448 | tf_op jit(solution)/shard_map/reduce_scatter | solution.py:25
  268.8 325.0 %all-gather.8.cloned.1.call-start = ((), (), s32[]{:S(2)}) async-start(), calls=%async_computation.7 | async-start | bytes 1114112 | tf_op jit(solution)/shard_map/all_gather | solution.py:32
  389.0 24.4 %all-to-all-start = ((f32[16,1,1024]{2,1,0:T(1,128)}), f32[16,1,1024]{2,1,0:T(1,128)S(1)}, u32[]{:S(2)}, u32[]{:S(2)}) async-start(f32[16,1,1024]{2,1,0:T(1,128)} %reshape.14), calls=%async_computation.1 | async-start | bytes 131072 | tf_op jit(solution)/shard_map/all_to_all | solution.py:23
  542.3 78.5 %copy-start.3 = (f32[64,256]{1,0:T(8,128)}, f32[64,256]{1,0:T(8,128)S(1)}, u32[]{:S(2)}) copy-start(f32[64,256]{1,0:T(8,128)S(1)} %fusion.3) | copy-start | bytes 196612
Sparse Core Ops, SparseCore 0:
  22.5 112.7 reduce-scatter.6
  137.9 115.8 all-gather.5
  265.0 122.3 all-reduce.1
  390.3 60.1 all-gather.3
  455.3 85.0 reduce-scatter.4
  542.9 50.8 all-gather.7
where the time goes:
time: 628 us
  waiting for transfers between devices  535 us (85%)
  blocking collectives  22.9 us (4%)
  matrix products  18.5 us (3%)
  starting transfers between devices  17.2 us (3%)
  between operations  14.2 us (2%)
  local copies, waits for them, and re-layouts  13.3 us (2%)
  other arithmetic  6.96 us (1%)
    all_gather x1, waiting for transfers between devices, on_device(): lax.all_gather(p_new, 'dev', axis=0, tiled=True).astype(jnp.float32)  119 us
    psum x1, waiting for transfers between devices, on_device(): proj_cols = lax.psum(proj_cols, 'outer')  118 us
    unnamed x7, waiting for transfers between devices  114 us
    reduce_scatter x1, waiting for transfers between devices, on_device(): lax.psum_scatter(jnp.dot(columns.T, p_old, preferred_element_type=jnp.flo...  89.9 us
    all_gather x1, waiting for transfers between devices, on_device(): second_piece = lax.all_gather(v_old, 'dev', axis=0, tiled=True)  51.5 us
    all_gather x1, waiting for transfers between devices, on_device(): first_piece = lax.all_gather(m_old, 'dev', axis=0, tiled=True)  35.6 us
    all_gather x1, blocking collectives, on_device(): lax.all_gather(direction, 'dev', axis=0, tiled=True)  22.9 us
    all_to_all x1, starting transfers between devices, on_device(): lax.all_to_all(proj_cols, 'dev', split_axis=0, concat_axis=1, tiled=True)  17 us
  transfers between devices with their start and end apart: 7, of which 7 were waited for; matrix products, arithmetic and copies ran while one was open for 1% of the time, Pallas kernels for 0%

commit v1 on v0

v1 whole, which is shorter than its diff:
```python
import jax
import jax.numpy as jnp
from jax import lax
from jax.sharding import Mesh, PartitionSpec as P

beta_mean = 0.9
beta_square = 0.95
bias_mean = 0.9999734386011124
bias_square = 0.9940794707796659
adam_epsilon = 1e-08
step_scale = 0.5

AXES = ("z", "yl", "x", "yh", "core")
SIZES = (8, 2, 4, 2, 2)
OUTER = ("z", "yl")
DEV = ("x", "yh", "core")
PLANE = ("x", "yh", "yl")
PAIRS = ("x", "yh")
SCALE = 4096.0


def swap(value, axis, bit, size):
    return lax.ppermute(value, axis, [(i, i ^ bit) for i in range(size)])


def cut(value, at, extent, axis):
    return lax.dynamic_slice_in_dim(value, at * extent, extent, axis)


def pieces(value):
    high = lax.reduce_precision(value, 8, 7)
    rest = value - high
    mid = lax.reduce_precision(rest, 8, 7)
    low = rest - mid
    return jnp.concatenate([high, mid, low], axis=1).astype(jnp.bfloat16)


def on_device(partials, p_old, p_new, weight, m_old, v_old):
    core = lax.axis_index("core")
    z, yl, yh, x = (lax.axis_index(name) for name in ("z", "yl", "yh", "x"))
    f32 = jnp.float32

    grad = partials[0]
    theirs = swap(cut(grad, 1 - core, 128, 1), "core", 1, 2)
    ours = cut(grad, core, 128, 1)
    chip_sum = ((ours.astype(f32) + theirs.astype(f32)) * SCALE).astype(jnp.float16)
    rows = lax.all_to_all(chip_sum.reshape(8, 1024, 128), PAIRS, 0, 0, tiled=True)

    p_other = swap(p_new, "core", 1, 2)

    moments = jnp.stack([m_old, v_old])
    moments_in = swap(cut(moments, 1 - core, 128, 2), "core", 1, 2)
    moments_own = cut(moments, core, 128, 2)
    moments = jnp.where(
        core == 0,
        jnp.concatenate([moments_own, moments_in], axis=1),
        jnp.concatenate([moments_in, moments_own], axis=1),
    )
    turn = [(a * 8 + b, b * 8 + a) for a in range(8) for b in range(8)]
    moments = lax.ppermute(moments, ("z", "x", "yh"), turn)

    p_rank = lax.dynamic_index_in_dim(p_new.reshape(512, 8, 2, 64), yl, 2, keepdims=False)
    margin = jnp.dot(
        p_rank.reshape(512, 512).T, cut(p_old, z, 128, 1), preferred_element_type=f32
    )
    margin = margin + swap(margin, "core", 1, 2)
    margin = margin.reshape(2, 2, 2, 64, 128)
    hi, lo = x // 2, x % 2

    def halve(value, place, axis, bit, size):
        keep = lax.dynamic_index_in_dim(value, place, 0, keepdims=False)
        give = lax.dynamic_index_in_dim(value, 1 - place, 0, keepdims=False)
        return keep + swap(give, axis, bit, size)

    margin = halve(margin, hi, "x", 2, 4)
    margin = halve(margin, lo, "x", 1, 4)
    margin = halve(margin, yh, "yh", 1, 2)
    first = jnp.dot(margin, moments[0], precision=lax.Precision.HIGHEST)
    second = jnp.dot(margin * margin, moments[1], precision=lax.Precision.HIGHEST)
    rotated = jnp.stack([first, second])
    for bit in (1, 2, 4):
        rotated = rotated + swap(rotated, "z", bit, 8)

    grad_rows = jnp.sum(rows.astype(f32), axis=0) * (1.0 / SCALE)
    split = pieces(grad_rows)
    across = (((0,), (0,)), ((), ()))
    terms = lax.dot_general(
        p_new, cut(split, core, 512, 0), across, preferred_element_type=f32
    ) + lax.dot_general(
        p_other, cut(split, 1 - core, 512, 0), across, preferred_element_type=f32
    )
    projected = terms[:, :128] + terms[:, 128:256] + terms[:, 256:]
    projected = lax.all_to_all(projected.reshape(16, 64, 128), PLANE, 0, 0, tiled=True)
    projected = jnp.sum(projected, axis=0)
    for bit in (1, 2, 4):
        projected = projected + swap(projected, "z", bit, 8)

    m_new = beta_mean * rotated[0] + (1.0 - beta_mean) * projected
    v_new = beta_square * rotated[1] + (1.0 - beta_square) * projected * projected
    direction = (m_new / bias_mean / (jnp.sqrt(v_new / bias_square) + adam_epsilon)).astype(
        jnp.bfloat16
    )

    def sides(own, other, axis):
        return jnp.where(
            core == 0,
            jnp.concatenate([own, other], axis=axis),
            jnp.concatenate([other, own], axis=axis),
        )

    spread = jnp.broadcast_to(direction[None], (16, 64, 128))
    mine = lax.all_to_all(spread, PLANE, 0, 0, tiled=True).reshape(1024, 128)
    other = swap(mine, "core", 1, 2)
    update = sides(
        jnp.dot(p_new, mine, preferred_element_type=f32),
        jnp.dot(p_new, other, preferred_element_type=f32),
        1,
    )
    new_weight = weight - step_scale * update

    made = jnp.stack([m_new, v_new])
    made = sides(made, swap(made, "core", 1, 2), 2)
    made = jnp.where(core == yl, made, swap(made, "yl", 1, 2))
    return (new_weight, made[0], made[1])


def solution(mesh):
    fine = Mesh(mesh.devices.reshape(SIZES), AXES)
    in_specs = (
        P(OUTER + DEV, None, None),
        P(DEV, None),
        P(DEV, None),
        P(DEV, None),
        P(DEV, None),
        P(DEV, None),
    )
    out_specs = (P(DEV, None), P(DEV, None), P(DEV, None))
    return jax.shard_map(
        on_device, mesh=fine, in_specs=in_specs, out_specs=out_specs, check_vma=False
    )
```

time: 628 us -> 140 us (0.22)
  waiting for transfers between devices: 535 us -> 55.7 us
  starting transfers between devices: 17.2 us -> 62.4 us
  blocking collectives: 22.9 us -> 0 us
  matrix products: 18.5 us -> 2.84 us
  between operations: 14.2 us -> 0.96 us
    all_gather x3 -> x0, waiting for transfers between devices: 206 us -> none  [the longest x1 119 us: on_device(): lax.all_gather(p_new, 'dev', axis=0, tiled=True).astype(jnp.float32)]
    psum x1 -> x0, waiting for transfers between devices: 118 us -> none  [on_device(): proj_cols = lax.psum(proj_cols, 'outer')]
    unnamed x7 -> x0, waiting for transfers between devices: 114 us -> none
    reduce_scatter x1 -> x0, waiting for transfers between devices: 89.9 us -> none  [on_device(): lax.psum_scatter(jnp.dot(columns.T, p_old, preferred_element_type=jnp.flo...]
    ppermute x0 -> x17, waiting for transfers between devices: none -> 43.2 us  [the longest x16 43.2 us: swap(): return lax.ppermute(value, axis, [(i, i ^ bit) for i in range(size)])]
    ppermute x0 -> x17, starting transfers between devices: none -> 32.9 us  [the longest x16 31.3 us: swap(): return lax.ppermute(value, axis, [(i, i ^ bit) for i in range(size)])]
    all_gather x1 -> x0, blocking collectives: 22.9 us -> none  [on_device(): lax.all_gather(direction, 'dev', axis=0, tiled=True)]
    dot_general x5 -> x7, matrix products: 18.5 us -> 2.84 us  [the longest x1 0.6 us: on_device(): lax.dot_general(p_other, cut(split, 1 - core, 512, 0), across, preferred_...]
  transfers between devices with their start and end apart: 7 -> 20, of which waited for: 7 -> 12; matrix products, arithmetic and copies ran while one was open for 1% -> 7% of each run, Pallas kernels for 0% -> 0%
where the time goes in v1:
time: 140 us
  starting transfers between devices  62.4 us (45%)
  waiting for transfers between devices  55.7 us (40%)
  other arithmetic  9.93 us (7%)
  local copies, waits for them, and re-layouts  8.06 us (6%)
  matrix products  2.84 us (2%)
    ppermute x16, waiting for transfers between devices, swap(): return lax.ppermute(value, axis, [(i, i ^ bit) for i in range(size)])  43.2 us
    ppermute x16, starting transfers between devices, swap(): return lax.ppermute(value, axis, [(i, i ^ bit) for i in range(size)])  31.3 us
    all_to_all x1, starting transfers between devices, on_device(): lax.all_to_all(projected.reshape(16, 64, 128), PLANE, 0, 0, tiled=True)  17.4 us
    all_to_all x1, starting transfers between devices, on_device(): mine = lax.all_to_all(spread, PLANE, 0, 0, tiled=True).reshape(1024, 128)  7.06 us
    all_to_all x1, waiting for transfers between devices, on_device(): mine = lax.all_to_all(spread, PLANE, 0, 0, tiled=True).reshape(1024, 128)  6.77 us
    all_to_all x1, waiting for transfers between devices, on_device(): lax.all_to_all(projected.reshape(16, 64, 128), PLANE, 0, 0, tiled=True)  5.67 us
    all_to_all x1, starting transfers between devices, on_device(): lax.all_to_all(chip_sum.reshape(8, 1024, 128), PAIRS, 0, 0, tiled=True)  5.05 us
    convert_element_type x1, other arithmetic, on_device(): ((ours.astype(f32) + theirs.astype(f32)) * SCALE).astype(jnp.float16)  4.37 us
  transfers between devices with their start and end apart: 20, of which 12 were waited for; matrix products, arithmetic and copies ran while one was open for 7% of the time, Pallas kernels for 0%

profile of v1, /device:TPU:1, one launch (start us, length us, event | category | flops | bytes accessed | tf_op | source)
XLA Modules:
  0.0 139.8 jit_solution(17975327720045522099)
XLA Ops:
  0.7 3.1 %dynamic-slice_bitcast_fusion = bf16[8192,128]{1,0:T(8,128)(2,1)} fusion(bf16[1,8192,256]{2,1,0:T(8,128)(2,1)} %param.6, s32[]{:T(128)S(6)} %select_n.96), kind=kLoop, calls=%fused_computation.4 | loop fusion | bytes 4194308 | tf_op jit(solution)/shard_map/dynamic_slice | solution.py:27
  3.8 3.2 %collective-permute-start.9 = (bf16[8192,128]{1,0:T(8,128)(2,1)}, bf16[8192,128]{1,0:T(8,128)(2,1)}, u32[]{:S(2)}, u32[]{:S(2)}) collective-permute-start(bf16[8192,128]{1,0:T(8,128)(2,1)} %dynamic-slice_bitcast_fusion), channel_id=1, source_target_pairs={{0,1},{1,0},{2,3},{3,2},{4,5},{5,4},{6,7},{7,6},{8,9},{9,8},{10,11... | collective-permute-start | bytes 6291464 | tf_op jit(solution)/shard_map/ppermute | solution.py:23
  7.0 4.1 %collective-permute-done.9 = bf16[8192,128]{1,0:T(8,128)(2,1)} collective-permute-done((bf16[8192,128]{1,0:T(8,128)(2,1)}, bf16[8192,128]{1,0:T(8,128)(2,1)}, u32[]{:S(2)}, u32[]{:S(2)}) %collective-permute-start.9) | collective-permute-done | bytes 2097184 | tf_op jit(solution)/shard_map/ppermute | solution.py:23
  11.2 4.4 %fusion.1 = f16[8192,128]{1,0:T(8,128)(2,1)} fusion(bf16[8192,128]{1,0:T(8,128)(2,1)} %collective-permute-done.9, bf16[1,8192,256]{2,1,0:T(8,128)(2,1)} %param.6, s32[]{:T(128)S(6)} %select_n.95), kind=kLoop, calls=%fused_computation.2 | loop fusion | flops 5242880 | bytes 6291460 | tf_op jit(solution)/shard_map/convert_element_type | solution.py:46
  15.5 5.0 %all-to-all-start = ((f16[8,1024,128]{2,1,0:T(8,128)(2,1)}), f16[8,1024,128]{2,1,0:T(8,128)(2,1)}, u32[]{:S(2)}, u32[]{:S(2)}) async-start(f16[8,1024,128]{2,1,0:T(8,128)(2,1)} %bitcast.76), calls=%async_computation | async-start | bytes 4194304 | tf_op jit(solution)/shard_map/all_to_all | solution.py:47
  20.6 0.5 copy.11
  21.2 0.3 fusion.8
  21.5 0.7 collective-permute-start
  22.3 1.2 collective-permute-done
  23.5 0.7 dynamic-slice_bitcast_fusion.1
  24.2 3.2 %collective-permute-start.1 = (f32[2,2,64,128]{3,2,1,0:T(8,128)}, f32[2,2,64,128]{3,2,1,0:T(8,128)}, u32[]{:S(2)}, u32[]{:S(2)}) collective-permute-start(f32[2,2,64,128]{3,2,1,0:T(8,128)} %dynamic-slice_bitcast_fusion.1), channel_id=1, source_target_pairs={{0,8},{4,12},{8,0},{12,4},{1,9},{5,13},{9,1},{13,5},{2,10},{6,14},... | collective-permute-start | bytes 393224 | tf_op jit(solution)/shard_map/ppermute | solution.py:23
  27.4 0.7 collective-permute-start.10
  28.0 1.4 %fusion.11 = (f32[2,64,128]{2,1,0:T(8,128)S(1)}, f32[2,64,128]{2,1,0:T(8,128)}) fusion(s32[]{:T(128)S(6)} %select_n.95, f32[1,64,256]{2,1,0:T(8,128)S(1)} %bitcast.83, f32[1,64,256]{2,1,0:T(8,128)} %bitcast.84, s32[]{:T(128)S(6)} %select_n.96), kind=kLoop, calls=%fused_computation.35 | loop fusion | flops 32768 | bytes 262152 | tf_op jit(solution)/shard_map/stack | solution.py:51
  29.5 25.0 %collective-permute-done.1 = f32[2,2,64,128]{3,2,1,0:T(8,128)} collective-permute-done((f32[2,2,64,128]{3,2,1,0:T(8,128)}, f32[2,2,64,128]{3,2,1,0:T(8,128)}, u32[]{:S(2)}, u32[]{:S(2)}) %collective-permute-start.1) | collective-permute-done | bytes 131104 | tf_op jit(solution)/shard_map/ppermute | solution.py:23
  54.4 0.9 bitcast_add_fusion
  55.5 0.7 maximum_select_fusion.1
  56.2 1.6 %collective-permute-start.5 = (f32[2,128,128]{2,1,0:T(8,128)}, f32[2,128,128]{2,1,0:T(8,128)S(1)}, u32[]{:S(2)}, u32[]{:S(2)}) collective-permute-start(f32[2,128,128]{2,1,0:T(8,128)} %maximum_select_fusion.1), channel_id=1, source_target_pairs={{0,0},{2,32},{4,64},{6,96},{8,128},{10,160},{12,192},{14,224},{32,... | collective-permute-start | bytes 393224 | tf_op jit(solution)/shard_map/ppermute | solution.py:60
  57.7 0.9 collective-permute-done.2
  58.6 3.9 %collective-permute-start.3 = (f32[64,128]{1,0:T(8,128)S(1)}, f32[64,128]{1,0:T(8,128)S(1)}, u32[]{:S(2)}, u32[]{:S(2)}) collective-permute-start(f32[64,128]{1,0:T(8,128)S(1)} %dynamic-slice_bitcast_fusion.3), channel_id=1, source_target_pairs={{0,2},{2,0},{1,3},{3,1},{4,6},{6,4},{5,7},{7,5},{8,10},{10,8},{9,1... | collective-permute-start | bytes 98312 | tf_op jit(solution)/shard_map/ppermute | solution.py:23
  62.5 1.3 collective-permute-done.3
  63.8 0.2 convolution_bitcast_fusion.3
  64.0 1.9 %convert_reduce_fusion = f32[1024,128]{1,0:T(8,128)S(1)} fusion(f16[8,1024,128]{2,1,0:T(8,128)(2,1)} %all-to-all-done), kind=kLoop, calls=%fused_computation.3 | loop fusion | flops 1966080 | bytes 2621440 | tf_op jit(solution)/shard_map/reduce_sum | solution.py:84
  66.2 0.6 fusion.6
  66.8 0.6 add_bitcast_fusion
  67.6 1.0 copy.12
  68.6 17.4 %all-to-all-start.1 = ((f32[16,64,128]{2,1,0:T(8,128)}), f32[16,64,128]{2,1,0:T(8,128)S(1)}, u32[]{:S(2)}, u32[]{:S(2)}) async-start(f32[16,64,128]{2,1,0:T(8,128)} %bitcast.20), calls=%async_computation.1 | async-start | bytes 1048576 | tf_op jit(solution)/shard_map/all_to_all | solution.py:93
  85.9 0.2 convolution_bitcast_fusion.2
  86.2 3.1 %collective-permute-done.6 = f32[2,64,128]{2,1,0:T(8,128)S(1)} collective-permute-done((f32[2,64,128]{2,1,0:T(8,128)S(1)}, f32[2,64,128]{2,1,0:T(8,128)S(1)}, u32[]{:S(2)}, u32[]{:S(2)}) %collective-permute-start.6) | collective-permute-done | bytes 65568 | tf_op jit(solution)/shard_map/ppermute | solution.py:23
  89.3 0.9 collective-permute-start.7
  90.2 5.7 %all-to-all-done.1 = f32[16,64,128]{2,1,0:T(8,128)S(1)} async-done(((f32[16,64,128]{2,1,0:T(8,128)}), f32[16,64,128]{2,1,0:T(8,128)S(1)}, u32[]{:S(2)}, u32[]{:S(2)}) %all-to-all-start.1) | async-done | bytes 524320 | tf_op jit(solution)/shard_map/all_to_all | solution.py:93
  96.0 6.5 %collective-permute-start.8 = (f32[2,64,128]{2,1,0:T(8,128)S(1)}, f32[2,64,128]{2,1,0:T(8,128)S(1)}, u32[]{:S(2)}, u32[]{:S(2)}) collective-permute-start(f32[2,64,128]{2,1,0:T(8,128)S(1)} %fusion.32), channel_id=1, source_target_pairs={{0,128},{32,160},{64,192},{96,224},{128,0},{160,32},{192,64},{224,... | collective-permute-start | bytes 196616 | tf_op jit(solution)/shard_map/ppermute | solution.py:23
  102.5 2.4 %collective-permute-start.12 = (f32[64,128]{1,0:T(8,128)S(1)}, f32[64,128]{1,0:T(8,128)S(1)}, u32[]{:S(2)}, u32[]{:S(2)}) collective-permute-start(f32[64,128]{1,0:T(8,128)S(1)} %add.132), channel_id=1, source_target_pairs={{0,64},{32,96},{64,0},{96,32},{128,192},{160,224},{192,128},{224,1... | collective-permute-start | bytes 98312 | tf_op jit(solution)/shard_map/ppermute | solution.py:23
  104.9 2.0 %collective-permute-done.12 = f32[64,128]{1,0:T(8,128)S(1)} collective-permute-done((f32[64,128]{1,0:T(8,128)S(1)}, f32[64,128]{1,0:T(8,128)S(1)}, u32[]{:S(2)}, u32[]{:S(2)}) %collective-permute-start.12) | collective-permute-done | bytes 32800 | tf_op jit(solution)/shard_map/ppermute | solution.py:23
  106.9 2.6 %collective-permute-start.13 = (f32[64,128]{1,0:T(8,128)S(1)}, f32[64,128]{1,0:T(8,128)S(1)}, u32[]{:S(2)}, u32[]{:S(2)}) collective-permute-start(f32[64,128]{1,0:T(8,128)S(1)} %add.133), channel_id=1, source_target_pairs={{0,128},{32,160},{64,192},{96,224},{128,0},{160,32},{192,64},{224,... | collective-permute-start | bytes 98312 | tf_op jit(solution)/shard_map/ppermute | solution.py:23
  109.5 4.1 %collective-permute-done.13 = f32[64,128]{1,0:T(8,128)S(1)} collective-permute-done((f32[64,128]{1,0:T(8,128)S(1)}, f32[64,128]{1,0:T(8,128)S(1)}, u32[]{:S(2)}, u32[]{:S(2)}) %collective-permute-start.13) | collective-permute-done | bytes 32800 | tf_op jit(solution)/shard_map/ppermute | solution.py:23
  113.7 4.6 %collective-permute-start.15 = (f32[2,64,128]{2,1,0:T(8,128)S(1)}, f32[2,64,128]{2,1,0:T(8,128)S(1)}, u32[]{:S(2)}, u32[]{:S(2)}) collective-permute-start(f32[2,64,128]{2,1,0:T(8,128)S(1)} %pad_maximum_fusion.2), channel_id=1, source_target_pairs={{0,1},{1,0},{2,3},{3,2},{4,5},{5,4},{6,7},{7,6},{8,9},{9,8},{10,11... | collective-permute-start | bytes 196616 | tf_op jit(solution)/shard_map/ppermute | solution.py:23
  118.3 0.9 collective-permute-done.15
  119.2 0.4 collective-permute-start.16
  119.6 0.2 copy.13
  119.8 0.8 broadcast_in_dim.2
  120.6 7.1 %all-to-all-start.2 = ((bf16[16,64,128]{2,1,0:T(8,128)(2,1)}), bf16[16,64,128]{2,1,0:T(8,128)(2,1)S(1)}, u32[]{:S(2)}, u32[]{:S(2)}) async-start(bf16[16,64,128]{2,1,0:T(8,128)(2,1)} %broadcast_in_dim.2), calls=%async_computation.2 | async-start | bytes 524288 | tf_op jit(solution)/shard_map/all_to_all | solution.py:112
  127.7 0.7 slice_bitcast_fusion
  128.3 6.8 %all-to-all-done.2 = bf16[16,64,128]{2,1,0:T(8,128)(2,1)S(1)} async-done(((bf16[16,64,128]{2,1,0:T(8,128)(2,1)}), bf16[16,64,128]{2,1,0:T(8,128)(2,1)S(1)}, u32[]{:S(2)}, u32[]{:S(2)}) %all-to-all-start.2) | async-done | bytes 262176 | tf_op jit(solution)/shard_map/all_to_all | solution.py:112
  135.1 2.0 %collective-permute-start.14 = (bf16[1024,128]{1,0:T(8,128)(2,1)S(1)}, bf16[1024,128]{1,0:T(8,128)(2,1)S(1)}, u32[]{:S(2)}, u32[]{:S(2)}) collective-permute-start(bf16[1024,128]{1,0:T(8,128)(2,1)S(1)} %bitcast.81), channel_id=1, source_target_pairs={{0,1},{1,0},{2,3},{3,2},{4,5},{5,4},{6,7},{7,6},{8,9},{9,8},{10,11... | collective-permute-start | bytes 786440 | tf_op jit(solution)/shard_map/ppermute | solution.py:23
  137.1 0.5 convolution_bitcast_fusion.1
  137.6 0.7 collective-permute-done.14
  138.2 0.5 convolution_bitcast_fusion
  138.8 1.0 copy.14
  (40 shorter events, 1.0 us)
Async XLA Ops:
  0.6 20.6 %copy-start = (bf16[512,1024]{1,0:T(8,128)(2,1)S(1)}, bf16[512,1024]{1,0:T(8,128)(2,1)}, u32[]{:S(2)}) copy-start(bf16[512,1024]{1,0:T(8,128)(2,1)} %param.7) | copy-start | bytes 3145732
  3.8 7.4 %collective-permute-start.9 = (bf16[8192,128]{1,0:T(8,128)(2,1)}, bf16[8192,128]{1,0:T(8,128)(2,1)}, u32[]{:S(2)}, u32[]{:S(2)}) collective-permute-start(bf16[8192,128]{1,0:T(8,128)(2,1)} %dynamic-slice_bitcast_fusion), channel_id=1, source_target_pairs={{0,1},{1,0},{2,3},{3,2},{4,5},{5,4},{6,7},{7,6},{8,9},{9,8},{10,11... | collective-permute-start | bytes 6291464 | tf_op jit(solution)/shard_map/ppermute | solution.py:23
  15.5 5.1 %copy-start.1 = (bf16[512,1024]{1,0:T(8,128)(2,1)S(1)}, bf16[512,1024]{1,0:T(8,128)(2,1)}, u32[]{:S(2)}) copy-start(bf16[512,1024]{1,0:T(8,128)(2,1)} %param.8) | copy-start | bytes 3145732
  15.5 48.5 %all-to-all-start = ((f16[8,1024,128]{2,1,0:T(8,128)(2,1)}), f16[8,1024,128]{2,1,0:T(8,128)(2,1)}, u32[]{:S(2)}, u32[]{:S(2)}) async-start(f16[8,1024,128]{2,1,0:T(8,128)(2,1)} %bitcast.76), calls=%async_computation | async-start | bytes 4194304 | tf_op jit(solution)/shard_map/all_to_all | solution.py:47
  20.6 7.4 %copy-start.3 = (f32[64,256]{1,0:T(8,128)S(1)}, f32[64,256]{1,0:T(8,128)}, u32[]{:S(2)}) copy-start(f32[64,256]{1,0:T(8,128)} %param.10) | copy-start | bytes 196612
  21.5 1.9 %collective-permute-start = (f32[512,128]{1,0:T(8,128)S(1)}, f32[512,128]{1,0:T(8,128)S(1)}, u32[]{:S(2)}, u32[]{:S(2)}) collective-permute-start(f32[512,128]{1,0:T(8,128)S(1)} %fusion.8), channel_id=1, source_target_pairs={{0,1},{1,0},{2,3},{3,2},{4,5},{5,4},{6,7},{7,6},{8,9},{9,8},{10,11... | collective-permute-start | bytes 786440 | tf_op jit(solution)/shard_map/ppermute | solution.py:23
  24.2 30.3 %collective-permute-start.1 = (f32[2,2,64,128]{3,2,1,0:T(8,128)}, f32[2,2,64,128]{3,2,1,0:T(8,128)}, u32[]{:S(2)}, u32[]{:S(2)}) collective-permute-start(f32[2,2,64,128]{3,2,1,0:T(8,128)} %dynamic-slice_bitcast_fusion.1), channel_id=1, source_target_pairs={{0,8},{4,12},{8,0},{12,4},{1,9},{5,13},{9,1},{13,5},{2,10},{6,14},... | collective-permute-start | bytes 393224 | tf_op jit(solution)/shard_map/ppermute | solution.py:23
  27.4 39.4 %collective-permute-start.10 = (bf16[512,1024]{1,0:T(8,128)(2,1)S(1)}, bf16[512,1024]{1,0:T(8,128)(2,1)S(1)}, u32[]{:S(2)}, u32[]{:S(2)}) collective-permute-start(bf16[512,1024]{1,0:T(8,128)(2,1)S(1)} %copy-done.1), channel_id=1, source_target_pairs={{0,1},{1,0},{2,3},{3,2},{4,5},{5,4},{6,7},{7,6},{8,9},{9,8},{10,11... | collective-permute-start | bytes 3145736 | tf_op jit(solution)/shard_map/ppermute | solution.py:23
  29.5 26.0 %collective-permute-start.4 = (f32[2,64,128]{2,1,0:T(8,128)}, f32[2,64,128]{2,1,0:T(8,128)S(1)}, u32[]{:S(2)}, u32[]{:S(2)}) collective-permute-start(f32[2,64,128]{2,1,0:T(8,128)} %get-tuple-element.18), channel_id=1, source_target_pairs={{0,1},{1,0},{2,3},{3,2},{4,5},{5,4},{6,7},{7,6},{8,9},{9,8},{10,11... | collective-permute-start | bytes 196616 | tf_op jit(solution)/shard_map/ppermute | solution.py:23
  55.4 3.2 %collective-permute-start.2 = (f32[2,64,128]{2,1,0:T(8,128)S(1)}, f32[2,64,128]{2,1,0:T(8,128)S(1)}, u32[]{:S(2)}, u32[]{:S(2)}) collective-permute-start(f32[2,64,128]{2,1,0:T(8,128)S(1)} %dynamic-slice_bitcast_fusion.2), channel_id=1, source_target_pairs={{0,4},{4,0},{8,12},{12,8},{1,5},{5,1},{9,13},{13,9},{2,6},{6,2},{1... | collective-permute-start | bytes 196616 | tf_op jit(solution)/shard_map/ppermute | solution.py:23
  56.2 6.4 %collective-permute-start.5 = (f32[2,128,128]{2,1,0:T(8,128)}, f32[2,128,128]{2,1,0:T(8,128)S(1)}, u32[]{:S(2)}, u32[]{:S(2)}) collective-permute-start(f32[2,128,128]{2,1,0:T(8,128)} %maximum_select_fusion.1), channel_id=1, source_target_pairs={{0,0},{2,32},{4,64},{6,96},{8,128},{10,160},{12,192},{14,224},{32,... | collective-permute-start | bytes 393224 | tf_op jit(solution)/shard_map/ppermute | solution.py:60
  58.6 5.2 %collective-permute-start.3 = (f32[64,128]{1,0:T(8,128)S(1)}, f32[64,128]{1,0:T(8,128)S(1)}, u32[]{:S(2)}, u32[]{:S(2)}) collective-permute-start(f32[64,128]{1,0:T(8,128)S(1)} %dynamic-slice_bitcast_fusion.3), channel_id=1, source_target_pairs={{0,2},{2,0},{1,3},{3,1},{4,6},{6,4},{5,7},{7,5},{8,10},{10,8},{9,1... | collective-permute-start | bytes 98312 | tf_op jit(solution)/shard_map/ppermute | solution.py:23
  67.6 52.0 %copy-start.2 = (f32[512,256]{1,0:T(8,128)S(1)}, f32[512,256]{1,0:T(8,128)}, u32[]{:S(2)}) copy-start(f32[512,256]{1,0:T(8,128)} %param.9) | copy-start | bytes 1572868
  68.6 27.3 %all-to-all-start.1 = ((f32[16,64,128]{2,1,0:T(8,128)}), f32[16,64,128]{2,1,0:T(8,128)S(1)}, u32[]{:S(2)}, u32[]{:S(2)}) async-start(f32[16,64,128]{2,1,0:T(8,128)} %bitcast.20), calls=%async_computation.1 | async-start | bytes 1048576 | tf_op jit(solution)/shard_map/all_to_all | solution.py:93
  86.1 3.2 %collective-permute-start.6 = (f32[2,64,128]{2,1,0:T(8,128)S(1)}, f32[2,64,128]{2,1,0:T(8,128)S(1)}, u32[]{:S(2)}, u32[]{:S(2)}) collective-permute-start(f32[2,64,128]{2,1,0:T(8,128)S(1)} %pad_maximum_fusion.1), channel_id=1, source_target_pairs={{0,32},{32,0},{64,96},{96,64},{128,160},{160,128},{192,224},{224,1... | collective-permute-start | bytes 196616 | tf_op jit(solution)/shard_map/ppermute | solution.py:23
  89.3 6.7 %collective-permute-start.7 = (f32[2,64,128]{2,1,0:T(8,128)S(1)}, f32[2,64,128]{2,1,0:T(8,128)S(1)}, u32[]{:S(2)}, u32[]{:S(2)}) collective-permute-start(f32[2,64,128]{2,1,0:T(8,128)S(1)} %fusion.24), channel_id=1, source_target_pairs={{0,64},{32,96},{64,0},{96,32},{128,192},{160,224},{192,128},{224,1... | collective-permute-start | bytes 196616 | tf_op jit(solution)/shard_map/ppermute | solution.py:23
  95.9 6.6 %collective-permute-start.11 = (f32[64,128]{1,0:T(8,128)S(1)}, f32[64,128]{1,0:T(8,128)S(1)}, u32[]{:S(2)}, u32[]{:S(2)}) collective-permute-start(f32[64,128]{1,0:T(8,128)S(1)} %reduce_sum.19), channel_id=1, source_target_pairs={{0,32},{32,0},{64,96},{96,64},{128,160},{160,128},{192,224},{224,1... | collective-permute-start | bytes 98312 | tf_op jit(solution)/shard_map/ppermute | solution.py:23
  96.0 13.4 %collective-permute-start.8 = (f32[2,64,128]{2,1,0:T(8,128)S(1)}, f32[2,64,128]{2,1,0:T(8,128)S(1)}, u32[]{:S(2)}, u32[]{:S(2)}) collective-permute-start(f32[2,64,128]{2,1,0:T(8,128)S(1)} %fusion.32), channel_id=1, source_target_pairs={{0,128},{32,160},{64,192},{96,224},{128,0},{160,32},{192,64},{224,... | collective-permute-start | bytes 196616 | tf_op jit(solution)/shard_map/ppermute | solution.py:23
  102.5 4.4 %collective-permute-start.12 = (f32[64,128]{1,0:T(8,128)S(1)}, f32[64,128]{1,0:T(8,128)S(1)}, u32[]{:S(2)}, u32[]{:S(2)}) collective-permute-start(f32[64,128]{1,0:T(8,128)S(1)} %add.132), channel_id=1, source_target_pairs={{0,64},{32,96},{64,0},{96,32},{128,192},{160,224},{192,128},{224,1... | collective-permute-start | bytes 98312 | tf_op jit(solution)/shard_map/ppermute | solution.py:23
  106.9 6.7 %collective-permute-start.13 = (f32[64,128]{1,0:T(8,128)S(1)}, f32[64,128]{1,0:T(8,128)S(1)}, u32[]{:S(2)}, u32[]{:S(2)}) collective-permute-start(f32[64,128]{1,0:T(8,128)S(1)} %add.133), channel_id=1, source_target_pairs={{0,128},{32,160},{64,192},{96,224},{128,0},{160,32},{192,64},{224,... | collective-permute-start | bytes 98312 | tf_op jit(solution)/shard_map/ppermute | solution.py:23
  113.7 5.5 %collective-permute-start.15 = (f32[2,64,128]{2,1,0:T(8,128)S(1)}, f32[2,64,128]{2,1,0:T(8,128)S(1)}, u32[]{:S(2)}, u32[]{:S(2)}) collective-permute-start(f32[2,64,128]{2,1,0:T(8,128)S(1)} %pad_maximum_fusion.2), channel_id=1, source_target_pairs={{0,1},{1,0},{2,3},{3,2},{4,5},{5,4},{6,7},{7,6},{8,9},{9,8},{10,11... | collective-permute-start | bytes 196616 | tf_op jit(solution)/shard_map/ppermute | solution.py:23
  119.2 8.4 %collective-permute-start.16 = (f32[2,64,256]{2,1,0:T(8,128)S(1)}, f32[2,64,256]{2,1,0:T(8,128)S(1)}, u32[]{:S(2)}, u32[]{:S(2)}) collective-permute-start(f32[2,64,256]{2,1,0:T(8,128)S(1)} %maximum_select_fusion.2), channel_id=1, source_target_pairs={{0,16},{16,0},{1,17},{17,1},{2,18},{18,2},{3,19},{19,3},{4,20},{20... | collective-permute-start | bytes 393224 | tf_op jit(solution)/shard_map/ppermute | solution.py:23
  120.6 14.5 %all-to-all-start.2 = ((bf16[16,64,128]{2,1,0:T(8,128)(2,1)}), bf16[16,64,128]{2,1,0:T(8,128)(2,1)S(1)}, u32[]{:S(2)}, u32[]{:S(2)}) async-start(bf16[16,64,128]{2,1,0:T(8,128)(2,1)} %broadcast_in_dim.2), calls=%async_computation.2 | async-start | bytes 524288 | tf_op jit(solution)/shard_map/all_to_all | solution.py:112
  135.1 3.2 %collective-permute-start.14 = (bf16[1024,128]{1,0:T(8,128)(2,1)S(1)}, bf16[1024,128]{1,0:T(8,128)(2,1)S(1)}, u32[]{:S(2)}, u32[]{:S(2)}) collective-permute-start(bf16[1024,128]{1,0:T(8,128)(2,1)S(1)} %bitcast.81), channel_id=1, source_target_pairs={{0,1},{1,0},{2,3},{3,2},{4,5},{5,4},{6,7},{7,6},{8,9},{9,8},{10,11... | collective-permute-start | bytes 786440 | tf_op jit(solution)/shard_map/ppermute | solution.py:23

commit v2 on v1

v2 whole, which is shorter than its diff:
```python
import jax
import jax.numpy as jnp
from jax import lax
from jax.sharding import Mesh, PartitionSpec as P

beta_mean = 0.9
beta_square = 0.95
bias_mean = 0.9999734386011124
bias_square = 0.9940794707796659
adam_epsilon = 1e-08
step_scale = 0.5

AXES = ("z", "yl", "x", "yh", "core")
SIZES = (8, 2, 4, 2, 2)
OUTER = ("z", "yl")
DEV = ("x", "yh", "core")
PLANE = ("x", "yh", "yl")
PAIRS = ("x", "yh")
SCALE = 4096.0
MARGIN_SCALE = 8192.0
PROJECTED_SCALE = 8.0


def swap(value, axis, bit, size):
    return lax.ppermute(value, axis, [(i, i ^ bit) for i in range(size)])


def cut(value, at, extent, axis):
    return lax.dynamic_slice_in_dim(value, at * extent, extent, axis)


def pieces(value):
    high = lax.reduce_precision(value, 8, 7)
    rest = value - high
    mid = lax.reduce_precision(rest, 8, 7)
    low = rest - mid
    return jnp.concatenate([high, mid, low], axis=1).astype(jnp.bfloat16)


def on_device(partials, p_old, p_new, weight, m_old, v_old):
    core = lax.axis_index("core")
    z, yl = lax.axis_index("z"), lax.axis_index("yl")
    f32 = jnp.float32

    def sides(own, other, axis):
        return jnp.where(
            core == 0,
            jnp.concatenate([own, other], axis=axis),
            jnp.concatenate([other, own], axis=axis),
        )

    p_other = swap(p_new, "core", 1, 2)

    turn = [(a * 8 + b, a * 8 + (a ^ b)) for a in range(8) for b in range(8)]
    turned = lax.ppermute(jnp.stack([m_old, v_old]), ("z", "x", "yh"), turn)

    p_rank = lax.dynamic_index_in_dim(p_new.reshape(512, 8, 2, 64), yl, 2, keepdims=False)
    product = jnp.dot(p_rank.reshape(512, 512).T, p_old, preferred_element_type=f32)
    met = (lax.broadcasted_iota(jnp.int32, (512, 128), 0) // 64) ^ z
    margin = product[:, :128]
    for place in range(1, 8):
        margin = jnp.where(met == place, product[:, place * 128 : place * 128 + 128], margin)
    margin = margin + swap(margin, "core", 1, 2)
    margin = (margin * MARGIN_SCALE).astype(jnp.float16).reshape(8, 64, 128)

    grad = partials[0]
    theirs = swap(cut(grad, 1 - core, 128, 1), "core", 1, 2)
    ours = cut(grad, core, 128, 1)
    chip_sum = ((ours.astype(f32) + theirs.astype(f32)) * SCALE).astype(jnp.float16)
    sent = jnp.concatenate([chip_sum.reshape(8, 1024, 128), margin], axis=1)
    sent, turned = lax.optimization_barrier((sent, turned))
    rows = lax.all_to_all(sent, PAIRS, 0, 0, tiled=True)

    moments_in = swap(cut(turned, 1 - core, 128, 2), "core", 1, 2)
    moments = sides(cut(turned, core, 128, 2), moments_in, 1)
    margin = jnp.sum(rows[:, 1024:].astype(f32), axis=0) * (1.0 / MARGIN_SCALE)
    first = jnp.dot(margin, moments[0], precision=lax.Precision.HIGHEST)
    second = jnp.dot(margin * margin, moments[1], precision=lax.Precision.HIGHEST)
    rotated = jnp.stack([first, second])
    for bit in (1, 2, 4):
        rotated = rotated + swap(rotated, "z", bit, 8)

    grad_rows = jnp.sum(rows[:, :1024].astype(f32), axis=0) * (1.0 / SCALE)
    split = pieces(grad_rows)
    across = (((0,), (0,)), ((), ()))
    terms = lax.dot_general(
        p_new, cut(split, core, 512, 0), across, preferred_element_type=f32
    ) + lax.dot_general(
        p_other, cut(split, 1 - core, 512, 0), across, preferred_element_type=f32
    )
    projected = terms[:, :128] + terms[:, 128:256] + terms[:, 256:]
    projected = (projected * PROJECTED_SCALE).astype(jnp.float16)
    projected = lax.all_to_all(projected.reshape(16, 64, 128), PLANE, 0, 0, tiled=True)
    projected = jnp.sum(projected.astype(f32), axis=0) * (1.0 / PROJECTED_SCALE)
    for bit in (1, 2, 4):
        projected = projected + swap(projected, "z", bit, 8)

    m_new = beta_mean * rotated[0] + (1.0 - beta_mean) * projected
    v_new = beta_square * rotated[1] + (1.0 - beta_square) * projected * projected
    direction = (m_new / bias_mean / (jnp.sqrt(v_new / bias_square) + adam_epsilon)).astype(
        jnp.bfloat16
    )

    spread = jnp.broadcast_to(direction[None], (16, 64, 128))
    mine = lax.all_to_all(spread, PLANE, 0, 0, tiled=True).reshape(1024, 128)
    other = swap(mine, "core", 1, 2)
    update = sides(
        jnp.dot(p_new, mine, preferred_element_type=f32),
        jnp.dot(p_new, other, preferred_element_type=f32),
        1,
    )
    new_weight = weight - step_scale * update

    made = jnp.stack([m_new, v_new])
    near = swap(made, "yl", 1, 2)
    kept = jnp.where(core == yl, made, near)
    given = jnp.where(core == yl, near, made)
    made = sides(kept, swap(given, "core", 1, 2), 2)
    return (new_weight, made[0], made[1])


def solution(mesh):
    fine = Mesh(mesh.devices.reshape(SIZES), AXES)
    in_specs = (
        P(OUTER + DEV, None, None),
        P(DEV, None),
        P(DEV, None),
        P(DEV, None),
        P(DEV, None),
        P(DEV, None),
    )
    out_specs = (P(DEV, None), P(DEV, None), P(DEV, None))
    return jax.shard_map(
        on_device, mesh=fine, in_specs=in_specs, out_specs=out_specs, check_vma=False
    )
```

time: 140 us -> 121 us (0.86)
  starting transfers between devices: 62.4 us -> 45.2 us
  waiting for transfers between devices: 55.7 us -> 53.2 us
    ppermute x16 -> x13, waiting for transfers between devices: 43.2 us -> 11.8 us  [swap(): return lax.ppermute(value, axis, [(i, i ^ bit) for i in range(size)])]
    all_to_all x1, waiting for transfers between devices: 0.01 us -> 30.9 us  [on_device(): rows = lax.all_to_all(sent, PAIRS, 0, 0, tiled=True)]
    all_to_all x1, starting transfers between devices: 17.4 us -> 3.53 us  [on_device(): lax.all_to_all(projected.reshape(16, 64, 128), PLANE, 0, 0, tiled=True)]
    all_to_all x1, starting transfers between devices: 7.06 us -> 3.56 us  [on_device(): mine = lax.all_to_all(spread, PLANE, 0, 0, tiled=True).reshape(1024, 128)]
    all_to_all x1, waiting for transfers between devices: 5.67 us -> 3.32 us  [on_device(): lax.all_to_all(projected.reshape(16, 64, 128), PLANE, 0, 0, tiled=True)]
    concatenate x0 -> x1, other arithmetic: none -> 2.04 us  [on_device(): sent = jnp.concatenate([chip_sum.reshape(8, 1024, 128), margin], axis=1)]
    reduce_sum x2 -> x3, other arithmetic: 1.96 us -> 2.9 us  [the longest x1 1.93 us: on_device(): grad_rows = jnp.sum(rows[:, :1024].astype(f32), axis=0) * (1.0 / SCALE)]
    ppermute x16 -> x13, starting transfers between devices: 31.3 us -> 31.5 us  [swap(): return lax.ppermute(value, axis, [(i, i ^ bit) for i in range(size)])]
  transfers between devices with their start and end apart: 20 -> 17, of which waited for: 12 -> 8; matrix products, arithmetic and copies ran while one was open for 7% -> 14% of each run, Pallas kernels for 0% -> 0%
where the time goes in v2:
time: 121 us; the launch traced here: 120 us
  waiting for transfers between devices  53.2 us (44%)
  starting transfers between devices  45.2 us (37%)
  other arithmetic  10.5 us (9%)
  local copies, waits for them, and re-layouts  7.35 us (6%)
  matrix products  3.24 us (3%)
    ppermute x13, starting transfers between devices, swap(): return lax.ppermute(value, axis, [(i, i ^ bit) for i in range(size)])  31.5 us
    all_to_all x1, waiting for transfers between devices, on_device(): rows = lax.all_to_all(sent, PAIRS, 0, 0, tiled=True)  30.9 us
    ppermute x13, waiting for transfers between devices, swap(): return lax.ppermute(value, axis, [(i, i ^ bit) for i in range(size)])  11.8 us
    all_to_all x1, waiting for transfers between devices, on_device(): mine = lax.all_to_all(spread, PLANE, 0, 0, tiled=True).reshape(1024, 128)  7.12 us
    all_to_all x1, starting transfers between devices, on_device(): rows = lax.all_to_all(sent, PAIRS, 0, 0, tiled=True)  5.05 us
    all_to_all x1, starting transfers between devices, on_device(): mine = lax.all_to_all(spread, PLANE, 0, 0, tiled=True).reshape(1024, 128)  3.56 us
    all_to_all x1, starting transfers between devices, on_device(): lax.all_to_all(projected.reshape(16, 64, 128), PLANE, 0, 0, tiled=True)  3.53 us
    all_to_all x1, waiting for transfers between devices, on_device(): lax.all_to_all(projected.reshape(16, 64, 128), PLANE, 0, 0, tiled=True)  3.32 us
  transfers between devices with their start and end apart: 17, of which 8 were waited for; matrix products, arithmetic and copies ran while one was open for 14% of the time, Pallas kernels for 0%

profile of v2, /device:TPU:1, one launch (start us, length us, event | category | flops | bytes accessed | tf_op | source)
XLA Modules:
  0.0 120.4 jit_solution(7556428134416934672)
XLA Ops:
  0.7 3.2 %dynamic-slice_bitcast_fusion = bf16[8192,128]{1,0:T(8,128)(2,1)} fusion(bf16[1,8192,256]{2,1,0:T(8,128)(2,1)} %param.6, s32[]{:T(128)S(6)} %select_n.83), kind=kLoop, calls=%fused_computation.5 | loop fusion | bytes 4194308 | tf_op jit(solution)/shard_map/dynamic_slice | solution.py:29
  3.9 3.2 %collective-permute-start = (bf16[8192,128]{1,0:T(8,128)(2,1)}, bf16[8192,128]{1,0:T(8,128)(2,1)}, u32[]{:S(2)}, u32[]{:S(2)}) collective-permute-start(bf16[8192,128]{1,0:T(8,128)(2,1)} %dynamic-slice_bitcast_fusion), channel_id=1, source_target_pairs={{0,1},{1,0},{2,3},{3,2},{4,5},{5,4},{6,7},{7,6},{8,9},{9,8},{10,11... | collective-permute-start | bytes 6291464 | tf_op jit(solution)/shard_map/ppermute | solution.py:25
  7.1 0.5 copy.11
  7.7 0.7 fusion.43
  8.5 1.0 fusion.15
  9.5 0.7 pad_maximum_fusion.2
  10.1 1.6 %collective-permute-start.2 = (f32[2,64,256]{2,1,0:T(8,128)}, f32[2,64,256]{2,1,0:T(8,128)S(1)}, u32[]{:S(2)}, u32[]{:S(2)}) collective-permute-start(f32[2,64,256]{2,1,0:T(8,128)} %pad_maximum_fusion.2), channel_id=1, source_target_pairs={{0,0},{2,2},{4,4},{6,6},{8,8},{10,10},{12,12},{14,14},{32,34},{34,... | collective-permute-start | bytes 393224 | tf_op jit(solution)/shard_map/ppermute | solution.py:55
  11.7 0.3 multiply_convert_fusion
  12.0 3.0 %fusion.1 = f16[8192,128]{1,0:T(8,128)(2,1)S(1)} fusion(bf16[8192,128]{1,0:T(8,128)(2,1)} %collective-permute-done, bf16[1,8192,256]{2,1,0:T(8,128)(2,1)} %param.6, s32[]{:T(128)S(6)} %select_n.82), kind=kLoop, calls=%fused_computation.2 | loop fusion | flops 5242880 | bytes 6291460 | tf_op jit(solution)/shard_map/convert_element_type | solution.py:69
  15.1 2.0 %pad_maximum_fusion = f16[8,1088,128]{2,1,0:T(8,128)(2,1)} fusion(f16[8,64,128]{2,1,0:T(8,128)(2,1)S(1)} %bitcast.66, f16[8,1024,128]{2,1,0:T(8,128)(2,1)S(1)} %bitcast.61), kind=kLoop, calls=%fused_computation.4 | loop fusion | flops 1114112 | bytes 4456448 | tf_op jit(solution)/shard_map/concatenate | solution.py:70
  17.1 5.0 %all-to-all-start = ((f16[8,1088,128]{2,1,0:T(8,128)(2,1)}), f16[8,1088,128]{2,1,0:T(8,128)(2,1)}, u32[]{:S(2)}, u32[]{:S(2)}) async-start(f16[8,1088,128]{2,1,0:T(8,128)(2,1)} %pad_maximum_fusion), calls=%async_computation | async-start | bytes 4456448 | tf_op jit(solution)/shard_map/all_to_all | solution.py:72
  22.2 0.9 collective-permute-start.3
  23.0 0.1 collective-permute-start.7
  23.1 0.8 collective-permute-done.3
  23.9 30.9 %all-to-all-done = f16[8,1088,128]{2,1,0:T(8,128)(2,1)} async-done(((f16[8,1088,128]{2,1,0:T(8,128)(2,1)}), f16[8,1088,128]{2,1,0:T(8,128)(2,1)}, u32[]{:S(2)}, u32[]{:S(2)}) %all-to-all-start) | async-done | bytes 2228256 | tf_op jit(solution)/shard_map/all_to_all | solution.py:72
  54.8 0.9 convert_reduce_fusion.2
  55.8 0.2 convolution_bitcast_fusion.3
  56.0 0.2 convolution_bitcast_fusion.2
  56.2 1.7 %collective-permute-start.4 = (f32[2,64,128]{2,1,0:T(8,128)S(1)}, f32[2,64,128]{2,1,0:T(8,128)S(1)}, u32[]{:S(2)}, u32[]{:S(2)}) collective-permute-start(f32[2,64,128]{2,1,0:T(8,128)S(1)} %pad_maximum_fusion.3), channel_id=1, source_target_pairs={{0,32},{32,0},{64,96},{96,64},{128,160},{160,128},{192,224},{224,1... | collective-permute-start | bytes 196616 | tf_op jit(solution)/shard_map/ppermute | solution.py:25
  57.9 1.9 %convert_reduce_fusion = f32[1024,128]{1,0:T(8,128)S(1)} fusion(f16[8,1088,128]{2,1,0:T(8,128)(2,1)} %all-to-all-done), kind=kLoop, calls=%fused_computation.3 | loop fusion | flops 1966080 | bytes 2621440 | tf_op jit(solution)/shard_map/reduce_sum | solution.py:83
  59.8 0.1 reduce-precision_convert_fusion.1
  59.9 0.1 pad_maximum_fusion.1
  60.0 0.6 fusion.8
  60.7 0.6 add_bitcast_fusion
  61.3 0.1 fusion.4
  61.4 0.9 copy.12
  62.3 3.5 %all-to-all-start.1 = ((f16[16,64,128]{2,1,0:T(8,128)(2,1)}), f16[16,64,128]{2,1,0:T(8,128)(2,1)S(1)}, u32[]{:S(2)}, u32[]{:S(2)}) async-start(f16[16,64,128]{2,1,0:T(8,128)(2,1)} %bitcast.14), calls=%async_computation.1 | async-start | bytes 524288 | tf_op jit(solution)/shard_map/all_to_all | solution.py:93
  65.9 4.0 %collective-permute-start.5 = (f32[2,64,128]{2,1,0:T(8,128)S(1)}, f32[2,64,128]{2,1,0:T(8,128)S(1)}, u32[]{:S(2)}, u32[]{:S(2)}) collective-permute-start(f32[2,64,128]{2,1,0:T(8,128)S(1)} %fusion.42), channel_id=1, source_target_pairs={{0,64},{32,96},{64,0},{96,32},{128,192},{160,224},{192,128},{224,1... | collective-permute-start | bytes 196616 | tf_op jit(solution)/shard_map/ppermute | solution.py:25
  69.9 3.3 %all-to-all-done.1 = f16[16,64,128]{2,1,0:T(8,128)(2,1)S(1)} async-done(((f16[16,64,128]{2,1,0:T(8,128)(2,1)}), f16[16,64,128]{2,1,0:T(8,128)(2,1)S(1)}, u32[]{:S(2)}, u32[]{:S(2)}) %all-to-all-start.1) | async-done | bytes 262176 | tf_op jit(solution)/shard_map/all_to_all | solution.py:93
  73.4 8.5 %collective-permute-start.6 = (f32[2,64,128]{2,1,0:T(8,128)S(1)}, f32[2,64,128]{2,1,0:T(8,128)S(1)}, u32[]{:S(2)}, u32[]{:S(2)}) collective-permute-start(f32[2,64,128]{2,1,0:T(8,128)S(1)} %fusion.52), channel_id=1, source_target_pairs={{0,128},{32,160},{64,192},{96,224},{128,0},{160,32},{192,64},{224,... | collective-permute-start | bytes 196616 | tf_op jit(solution)/shard_map/ppermute | solution.py:25
  81.9 1.1 collective-permute-start.9
  83.0 3.1 %collective-permute-done.9 = f32[64,128]{1,0:T(8,128)S(1)} collective-permute-done((f32[64,128]{1,0:T(8,128)S(1)}, f32[64,128]{1,0:T(8,128)S(1)}, u32[]{:S(2)}, u32[]{:S(2)}) %collective-permute-start.9) | collective-permute-done | bytes 32800 | tf_op jit(solution)/shard_map/ppermute | solution.py:25
  86.1 2.2 %collective-permute-start.10 = (f32[64,128]{1,0:T(8,128)S(1)}, f32[64,128]{1,0:T(8,128)S(1)}, u32[]{:S(2)}, u32[]{:S(2)}) collective-permute-start(f32[64,128]{1,0:T(8,128)S(1)} %add.83), channel_id=1, source_target_pairs={{0,128},{32,160},{64,192},{96,224},{128,0},{160,32},{192,64},{224,... | collective-permute-start | bytes 98312 | tf_op jit(solution)/shard_map/ppermute | solution.py:25
  88.3 4.5 %collective-permute-done.10 = f32[64,128]{1,0:T(8,128)S(1)} collective-permute-done((f32[64,128]{1,0:T(8,128)S(1)}, f32[64,128]{1,0:T(8,128)S(1)}, u32[]{:S(2)}, u32[]{:S(2)}) %collective-permute-start.10) | collective-permute-done | bytes 32800 | tf_op jit(solution)/shard_map/ppermute | solution.py:25
  92.8 0.4 collective-permute-start.12
  93.2 2.8 %collective-permute-done.12 = f32[2,64,128]{2,1,0:T(8,128)S(1)} collective-permute-done((f32[2,64,128]{2,1,0:T(8,128)S(1)}, f32[2,64,128]{2,1,0:T(8,128)S(1)}, u32[]{:S(2)}, u32[]{:S(2)}) %collective-permute-start.12) | collective-permute-done | bytes 65568 | tf_op jit(solution)/shard_map/ppermute | solution.py:25
  96.1 7.6 %collective-permute-start.13 = (f32[2,64,128]{2,1,0:T(8,128)S(1)}, f32[2,64,128]{2,1,0:T(8,128)S(1)}, u32[]{:S(2)}, u32[]{:S(2)}) collective-permute-start(f32[2,64,128]{2,1,0:T(8,128)S(1)} %get-tuple-element.19), channel_id=1, source_target_pairs={{0,1},{1,0},{2,3},{3,2},{4,5},{5,4},{6,7},{7,6},{8,9},{9,8},{10,11... | collective-permute-start | bytes 196616 | tf_op jit(solution)/shard_map/ppermute | solution.py:25
  103.7 0.2 copy.13
  103.9 0.8 broadcast_in_dim.2
  104.7 3.6 %all-to-all-start.2 = ((bf16[16,64,128]{2,1,0:T(8,128)(2,1)}), bf16[16,64,128]{2,1,0:T(8,128)(2,1)S(1)}, u32[]{:S(2)}, u32[]{:S(2)}) async-start(bf16[16,64,128]{2,1,0:T(8,128)(2,1)} %broadcast_in_dim.2), calls=%async_computation.2 | async-start | bytes 524288 | tf_op jit(solution)/shard_map/all_to_all | solution.py:105
  108.3 0.7 slice_bitcast_fusion
  108.9 7.1 %all-to-all-done.2 = bf16[16,64,128]{2,1,0:T(8,128)(2,1)S(1)} async-done(((bf16[16,64,128]{2,1,0:T(8,128)(2,1)}), bf16[16,64,128]{2,1,0:T(8,128)(2,1)S(1)}, u32[]{:S(2)}, u32[]{:S(2)}) %all-to-all-start.2) | async-done | bytes 262176 | tf_op jit(solution)/shard_map/all_to_all | solution.py:105
  116.0 1.6 %collective-permute-start.11 = (bf16[1024,128]{1,0:T(8,128)(2,1)S(1)}, bf16[1024,128]{1,0:T(8,128)(2,1)S(1)}, u32[]{:S(2)}, u32[]{:S(2)}) collective-permute-start(bf16[1024,128]{1,0:T(8,128)(2,1)S(1)} %bitcast.64), channel_id=1, source_target_pairs={{0,1},{1,0},{2,3},{3,2},{4,5},{5,4},{6,7},{7,6},{8,9},{9,8},{10,11... | collective-permute-start | bytes 786440 | tf_op jit(solution)/shard_map/ppermute | solution.py:25
  117.7 0.5 convolution_bitcast_fusion.1
  118.2 0.7 collective-permute-done.11
  118.8 0.5 convolution_bitcast_fusion
  119.3 0.1 fusion.6
  119.4 1.0 copy.14
  (40 shorter events, 0.4 us)
Async XLA Ops:
  0.6 7.1 %copy-start = (bf16[512,1024]{1,0:T(8,128)(2,1)S(1)}, bf16[512,1024]{1,0:T(8,128)(2,1)}, u32[]{:S(2)}) copy-start(bf16[512,1024]{1,0:T(8,128)(2,1)} %param.7) | copy-start | bytes 3145732
  0.7 6.5 %copy-start.1 = (bf16[512,1024]{1,0:T(8,128)(2,1)S(1)}, bf16[512,1024]{1,0:T(8,128)(2,1)}, u32[]{:S(2)}) copy-start(bf16[512,1024]{1,0:T(8,128)(2,1)} %param.8) | copy-start | bytes 3145732
  3.9 8.1 %collective-permute-start = (bf16[8192,128]{1,0:T(8,128)(2,1)}, bf16[8192,128]{1,0:T(8,128)(2,1)}, u32[]{:S(2)}, u32[]{:S(2)}) collective-permute-start(bf16[8192,128]{1,0:T(8,128)(2,1)} %dynamic-slice_bitcast_fusion), channel_id=1, source_target_pairs={{0,1},{1,0},{2,3},{3,2},{4,5},{5,4},{6,7},{7,6},{8,9},{9,8},{10,11... | collective-permute-start | bytes 6291464 | tf_op jit(solution)/shard_map/ppermute | solution.py:25
  8.5 1.0 copy-start.4
  8.5 1.0 copy-start.5
  9.5 2.2 %collective-permute-start.1 = (f32[512,128]{1,0:T(8,128)}, f32[512,128]{1,0:T(8,128)S(1)}, u32[]{:S(2)}, u32[]{:S(2)}) collective-permute-start(f32[512,128]{1,0:T(8,128)} %fusion.15), channel_id=1, source_target_pairs={{0,1},{1,0},{2,3},{3,2},{4,5},{5,4},{6,7},{7,6},{8,9},{9,8},{10,11... | collective-permute-start | bytes 786440 | tf_op jit(solution)/shard_map/ppermute | solution.py:25
  10.1 6.9 %collective-permute-start.2 = (f32[2,64,256]{2,1,0:T(8,128)}, f32[2,64,256]{2,1,0:T(8,128)S(1)}, u32[]{:S(2)}, u32[]{:S(2)}) collective-permute-start(f32[2,64,256]{2,1,0:T(8,128)} %pad_maximum_fusion.2), channel_id=1, source_target_pairs={{0,0},{2,2},{4,4},{6,6},{8,8},{10,10},{12,12},{14,14},{32,34},{34,... | collective-permute-start | bytes 393224 | tf_op jit(solution)/shard_map/ppermute | solution.py:55
  17.1 5.9 %copy-start.2 = (bf16[512,1024]{1,0:T(8,128)(2,1)S(1)}, bf16[512,1024]{1,0:T(8,128)(2,1)}, u32[]{:S(2)}) copy-start(bf16[512,1024]{1,0:T(8,128)(2,1)} %param.8) | copy-start | bytes 3145732
  17.1 37.7 %all-to-all-start = ((f16[8,1088,128]{2,1,0:T(8,128)(2,1)}), f16[8,1088,128]{2,1,0:T(8,128)(2,1)}, u32[]{:S(2)}, u32[]{:S(2)}) async-start(f16[8,1088,128]{2,1,0:T(8,128)(2,1)} %pad_maximum_fusion), calls=%async_computation | async-start | bytes 4456448 | tf_op jit(solution)/shard_map/all_to_all | solution.py:72
  22.2 1.8 %collective-permute-start.3 = (f32[2,64,128]{2,1,0:T(8,128)S(1)}, f32[2,64,128]{2,1,0:T(8,128)S(1)}, u32[]{:S(2)}, u32[]{:S(2)}) collective-permute-start(f32[2,64,128]{2,1,0:T(8,128)S(1)} %get-tuple-element.24), channel_id=1, source_target_pairs={{0,1},{1,0},{2,3},{3,2},{4,5},{5,4},{6,7},{7,6},{8,9},{9,8},{10,11... | collective-permute-start | bytes 196616 | tf_op jit(solution)/shard_map/ppermute | solution.py:25
  23.0 37.6 %collective-permute-start.7 = (bf16[512,1024]{1,0:T(8,128)(2,1)S(1)}, bf16[512,1024]{1,0:T(8,128)(2,1)S(1)}, u32[]{:S(2)}, u32[]{:S(2)}) collective-permute-start(bf16[512,1024]{1,0:T(8,128)(2,1)S(1)} %copy-done.2), channel_id=1, source_target_pairs={{0,1},{1,0},{2,3},{3,2},{4,5},{5,4},{6,7},{7,6},{8,9},{9,8},{10,11... | collective-permute-start | bytes 3145736 | tf_op jit(solution)/shard_map/ppermute | solution.py:25
  56.2 9.7 %collective-permute-start.4 = (f32[2,64,128]{2,1,0:T(8,128)S(1)}, f32[2,64,128]{2,1,0:T(8,128)S(1)}, u32[]{:S(2)}, u32[]{:S(2)}) collective-permute-start(f32[2,64,128]{2,1,0:T(8,128)S(1)} %pad_maximum_fusion.3), channel_id=1, source_target_pairs={{0,32},{32,0},{64,96},{96,64},{128,160},{160,128},{192,224},{224,1... | collective-permute-start | bytes 196616 | tf_op jit(solution)/shard_map/ppermute | solution.py:25
  61.3 42.4 %copy-start.3 = (f32[512,256]{1,0:T(8,128)S(1)}, f32[512,256]{1,0:T(8,128)}, u32[]{:S(2)}) copy-start(f32[512,256]{1,0:T(8,128)} %param.9) | copy-start | bytes 1572868
  62.3 10.9 %all-to-all-start.1 = ((f16[16,64,128]{2,1,0:T(8,128)(2,1)}), f16[16,64,128]{2,1,0:T(8,128)(2,1)S(1)}, u32[]{:S(2)}, u32[]{:S(2)}) async-start(f16[16,64,128]{2,1,0:T(8,128)(2,1)} %bitcast.14), calls=%async_computation.1 | async-start | bytes 524288 | tf_op jit(solution)/shard_map/all_to_all | solution.py:93
  65.9 7.5 %collective-permute-start.5 = (f32[2,64,128]{2,1,0:T(8,128)S(1)}, f32[2,64,128]{2,1,0:T(8,128)S(1)}, u32[]{:S(2)}, u32[]{:S(2)}) collective-permute-start(f32[2,64,128]{2,1,0:T(8,128)S(1)} %fusion.42), channel_id=1, source_target_pairs={{0,64},{32,96},{64,0},{96,32},{128,192},{160,224},{192,128},{224,1... | collective-permute-start | bytes 196616 | tf_op jit(solution)/shard_map/ppermute | solution.py:25
  73.3 8.6 %collective-permute-start.8 = (f32[64,128]{1,0:T(8,128)S(1)}, f32[64,128]{1,0:T(8,128)S(1)}, u32[]{:S(2)}, u32[]{:S(2)}) collective-permute-start(f32[64,128]{1,0:T(8,128)S(1)} %broadcast_multiply_fusion), channel_id=1, source_target_pairs={{0,32},{32,0},{64,96},{96,64},{128,160},{160,128},{192,224},{224,1... | collective-permute-start | bytes 98312 | tf_op jit(solution)/shard_map/ppermute | solution.py:25
  73.4 14.9 %collective-permute-start.6 = (f32[2,64,128]{2,1,0:T(8,128)S(1)}, f32[2,64,128]{2,1,0:T(8,128)S(1)}, u32[]{:S(2)}, u32[]{:S(2)}) collective-permute-start(f32[2,64,128]{2,1,0:T(8,128)S(1)} %fusion.52), channel_id=1, source_target_pairs={{0,128},{32,160},{64,192},{96,224},{128,0},{160,32},{192,64},{224,... | collective-permute-start | bytes 196616 | tf_op jit(solution)/shard_map/ppermute | solution.py:25
  81.9 4.2 %collective-permute-start.9 = (f32[64,128]{1,0:T(8,128)S(1)}, f32[64,128]{1,0:T(8,128)S(1)}, u32[]{:S(2)}, u32[]{:S(2)}) collective-permute-start(f32[64,128]{1,0:T(8,128)S(1)} %fusion.39), channel_id=1, source_target_pairs={{0,64},{32,96},{64,0},{96,32},{128,192},{160,224},{192,128},{224,1... | collective-permute-start | bytes 98312 | tf_op jit(solution)/shard_map/ppermute | solution.py:25
  86.1 6.7 %collective-permute-start.10 = (f32[64,128]{1,0:T(8,128)S(1)}, f32[64,128]{1,0:T(8,128)S(1)}, u32[]{:S(2)}, u32[]{:S(2)}) collective-permute-start(f32[64,128]{1,0:T(8,128)S(1)} %add.83), channel_id=1, source_target_pairs={{0,128},{32,160},{64,192},{96,224},{128,0},{160,32},{192,64},{224,... | collective-permute-start | bytes 98312 | tf_op jit(solution)/shard_map/ppermute | solution.py:25
  92.8 3.2 %collective-permute-start.12 = (f32[2,64,128]{2,1,0:T(8,128)S(1)}, f32[2,64,128]{2,1,0:T(8,128)S(1)}, u32[]{:S(2)}, u32[]{:S(2)}) collective-permute-start(f32[2,64,128]{2,1,0:T(8,128)S(1)} %pad_maximum_fusion.4), channel_id=1, source_target_pairs={{0,16},{16,0},{1,17},{17,1},{2,18},{18,2},{3,19},{19,3},{4,20},{20... | collective-permute-start | bytes 196616 | tf_op jit(solution)/shard_map/ppermute | solution.py:25
  96.1 12.2 %collective-permute-start.13 = (f32[2,64,128]{2,1,0:T(8,128)S(1)}, f32[2,64,128]{2,1,0:T(8,128)S(1)}, u32[]{:S(2)}, u32[]{:S(2)}) collective-permute-start(f32[2,64,128]{2,1,0:T(8,128)S(1)} %get-tuple-element.19), channel_id=1, source_target_pairs={{0,1},{1,0},{2,3},{3,2},{4,5},{5,4},{6,7},{7,6},{8,9},{9,8},{10,11... | collective-permute-start | bytes 196616 | tf_op jit(solution)/shard_map/ppermute | solution.py:25
  104.7 11.4 %all-to-all-start.2 = ((bf16[16,64,128]{2,1,0:T(8,128)(2,1)}), bf16[16,64,128]{2,1,0:T(8,128)(2,1)S(1)}, u32[]{:S(2)}, u32[]{:S(2)}) async-start(bf16[16,64,128]{2,1,0:T(8,128)(2,1)} %broadcast_in_dim.2), calls=%async_computation.2 | async-start | bytes 524288 | tf_op jit(solution)/shard_map/all_to_all | solution.py:105
  116.0 2.8 %collective-permute-start.11 = (bf16[1024,128]{1,0:T(8,128)(2,1)S(1)}, bf16[1024,128]{1,0:T(8,128)(2,1)S(1)}, u32[]{:S(2)}, u32[]{:S(2)}) collective-permute-start(bf16[1024,128]{1,0:T(8,128)(2,1)S(1)} %bitcast.64), channel_id=1, source_target_pairs={{0,1},{1,0},{2,3},{3,2},{4,5},{5,4},{6,7},{7,6},{8,9},{9,8},{10,11... | collective-permute-start | bytes 786440 | tf_op jit(solution)/shard_map/ppermute | solution.py:25

commit v3 on v2

--- a/solution.py
+++ b/solution.py
@@ -32,9 +32,7 @@
 def pieces(value):
     high = lax.reduce_precision(value, 8, 7)
     rest = value - high
-    mid = lax.reduce_precision(rest, 8, 7)
-    low = rest - mid
-    return jnp.concatenate([high, mid, low], axis=1).astype(jnp.bfloat16)
+    return jnp.concatenate([high, rest], axis=1).astype(jnp.bfloat16)
 
 
 def on_device(partials, p_old, p_new, weight, m_old, v_old):
@@ -52,7 +50,10 @@
     p_other = swap(p_new, "core", 1, 2)
 
     turn = [(a * 8 + b, a * 8 + (a ^ b)) for a in range(8) for b in range(8)]
-    turned = lax.ppermute(jnp.stack([m_old, v_old]), ("z", "x", "yh"), turn)
+    moments = jnp.stack([m_old, v_old])
+    moments_in = swap(cut(moments, 1 - core, 128, 2), "core", 1, 2)
+    moments = sides(cut(moments, core, 128, 2), moments_in, 1)
+    moments = lax.ppermute(moments, ("z", "x", "yh"), turn)
 
     p_rank = lax.dynamic_index_in_dim(p_new.reshape(512, 8, 2, 64), yl, 2, keepdims=False)
     product = jnp.dot(p_rank.reshape(512, 512).T, p_old, preferred_element_type=f32)
@@ -68,17 +69,7 @@
     ours = cut(grad, core, 128, 1)
     chip_sum = ((ours.astype(f32) + theirs.astype(f32)) * SCALE).astype(jnp.float16)
     sent = jnp.concatenate([chip_sum.reshape(8, 1024, 128), margin], axis=1)
-    sent, turned = lax.optimization_barrier((sent, turned))
     rows = lax.all_to_all(sent, PAIRS, 0, 0, tiled=True)
-
-    moments_in = swap(cut(turned, 1 - core, 128, 2), "core", 1, 2)
-    moments = sides(cut(turned, core, 128, 2), moments_in, 1)
-    margin = jnp.sum(rows[:, 1024:].astype(f32), axis=0) * (1.0 / MARGIN_SCALE)
-    first = jnp.dot(margin, moments[0], precision=lax.Precision.HIGHEST)
-    second = jnp.dot(margin * margin, moments[1], precision=lax.Precision.HIGHEST)
-    rotated = jnp.stack([first, second])
-    for bit in (1, 2, 4):
-        rotated = rotated + swap(rotated, "z", bit, 8)
 
     grad_rows = jnp.sum(rows[:, :1024].astype(f32), axis=0) * (1.0 / SCALE)
     split = pieces(grad_rows)
@@ -88,21 +79,30 @@
     ) + lax.dot_general(
         p_other, cut(split, 1 - core, 512, 0), across, preferred_element_type=f32
     )
-    projected = terms[:, :128] + terms[:, 128:256] + terms[:, 256:]
+    projected = terms[:, :128] + terms[:, 128:]
     projected = (projected * PROJECTED_SCALE).astype(jnp.float16)
+    projected, rows = lax.optimization_barrier((projected, rows))
     projected = lax.all_to_all(projected.reshape(16, 64, 128), PLANE, 0, 0, tiled=True)
     projected = jnp.sum(projected.astype(f32), axis=0) * (1.0 / PROJECTED_SCALE)
+    margin = jnp.sum(rows[:, 1024:].astype(f32), axis=0) * (1.0 / MARGIN_SCALE)
+    first = jnp.dot(margin, moments[0], precision=lax.Precision.HIGHEST)
+    second = jnp.dot(margin * margin, moments[1], precision=lax.Precision.HIGHEST)
+    shares = jnp.stack([projected, first, second])
     for bit in (1, 2, 4):
-        projected = projected + swap(projected, "z", bit, 8)
+        shares = shares + swap(shares, "z", bit, 8)
+    projected, first, second = shares[0], shares[1], shares[2]
 
-    m_new = beta_mean * rotated[0] + (1.0 - beta_mean) * projected
-    v_new = beta_square * rotated[1] + (1.0 - beta_square) * projected * projected
+    m_new = beta_mean * first + (1.0 - beta_mean) * projected
+    v_new = beta_square * second + (1.0 - beta_square) * projected * projected
     direction = (m_new / bias_mean / (jnp.sqrt(v_new / bias_square) + adam_epsilon)).astype(
         jnp.bfloat16
     )
 
     spread = jnp.broadcast_to(direction[None], (16, 64, 128))
     mine = lax.all_to_all(spread, PLANE, 0, 0, tiled=True).reshape(1024, 128)
+    made = jnp.stack([m_new, v_new])
+    near = swap(made, "yl", 1, 2)
+    near, mine = lax.optimization_barrier((near, mine))
     other = swap(mine, "core", 1, 2)
     update = sides(
         jnp.dot(p_new, mine, preferred_element_type=f32),
@@ -111,8 +111,6 @@
     )
     new_weight = weight - step_scale * update
 
-    made = jnp.stack([m_new, v_new])
-    near = swap(made, "yl", 1, 2)
     kept = jnp.where(core == yl, made, near)
     given = jnp.where(core == yl, near, made)
     made = sides(kept, swap(given, "core", 1, 2), 2)

time: 121 us -> 114 us (0.942)
  starting transfers between devices: 45.2 us -> 40.9 us
  waiting for transfers between devices: 53.2 us -> 48.9 us
  matrix products: 3.24 us -> 4.65 us
    ppermute x13 -> x10, starting transfers between devices: 31.5 us -> 27.4 us  [swap(): return lax.ppermute(value, axis, [(i, i ^ bit) for i in range(size)])]
    all_to_all x1, waiting for transfers between devices: 7.12 us -> 3.64 us  [on_device(): mine = lax.all_to_all(spread, PLANE, 0, 0, tiled=True).reshape(1024, 128)]
    all_to_all x1, waiting for transfers between devices: 30.9 us -> 28.3 us  [on_device(): rows = lax.all_to_all(sent, PAIRS, 0, 0, tiled=True)]
    ppermute x13 -> x10, waiting for transfers between devices: 11.8 us -> 12.6 us  [swap(): return lax.ppermute(value, axis, [(i, i ^ bit) for i in range(size)])]
    dynamic_slice x2 -> x1, local copies, waits for them, and re-layouts: 3.21 us -> 3.21 us  [cut(): return lax.dynamic_slice_in_dim(value, at * extent, extent, axis)]
  transfers between devices with their start and end apart: 17 -> 14, of which waited for: 8 -> 10; matrix products, arithmetic and copies ran while one was open for 14% -> 10% of each run, Pallas kernels for 0% -> 0%
where the time goes in v3:
time: 114 us; the launch traced here: 113 us
  waiting for transfers between devices  48.9 us (43%)
  starting transfers between devices  40.9 us (36%)
  other arithmetic  10.5 us (9%)
  local copies, waits for them, and re-layouts  7.35 us (6%)
  matrix products  4.65 us (4%)
    all_to_all x1, waiting for transfers between devices, on_device(): rows = lax.all_to_all(sent, PAIRS, 0, 0, tiled=True)  28.3 us
    ppermute x10, starting transfers between devices, swap(): return lax.ppermute(value, axis, [(i, i ^ bit) for i in range(size)])  27.4 us
    ppermute x10, waiting for transfers between devices, swap(): return lax.ppermute(value, axis, [(i, i ^ bit) for i in range(size)])  12.6 us
    all_to_all x1, starting transfers between devices, on_device(): rows = lax.all_to_all(sent, PAIRS, 0, 0, tiled=True)  5.05 us
    all_to_all x1, waiting for transfers between devices, on_device(): lax.all_to_all(projected.reshape(16, 64, 128), PLANE, 0, 0, tiled=True)  4.28 us
    all_to_all x1, starting transfers between devices, on_device(): mine = lax.all_to_all(spread, PLANE, 0, 0, tiled=True).reshape(1024, 128)  3.67 us
    all_to_all x1, waiting for transfers between devices, on_device(): mine = lax.all_to_all(spread, PLANE, 0, 0, tiled=True).reshape(1024, 128)  3.64 us
    all_to_all x1, starting transfers between devices, on_device(): lax.all_to_all(projected.reshape(16, 64, 128), PLANE, 0, 0, tiled=True)  3.53 us
  transfers between devices with their start and end apart: 14, of which 10 were waited for; matrix products, arithmetic and copies ran while one was open for 10% of the time, Pallas kernels for 0%

profile of v3, /device:TPU:1, one launch (start us, length us, event | category | flops | bytes accessed | tf_op | source)
XLA Modules:
  0.0 113.2 jit_solution(5969490229558874508)
XLA Ops:
  0.7 3.2 %dynamic-slice_bitcast_fusion = bf16[8192,128]{1,0:T(8,128)(2,1)} fusion(bf16[1,8192,256]{2,1,0:T(8,128)(2,1)} %param.6, s32[]{:T(128)S(6)} %select_n.83), kind=kLoop, calls=%fused_computation.5 | loop fusion | bytes 4194308 | tf_op jit(solution)/shard_map/dynamic_slice | solution.py:29
  3.9 3.2 %collective-permute-start = (bf16[8192,128]{1,0:T(8,128)(2,1)}, bf16[8192,128]{1,0:T(8,128)(2,1)}, u32[]{:S(2)}, u32[]{:S(2)}) collective-permute-start(bf16[8192,128]{1,0:T(8,128)(2,1)} %dynamic-slice_bitcast_fusion), channel_id=1, source_target_pairs={{0,1},{1,0},{2,3},{3,2},{4,5},{5,4},{6,7},{7,6},{8,9},{9,8},{10,11... | collective-permute-start | bytes 6291464 | tf_op jit(solution)/shard_map/ppermute | solution.py:25
  7.1 0.5 copy.11
  7.7 0.1 constant_dynamic-slice_fusion
  7.8 0.7 fusion.48
  8.5 1.0 fusion.18
  9.5 2.0 %collective-permute-done.1 = f32[512,128]{1,0:T(8,128)S(1)} collective-permute-done((f32[512,128]{1,0:T(8,128)}, f32[512,128]{1,0:T(8,128)S(1)}, u32[]{:S(2)}, u32[]{:S(2)}) %collective-permute-start.1) | collective-permute-done | bytes 262176 | tf_op jit(solution)/shard_map/ppermute | solution.py:25
  11.5 0.3 multiply_convert_fusion
  11.8 3.0 %fusion.1 = f16[8192,128]{1,0:T(8,128)(2,1)S(1)} fusion(bf16[8192,128]{1,0:T(8,128)(2,1)} %collective-permute-done, bf16[1,8192,256]{2,1,0:T(8,128)(2,1)} %param.6, s32[]{:T(128)S(6)} %select_n.82), kind=kLoop, calls=%fused_computation.2 | loop fusion | flops 5242880 | bytes 6291460 | tf_op jit(solution)/shard_map/convert_element_type | solution.py:70
  14.8 2.0 %pad_maximum_fusion = f16[8,1088,128]{2,1,0:T(8,128)(2,1)} fusion(f16[8,64,128]{2,1,0:T(8,128)(2,1)S(1)} %bitcast.50, f16[8,1024,128]{2,1,0:T(8,128)(2,1)S(1)} %bitcast.45), kind=kLoop, calls=%fused_computation.4 | loop fusion | flops 1114112 | bytes 4456448 | tf_op jit(solution)/shard_map/concatenate | solution.py:71
  16.9 5.0 %all-to-all-start = ((f16[8,1088,128]{2,1,0:T(8,128)(2,1)}), f16[8,1088,128]{2,1,0:T(8,128)(2,1)}, u32[]{:S(2)}, u32[]{:S(2)}) async-start(f16[8,1088,128]{2,1,0:T(8,128)(2,1)} %pad_maximum_fusion), calls=%async_computation | async-start | bytes 4456448 | tf_op jit(solution)/shard_map/all_to_all | solution.py:72
  21.9 0.7 collective-permute-start.2
  22.7 0.1 collective-permute-start.3
  22.8 2.2 %collective-permute-done.3 = f32[2,64,128]{2,1,0:T(8,128)S(1)} collective-permute-done((f32[2,64,128]{2,1,0:T(8,128)S(1)}, f32[2,64,128]{2,1,0:T(8,128)S(1)}, u32[]{:S(2)}, u32[]{:S(2)}) %collective-permute-start.3) | collective-permute-done | bytes 65568 | tf_op jit(solution)/shard_map/ppermute | solution.py:25
  25.0 1.3 %collective-permute-start.4 = (f32[2,128,128]{2,1,0:T(8,128)S(1)}, f32[2,128,128]{2,1,0:T(8,128)}, u32[]{:S(2)}, u32[]{:S(2)}) collective-permute-start(f32[2,128,128]{2,1,0:T(8,128)S(1)} %maximum_select_fusion.1), channel_id=1, source_target_pairs={{0,0},{2,2},{4,4},{6,6},{8,8},{10,10},{12,12},{14,14},{32,34},{34,... | collective-permute-start | bytes 393224 | tf_op jit(solution)/shard_map/ppermute | solution.py:56
  26.3 28.3 %all-to-all-done = f16[8,1088,128]{2,1,0:T(8,128)(2,1)} async-done(((f16[8,1088,128]{2,1,0:T(8,128)(2,1)}), f16[8,1088,128]{2,1,0:T(8,128)(2,1)}, u32[]{:S(2)}, u32[]{:S(2)}) %all-to-all-start) | async-done | bytes 2228256 | tf_op jit(solution)/shard_map/all_to_all | solution.py:72
  54.7 1.9 %convert_reduce_fusion = f32[1024,128]{1,0:T(8,128)S(1)} fusion(f16[8,1088,128]{2,1,0:T(8,128)(2,1)} %all-to-all-done), kind=kLoop, calls=%fused_computation.3 | loop fusion | flops 1966080 | bytes 2621440 | tf_op jit(solution)/shard_map/reduce_sum | solution.py:74
  56.6 0.1 fusion.3
  56.7 0.5 fusion.11
  57.2 0.5 fusion.2
  57.7 0.1 fusion.5
  57.8 0.9 copy.12
  58.7 3.5 %all-to-all-start.1 = ((f16[16,64,128]{2,1,0:T(8,128)(2,1)}), f16[16,64,128]{2,1,0:T(8,128)(2,1)S(1)}, u32[]{:S(2)}, u32[]{:S(2)}) async-start(f16[16,64,128]{2,1,0:T(8,128)(2,1)} %bitcast.7), calls=%async_computation.1 | async-start | bytes 524288 | tf_op jit(solution)/shard_map/all_to_all | solution.py:85
  62.2 0.9 convert_reduce_fusion.2
  63.2 1.0 convolution_bitcast_fusion.3
  64.2 1.0 convolution_bitcast_fusion.2
  65.2 4.3 %all-to-all-done.1 = f16[16,64,128]{2,1,0:T(8,128)(2,1)S(1)} async-done(((f16[16,64,128]{2,1,0:T(8,128)(2,1)}), f16[16,64,128]{2,1,0:T(8,128)(2,1)S(1)}, u32[]{:S(2)}, u32[]{:S(2)}) %all-to-all-start.1) | async-done | bytes 262176 | tf_op jit(solution)/shard_map/all_to_all | solution.py:85
  69.6 1.7 %collective-permute-start.5 = (f32[3,64,128]{2,1,0:T(8,128)S(1)}, f32[3,64,128]{2,1,0:T(8,128)S(1)}, u32[]{:S(2)}, u32[]{:S(2)}) collective-permute-start(f32[3,64,128]{2,1,0:T(8,128)S(1)} %pad_maximum_fusion.1), channel_id=1, source_target_pairs={{0,32},{32,0},{64,96},{96,64},{128,160},{160,128},{192,224},{224,1... | collective-permute-start | bytes 294920 | tf_op jit(solution)/shard_map/ppermute | solution.py:25
  71.3 2.0 %collective-permute-done.5 = f32[3,64,128]{2,1,0:T(8,128)S(1)} collective-permute-done((f32[3,64,128]{2,1,0:T(8,128)S(1)}, f32[3,64,128]{2,1,0:T(8,128)S(1)}, u32[]{:S(2)}, u32[]{:S(2)}) %collective-permute-start.5) | collective-permute-done | bytes 98336 | tf_op jit(solution)/shard_map/ppermute | solution.py:25
  73.3 3.1 %collective-permute-start.6 = (f32[3,64,128]{2,1,0:T(8,128)S(1)}, f32[3,64,128]{2,1,0:T(8,128)S(1)}, u32[]{:S(2)}, u32[]{:S(2)}) collective-permute-start(f32[3,64,128]{2,1,0:T(8,128)S(1)} %fusion.45), channel_id=1, source_target_pairs={{0,64},{32,96},{64,0},{96,32},{128,192},{160,224},{192,128},{224,1... | collective-permute-start | bytes 294920 | tf_op jit(solution)/shard_map/ppermute | solution.py:25
  76.5 2.0 %collective-permute-done.6 = f32[3,64,128]{2,1,0:T(8,128)S(1)} collective-permute-done((f32[3,64,128]{2,1,0:T(8,128)S(1)}, f32[3,64,128]{2,1,0:T(8,128)S(1)}, u32[]{:S(2)}, u32[]{:S(2)}) %collective-permute-start.6) | collective-permute-done | bytes 98336 | tf_op jit(solution)/shard_map/ppermute | solution.py:25
  78.5 9.5 %collective-permute-start.7 = (f32[3,64,128]{2,1,0:T(8,128)S(1)}, f32[3,64,128]{2,1,0:T(8,128)S(1)}, u32[]{:S(2)}, u32[]{:S(2)}) collective-permute-start(f32[3,64,128]{2,1,0:T(8,128)S(1)} %fusion.57), channel_id=1, source_target_pairs={{0,128},{32,160},{64,192},{96,224},{128,0},{160,32},{192,64},{224,... | collective-permute-start | bytes 294920 | tf_op jit(solution)/shard_map/ppermute | solution.py:25
  87.9 2.0 %collective-permute-done.7 = f32[3,64,128]{2,1,0:T(8,128)S(1)} collective-permute-done((f32[3,64,128]{2,1,0:T(8,128)S(1)}, f32[3,64,128]{2,1,0:T(8,128)S(1)}, u32[]{:S(2)}, u32[]{:S(2)}) %collective-permute-start.7) | collective-permute-done | bytes 98336 | tf_op jit(solution)/shard_map/ppermute | solution.py:25
  90.0 0.8 broadcast_in_dim.9
  90.8 3.7 %all-to-all-start.2 = ((bf16[16,64,128]{2,1,0:T(8,128)(2,1)}), bf16[16,64,128]{2,1,0:T(8,128)(2,1)S(1)}, u32[]{:S(2)}, u32[]{:S(2)}) async-start(bf16[16,64,128]{2,1,0:T(8,128)(2,1)} %broadcast_in_dim.9), calls=%async_computation.2 | async-start | bytes 524288 | tf_op jit(solution)/shard_map/all_to_all | solution.py:102
  94.5 1.4 %collective-permute-start.8 = (f32[2,64,128]{2,1,0:T(8,128)S(1)}, f32[2,64,128]{2,1,0:T(8,128)}, u32[]{:S(2)}, u32[]{:S(2)}) collective-permute-start(f32[2,64,128]{2,1,0:T(8,128)S(1)} %pad_maximum_fusion.2), channel_id=1, source_target_pairs={{0,16},{16,0},{1,17},{17,1},{2,18},{18,2},{3,19},{19,3},{4,20},{20... | collective-permute-start | bytes 196616 | tf_op jit(solution)/shard_map/ppermute | solution.py:25
  95.9 0.2 copy.13
  96.1 2.0 %collective-permute-done.8 = f32[2,64,128]{2,1,0:T(8,128)} collective-permute-done((f32[2,64,128]{2,1,0:T(8,128)S(1)}, f32[2,64,128]{2,1,0:T(8,128)}, u32[]{:S(2)}, u32[]{:S(2)}) %collective-permute-start.8) | collective-permute-done | bytes 65568 | tf_op jit(solution)/shard_map/ppermute | solution.py:25
  98.1 3.6 %all-to-all-done.2 = bf16[16,64,128]{2,1,0:T(8,128)(2,1)S(1)} async-done(((bf16[16,64,128]{2,1,0:T(8,128)(2,1)}), bf16[16,64,128]{2,1,0:T(8,128)(2,1)S(1)}, u32[]{:S(2)}, u32[]{:S(2)}) %all-to-all-start.2) | async-done | bytes 262176 | tf_op jit(solution)/shard_map/all_to_all | solution.py:102
  101.8 0.9 broadcast_select_fusion.1
  102.6 7.4 %collective-permute-start.10 = (f32[2,64,128]{2,1,0:T(8,128)S(1)}, f32[2,64,128]{2,1,0:T(8,128)S(1)}, u32[]{:S(2)}, u32[]{:S(2)}) collective-permute-start(f32[2,64,128]{2,1,0:T(8,128)S(1)} %get-tuple-element.25), channel_id=1, source_target_pairs={{0,1},{1,0},{2,3},{3,2},{4,5},{5,4},{6,7},{7,6},{8,9},{9,8},{10,11... | collective-permute-start | bytes 196616 | tf_op jit(solution)/shard_map/ppermute | solution.py:25
  110.0 0.1 collective-permute-start.9
  110.1 0.5 convolution_bitcast_fusion.1
  110.6 0.3 collective-permute-done.10
  110.9 0.7 slice_bitcast_fusion
  111.6 0.5 convolution_bitcast_fusion
  112.1 0.1 fusion.7
  112.2 1.0 copy.14
  (30 shorter events, 0.2 us)
Async XLA Ops:
  0.6 7.1 %copy-start = (bf16[512,1024]{1,0:T(8,128)(2,1)S(1)}, bf16[512,1024]{1,0:T(8,128)(2,1)}, u32[]{:S(2)}) copy-start(bf16[512,1024]{1,0:T(8,128)(2,1)} %param.7) | copy-start | bytes 3145732
  0.6 6.5 %copy-start.1 = (bf16[512,1024]{1,0:T(8,128)(2,1)S(1)}, bf16[512,1024]{1,0:T(8,128)(2,1)}, u32[]{:S(2)}) copy-start(bf16[512,1024]{1,0:T(8,128)(2,1)} %param.8) | copy-start | bytes 3145732
  3.9 7.9 %collective-permute-start = (bf16[8192,128]{1,0:T(8,128)(2,1)}, bf16[8192,128]{1,0:T(8,128)(2,1)}, u32[]{:S(2)}, u32[]{:S(2)}) collective-permute-start(bf16[8192,128]{1,0:T(8,128)(2,1)} %dynamic-slice_bitcast_fusion), channel_id=1, source_target_pairs={{0,1},{1,0},{2,3},{3,2},{4,5},{5,4},{6,7},{7,6},{8,9},{9,8},{10,11... | collective-permute-start | bytes 6291464 | tf_op jit(solution)/shard_map/ppermute | solution.py:25
  9.5 2.0 %collective-permute-start.1 = (f32[512,128]{1,0:T(8,128)}, f32[512,128]{1,0:T(8,128)S(1)}, u32[]{:S(2)}, u32[]{:S(2)}) collective-permute-start(f32[512,128]{1,0:T(8,128)} %fusion.18), channel_id=1, source_target_pairs={{0,1},{1,0},{2,3},{3,2},{4,5},{5,4},{6,7},{7,6},{8,9},{9,8},{10,11... | collective-permute-start | bytes 786440 | tf_op jit(solution)/shard_map/ppermute | solution.py:25
  16.8 5.1 %copy-start.2 = (bf16[512,1024]{1,0:T(8,128)(2,1)S(1)}, bf16[512,1024]{1,0:T(8,128)(2,1)}, u32[]{:S(2)}) copy-start(bf16[512,1024]{1,0:T(8,128)(2,1)} %param.8) | copy-start | bytes 3145732
  16.9 5.8 %copy-start.4 = (f32[64,256]{1,0:T(8,128)S(1)}, f32[64,256]{1,0:T(8,128)}, u32[]{:S(2)}) copy-start(f32[64,256]{1,0:T(8,128)} %param.10) | copy-start | bytes 196612
  16.9 5.8 %copy-start.5 = (f32[64,256]{1,0:T(8,128)S(1)}, f32[64,256]{1,0:T(8,128)}, u32[]{:S(2)}) copy-start(f32[64,256]{1,0:T(8,128)} %param.11) | copy-start | bytes 196612
  16.9 37.8 %all-to-all-start = ((f16[8,1088,128]{2,1,0:T(8,128)(2,1)}), f16[8,1088,128]{2,1,0:T(8,128)(2,1)}, u32[]{:S(2)}, u32[]{:S(2)}) async-start(f16[8,1088,128]{2,1,0:T(8,128)(2,1)} %pad_maximum_fusion), calls=%async_computation | async-start | bytes 4456448 | tf_op jit(solution)/shard_map/all_to_all | solution.py:72
  21.9 35.3 %collective-permute-start.2 = (bf16[512,1024]{1,0:T(8,128)(2,1)S(1)}, bf16[512,1024]{1,0:T(8,128)(2,1)S(1)}, u32[]{:S(2)}, u32[]{:S(2)}) collective-permute-start(bf16[512,1024]{1,0:T(8,128)(2,1)S(1)} %copy-done.2), channel_id=1, source_target_pairs={{0,1},{1,0},{2,3},{3,2},{4,5},{5,4},{6,7},{7,6},{8,9},{9,8},{10,11... | collective-permute-start | bytes 3145736 | tf_op jit(solution)/shard_map/ppermute | solution.py:25
  22.7 2.4 %collective-permute-start.3 = (f32[2,64,128]{2,1,0:T(8,128)S(1)}, f32[2,64,128]{2,1,0:T(8,128)S(1)}, u32[]{:S(2)}, u32[]{:S(2)}) collective-permute-start(f32[2,64,128]{2,1,0:T(8,128)S(1)} %get-tuple-element.27), channel_id=1, source_target_pairs={{0,1},{1,0},{2,3},{3,2},{4,5},{5,4},{6,7},{7,6},{8,9},{9,8},{10,11... | collective-permute-start | bytes 196616 | tf_op jit(solution)/shard_map/ppermute | solution.py:25
  25.0 38.1 %collective-permute-start.4 = (f32[2,128,128]{2,1,0:T(8,128)S(1)}, f32[2,128,128]{2,1,0:T(8,128)}, u32[]{:S(2)}, u32[]{:S(2)}) collective-permute-start(f32[2,128,128]{2,1,0:T(8,128)S(1)} %maximum_select_fusion.1), channel_id=1, source_target_pairs={{0,0},{2,2},{4,4},{6,6},{8,8},{10,10},{12,12},{14,14},{32,34},{34,... | collective-permute-start | bytes 393224 | tf_op jit(solution)/shard_map/ppermute | solution.py:56
  57.8 38.1 %copy-start.3 = (f32[512,256]{1,0:T(8,128)S(1)}, f32[512,256]{1,0:T(8,128)}, u32[]{:S(2)}) copy-start(f32[512,256]{1,0:T(8,128)} %param.9) | copy-start | bytes 1572868
  58.7 10.8 %all-to-all-start.1 = ((f16[16,64,128]{2,1,0:T(8,128)(2,1)}), f16[16,64,128]{2,1,0:T(8,128)(2,1)S(1)}, u32[]{:S(2)}, u32[]{:S(2)}) async-start(f16[16,64,128]{2,1,0:T(8,128)(2,1)} %bitcast.7), calls=%async_computation.1 | async-start | bytes 524288 | tf_op jit(solution)/shard_map/all_to_all | solution.py:85
  69.6 3.7 %collective-permute-start.5 = (f32[3,64,128]{2,1,0:T(8,128)S(1)}, f32[3,64,128]{2,1,0:T(8,128)S(1)}, u32[]{:S(2)}, u32[]{:S(2)}) collective-permute-start(f32[3,64,128]{2,1,0:T(8,128)S(1)} %pad_maximum_fusion.1), channel_id=1, source_target_pairs={{0,32},{32,0},{64,96},{96,64},{128,160},{160,128},{192,224},{224,1... | collective-permute-start | bytes 294920 | tf_op jit(solution)/shard_map/ppermute | solution.py:25
  73.3 5.1 %collective-permute-start.6 = (f32[3,64,128]{2,1,0:T(8,128)S(1)}, f32[3,64,128]{2,1,0:T(8,128)S(1)}, u32[]{:S(2)}, u32[]{:S(2)}) collective-permute-start(f32[3,64,128]{2,1,0:T(8,128)S(1)} %fusion.45), channel_id=1, source_target_pairs={{0,64},{32,96},{64,0},{96,32},{128,192},{160,224},{192,128},{224,1... | collective-permute-start | bytes 294920 | tf_op jit(solution)/shard_map/ppermute | solution.py:25
  78.5 11.5 %collective-permute-start.7 = (f32[3,64,128]{2,1,0:T(8,128)S(1)}, f32[3,64,128]{2,1,0:T(8,128)S(1)}, u32[]{:S(2)}, u32[]{:S(2)}) collective-permute-start(f32[3,64,128]{2,1,0:T(8,128)S(1)} %fusion.57), channel_id=1, source_target_pairs={{0,128},{32,160},{64,192},{96,224},{128,0},{160,32},{192,64},{224,... | collective-permute-start | bytes 294920 | tf_op jit(solution)/shard_map/ppermute | solution.py:25
  90.8 11.0 %all-to-all-start.2 = ((bf16[16,64,128]{2,1,0:T(8,128)(2,1)}), bf16[16,64,128]{2,1,0:T(8,128)(2,1)S(1)}, u32[]{:S(2)}, u32[]{:S(2)}) async-start(bf16[16,64,128]{2,1,0:T(8,128)(2,1)} %broadcast_in_dim.9), calls=%async_computation.2 | async-start | bytes 524288 | tf_op jit(solution)/shard_map/all_to_all | solution.py:102
  94.5 3.7 %collective-permute-start.8 = (f32[2,64,128]{2,1,0:T(8,128)S(1)}, f32[2,64,128]{2,1,0:T(8,128)}, u32[]{:S(2)}, u32[]{:S(2)}) collective-permute-start(f32[2,64,128]{2,1,0:T(8,128)S(1)} %pad_maximum_fusion.2), channel_id=1, source_target_pairs={{0,16},{16,0},{1,17},{17,1},{2,18},{18,2},{3,19},{19,3},{4,20},{20... | collective-permute-start | bytes 196616 | tf_op jit(solution)/shard_map/ppermute | solution.py:25
  102.6 8.3 %collective-permute-start.10 = (f32[2,64,128]{2,1,0:T(8,128)S(1)}, f32[2,64,128]{2,1,0:T(8,128)S(1)}, u32[]{:S(2)}, u32[]{:S(2)}) collective-permute-start(f32[2,64,128]{2,1,0:T(8,128)S(1)} %get-tuple-element.25), channel_id=1, source_target_pairs={{0,1},{1,0},{2,3},{3,2},{4,5},{5,4},{6,7},{7,6},{8,9},{9,8},{10,11... | collective-permute-start | bytes 196616 | tf_op jit(solution)/shard_map/ppermute | solution.py:25
  110.0 1.6 %collective-permute-start.9 = (bf16[1024,128]{1,0:T(8,128)(2,1)S(1)}, bf16[1024,128]{1,0:T(8,128)(2,1)S(1)}, u32[]{:S(2)}, u32[]{:S(2)}) collective-permute-start(bf16[1024,128]{1,0:T(8,128)(2,1)S(1)} %bitcast.48), channel_id=1, source_target_pairs={{0,1},{1,0},{2,3},{3,2},{4,5},{5,4},{6,7},{7,6},{8,9},{9,8},{10,11... | collective-permute-start | bytes 786440 | tf_op jit(solution)/shard_map/ppermute | solution.py:25

commit v4 on v3

--- a/solution.py
+++ b/solution.py
@@ -50,10 +50,7 @@
     p_other = swap(p_new, "core", 1, 2)
 
     turn = [(a * 8 + b, a * 8 + (a ^ b)) for a in range(8) for b in range(8)]
-    moments = jnp.stack([m_old, v_old])
-    moments_in = swap(cut(moments, 1 - core, 128, 2), "core", 1, 2)
-    moments = sides(cut(moments, core, 128, 2), moments_in, 1)
-    moments = lax.ppermute(moments, ("z", "x", "yh"), turn)
+    turned = lax.ppermute(jnp.stack([m_old, v_old]), ("z", "x", "yh"), turn)
 
     p_rank = lax.dynamic_index_in_dim(p_new.reshape(512, 8, 2, 64), yl, 2, keepdims=False)
     product = jnp.dot(p_rank.reshape(512, 512).T, p_old, preferred_element_type=f32)
@@ -65,10 +62,11 @@
     margin = (margin * MARGIN_SCALE).astype(jnp.float16).reshape(8, 64, 128)
 
     grad = partials[0]
-    theirs = swap(cut(grad, 1 - core, 128, 1), "core", 1, 2)
+    theirs = cut(swap(grad, "core", 1, 2), core, 128, 1)
     ours = cut(grad, core, 128, 1)
     chip_sum = ((ours.astype(f32) + theirs.astype(f32)) * SCALE).astype(jnp.float16)
     sent = jnp.concatenate([chip_sum.reshape(8, 1024, 128), margin], axis=1)
+    sent, turned = lax.optimization_barrier((sent, turned))
     rows = lax.all_to_all(sent, PAIRS, 0, 0, tiled=True)
 
     grad_rows = jnp.sum(rows[:, :1024].astype(f32), axis=0) * (1.0 / SCALE)
@@ -84,6 +82,8 @@
     projected, rows = lax.optimization_barrier((projected, rows))
     projected = lax.all_to_all(projected.reshape(16, 64, 128), PLANE, 0, 0, tiled=True)
     projected = jnp.sum(projected.astype(f32), axis=0) * (1.0 / PROJECTED_SCALE)
+    moments_in = swap(cut(turned, 1 - core, 128, 2), "core", 1, 2)
+    moments = sides(cut(turned, core, 128, 2), moments_in, 1)
     margin = jnp.sum(rows[:, 1024:].astype(f32), axis=0) * (1.0 / MARGIN_SCALE)
     first = jnp.dot(margin, moments[0], precision=lax.Precision.HIGHEST)
     second = jnp.dot(margin * margin, moments[1], precision=lax.Precision.HIGHEST)

time: 114 us -> 113 us (level)
  waiting for transfers between devices: 48.9 us -> 52.5 us
  local copies, waits for them, and re-layouts: 7.35 us -> 5.11 us
  matrix products: 4.65 us -> 2.97 us
  starting transfers between devices: 40.9 us -> 39.7 us
    dynamic_slice x1, local copies, waits for them, and re-layouts: 3.21 us -> 0.01 us  [cut(): return lax.dynamic_slice_in_dim(value, at * extent, extent, axis)]
    ppermute x10, starting transfers between devices: 27.4 us -> 25.5 us  [swap(): return lax.ppermute(value, axis, [(i, i ^ bit) for i in range(size)])]
    all_to_all x1, waiting for transfers between devices: 4.28 us -> 5.97 us  [on_device(): lax.all_to_all(projected.reshape(16, 64, 128), PLANE, 0, 0, tiled=True)]
    all_to_all x1, waiting for transfers between devices: 28.3 us -> 29.6 us  [on_device(): rows = lax.all_to_all(sent, PAIRS, 0, 0, tiled=True)]
    unnamed x15 -> x13, local copies, waits for them, and re-layouts: 1.76 us -> 2.72 us
  transfers between devices with their start and end apart: 14 -> 14, of which waited for: 10 -> 10; matrix products, arithmetic and copies ran while one was open for 10% -> 13% of each run, Pallas kernels for 0% -> 0%
where the time goes in v4:
time: 113 us; the launch traced here: 112 us
  waiting for transfers between devices  52.5 us (46%)
  starting transfers between devices  39.7 us (35%)
  other arithmetic  11.2 us (10%)
  local copies, waits for them, and re-layouts  5.11 us (5%)
  matrix products  2.97 us (3%)
    all_to_all x1, waiting for transfers between devices, on_device(): rows = lax.all_to_all(sent, PAIRS, 0, 0, tiled=True)  29.6 us
    ppermute x10, starting transfers between devices, swap(): return lax.ppermute(value, axis, [(i, i ^ bit) for i in range(size)])  25.5 us
    ppermute x10, waiting for transfers between devices, swap(): return lax.ppermute(value, axis, [(i, i ^ bit) for i in range(size)])  13.2 us
    all_to_all x1, waiting for transfers between devices, on_device(): lax.all_to_all(projected.reshape(16, 64, 128), PLANE, 0, 0, tiled=True)  5.97 us
    all_to_all x1, starting transfers between devices, on_device(): rows = lax.all_to_all(sent, PAIRS, 0, 0, tiled=True)  5.05 us
    all_to_all x1, starting transfers between devices, on_device(): mine = lax.all_to_all(spread, PLANE, 0, 0, tiled=True).reshape(1024, 128)  4.07 us
    all_to_all x1, waiting for transfers between devices, on_device(): mine = lax.all_to_all(spread, PLANE, 0, 0, tiled=True).reshape(1024, 128)  3.64 us
    all_to_all x1, starting transfers between devices, on_device(): lax.all_to_all(projected.reshape(16, 64, 128), PLANE, 0, 0, tiled=True)  3.53 us
  transfers between devices with their start and end apart: 14, of which 10 were waited for; matrix products, arithmetic and copies ran while one was open for 13% of the time, Pallas kernels for 0%

profile of v4, /device:TPU:1, one launch (start us, length us, event | category | flops | bytes accessed | tf_op | source)
XLA Modules:
  0.0 112.3 jit_solution(6090683157594718688)
XLA Ops:
  0.6 3.3 %collective-permute-start = (bf16[8192,256]{1,0:T(8,128)(2,1)}, bf16[8192,256]{1,0:T(8,128)(2,1)}, u32[]{:S(2)}, u32[]{:S(2)}) collective-permute-start(bf16[8192,256]{1,0:T(8,128)(2,1)} %bitcast.47), channel_id=1, source_target_pairs={{0,1},{1,0},{2,3},{3,2},{4,5},{5,4},{6,7},{7,6},{8,9},{9,8},{10,11... | collective-permute-start | bytes 12582920 | tf_op jit(solution)/shard_map/ppermute | solution.py:25
  4.0 1.5 %copy.11 = bf16[512,1024]{0,1:T(8,128)(2,1)S(1)} copy(bf16[512,1024]{1,0:T(8,128)(2,1)} %param.8) | data formatting | bytes 2097152 | tf_op args[2]
  5.6 0.7 fusion.46
  6.3 1.0 fusion.18
  7.3 0.1 collective-permute-start.1
  7.4 0.7 pad_maximum_fusion.1
  8.1 1.6 %collective-permute-start.2 = (f32[2,64,256]{2,1,0:T(8,128)}, f32[2,64,256]{2,1,0:T(8,128)S(1)}, u32[]{:S(2)}, u32[]{:S(2)}) collective-permute-start(f32[2,64,256]{2,1,0:T(8,128)} %pad_maximum_fusion.1), channel_id=1, source_target_pairs={{0,0},{2,2},{4,4},{6,6},{8,8},{10,10},{12,12},{14,14},{32,34},{34,... | collective-permute-start | bytes 393224 | tf_op jit(solution)/shard_map/ppermute | solution.py:53
  9.6 1.7 %collective-permute-done.1 = f32[512,128]{1,0:T(8,128)S(1)} collective-permute-done((f32[512,128]{1,0:T(8,128)}, f32[512,128]{1,0:T(8,128)S(1)}, u32[]{:S(2)}, u32[]{:S(2)}) %collective-permute-start.1) | collective-permute-done | bytes 262176 | tf_op jit(solution)/shard_map/ppermute | solution.py:25
  11.3 0.3 multiply_convert_fusion
  11.6 3.0 %fusion.1 = f16[8192,128]{1,0:T(8,128)(2,1)S(1)} fusion(bf16[8192,256]{1,0:T(8,128)(2,1)} %collective-permute-done, s32[]{:T(128)S(6)} %select_n.82, bf16[1,8192,256]{2,1,0:T(8,128)(2,1)} %param.6), kind=kLoop, calls=%fused_computation.2 | loop fusion | flops 5242880 | bytes 6291460 | tf_op jit(solution)/shard_map/convert_element_type | solution.py:67
  14.7 2.0 %pad_maximum_fusion = f16[8,1088,128]{2,1,0:T(8,128)(2,1)} fusion(f16[8,64,128]{2,1,0:T(8,128)(2,1)S(1)} %bitcast.50, f16[8,1024,128]{2,1,0:T(8,128)(2,1)S(1)} %bitcast.44), kind=kLoop, calls=%fused_computation.4 | loop fusion | flops 1114112 | bytes 4456448 | tf_op jit(solution)/shard_map/concatenate | solution.py:68
  16.7 5.0 %all-to-all-start = ((f16[8,1088,128]{2,1,0:T(8,128)(2,1)}), f16[8,1088,128]{2,1,0:T(8,128)(2,1)}, u32[]{:S(2)}, u32[]{:S(2)}) async-start(f16[8,1088,128]{2,1,0:T(8,128)(2,1)} %pad_maximum_fusion), calls=%async_computation | async-start | bytes 4456448 | tf_op jit(solution)/shard_map/all_to_all | solution.py:70
  21.8 0.7 collective-permute-start.3
  22.5 0.1 collective-permute-start.4
  22.6 2.3 %collective-permute-done.4 = f32[2,64,128]{2,1,0:T(8,128)S(1)} collective-permute-done((f32[2,64,128]{2,1,0:T(8,128)S(1)}, f32[2,64,128]{2,1,0:T(8,128)S(1)}, u32[]{:S(2)}, u32[]{:S(2)}) %collective-permute-start.4) | collective-permute-done | bytes 65568 | tf_op jit(solution)/shard_map/ppermute | solution.py:25
  24.9 29.6 %all-to-all-done = f16[8,1088,128]{2,1,0:T(8,128)(2,1)} async-done(((f16[8,1088,128]{2,1,0:T(8,128)(2,1)}), f16[8,1088,128]{2,1,0:T(8,128)(2,1)}, u32[]{:S(2)}, u32[]{:S(2)}) %all-to-all-start) | async-done | bytes 2228256 | tf_op jit(solution)/shard_map/all_to_all | solution.py:70
  54.6 1.9 %convert_reduce_fusion = f32[1024,128]{1,0:T(8,128)S(1)} fusion(f16[8,1088,128]{2,1,0:T(8,128)(2,1)} %all-to-all-done), kind=kLoop, calls=%fused_computation.3 | loop fusion | flops 1966080 | bytes 2621440 | tf_op jit(solution)/shard_map/reduce_sum | solution.py:72
  56.5 0.1 fusion.3
  56.6 0.5 fusion.11
  57.1 0.5 fusion.2
  57.5 0.1 fusion.5
  57.6 0.9 copy.12
  58.5 3.5 %all-to-all-start.1 = ((f16[16,64,128]{2,1,0:T(8,128)(2,1)}), f16[16,64,128]{2,1,0:T(8,128)(2,1)S(1)}, u32[]{:S(2)}, u32[]{:S(2)}) async-start(f16[16,64,128]{2,1,0:T(8,128)(2,1)} %bitcast.9), calls=%async_computation.1 | async-start | bytes 524288 | tf_op jit(solution)/shard_map/all_to_all | solution.py:83
  62.1 0.9 convert_reduce_fusion.2
  63.0 0.2 convolution_bitcast_fusion.3
  63.2 0.2 convolution_bitcast_fusion.2
  63.4 6.0 %all-to-all-done.1 = f16[16,64,128]{2,1,0:T(8,128)(2,1)S(1)} async-done(((f16[16,64,128]{2,1,0:T(8,128)(2,1)}), f16[16,64,128]{2,1,0:T(8,128)(2,1)S(1)}, u32[]{:S(2)}, u32[]{:S(2)}) %all-to-all-start.1) | async-done | bytes 262176 | tf_op jit(solution)/shard_map/all_to_all | solution.py:83
  69.5 1.4 %collective-permute-start.5 = (f32[3,64,128]{2,1,0:T(8,128)S(1)}, f32[3,64,128]{2,1,0:T(8,128)S(1)}, u32[]{:S(2)}, u32[]{:S(2)}) collective-permute-start(f32[3,64,128]{2,1,0:T(8,128)S(1)} %pad_maximum_fusion.2), channel_id=1, source_target_pairs={{0,32},{32,0},{64,96},{96,64},{128,160},{160,128},{192,224},{224,1... | collective-permute-start | bytes 294920 | tf_op jit(solution)/shard_map/ppermute | solution.py:25
  70.8 2.2 %collective-permute-done.5 = f32[3,64,128]{2,1,0:T(8,128)S(1)} collective-permute-done((f32[3,64,128]{2,1,0:T(8,128)S(1)}, f32[3,64,128]{2,1,0:T(8,128)S(1)}, u32[]{:S(2)}, u32[]{:S(2)}) %collective-permute-start.5) | collective-permute-done | bytes 98336 | tf_op jit(solution)/shard_map/ppermute | solution.py:25
  73.0 3.1 %collective-permute-start.6 = (f32[3,64,128]{2,1,0:T(8,128)S(1)}, f32[3,64,128]{2,1,0:T(8,128)S(1)}, u32[]{:S(2)}, u32[]{:S(2)}) collective-permute-start(f32[3,64,128]{2,1,0:T(8,128)S(1)} %fusion.43), channel_id=1, source_target_pairs={{0,64},{32,96},{64,0},{96,32},{128,192},{160,224},{192,128},{224,1... | collective-permute-start | bytes 294920 | tf_op jit(solution)/shard_map/ppermute | solution.py:25
  76.1 2.6 %collective-permute-done.6 = f32[3,64,128]{2,1,0:T(8,128)S(1)} collective-permute-done((f32[3,64,128]{2,1,0:T(8,128)S(1)}, f32[3,64,128]{2,1,0:T(8,128)S(1)}, u32[]{:S(2)}, u32[]{:S(2)}) %collective-permute-start.6) | collective-permute-done | bytes 98336 | tf_op jit(solution)/shard_map/ppermute | solution.py:25
  78.7 5.9 %collective-permute-start.7 = (f32[3,64,128]{2,1,0:T(8,128)S(1)}, f32[3,64,128]{2,1,0:T(8,128)S(1)}, u32[]{:S(2)}, u32[]{:S(2)}) collective-permute-start(f32[3,64,128]{2,1,0:T(8,128)S(1)} %fusion.55), channel_id=1, source_target_pairs={{0,128},{32,160},{64,192},{96,224},{128,0},{160,32},{192,64},{224,... | collective-permute-start | bytes 294920 | tf_op jit(solution)/shard_map/ppermute | solution.py:25
  84.6 2.1 %collective-permute-done.7 = f32[3,64,128]{2,1,0:T(8,128)S(1)} collective-permute-done((f32[3,64,128]{2,1,0:T(8,128)S(1)}, f32[3,64,128]{2,1,0:T(8,128)S(1)}, u32[]{:S(2)}, u32[]{:S(2)}) %collective-permute-start.7) | collective-permute-done | bytes 98336 | tf_op jit(solution)/shard_map/ppermute | solution.py:25
  86.7 0.8 broadcast_in_dim.9
  87.5 4.1 %all-to-all-start.2 = ((bf16[16,64,128]{2,1,0:T(8,128)(2,1)}), bf16[16,64,128]{2,1,0:T(8,128)(2,1)S(1)}, u32[]{:S(2)}, u32[]{:S(2)}) async-start(bf16[16,64,128]{2,1,0:T(8,128)(2,1)} %broadcast_in_dim.9), calls=%async_computation.2 | async-start | bytes 524288 | tf_op jit(solution)/shard_map/all_to_all | solution.py:102
  91.6 1.4 %collective-permute-start.8 = (f32[2,64,128]{2,1,0:T(8,128)S(1)}, f32[2,64,128]{2,1,0:T(8,128)}, u32[]{:S(2)}, u32[]{:S(2)}) collective-permute-start(f32[2,64,128]{2,1,0:T(8,128)S(1)} %pad_maximum_fusion.3), channel_id=1, source_target_pairs={{0,16},{16,0},{1,17},{17,1},{2,18},{18,2},{3,19},{19,3},{4,20},{20... | collective-permute-start | bytes 196616 | tf_op jit(solution)/shard_map/ppermute | solution.py:25
  93.0 0.2 copy.13
  93.2 2.0 %collective-permute-done.8 = f32[2,64,128]{2,1,0:T(8,128)} collective-permute-done((f32[2,64,128]{2,1,0:T(8,128)S(1)}, f32[2,64,128]{2,1,0:T(8,128)}, u32[]{:S(2)}, u32[]{:S(2)}) %collective-permute-start.8) | collective-permute-done | bytes 65568 | tf_op jit(solution)/shard_map/ppermute | solution.py:25
  95.3 3.6 %all-to-all-done.2 = bf16[16,64,128]{2,1,0:T(8,128)(2,1)S(1)} async-done(((bf16[16,64,128]{2,1,0:T(8,128)(2,1)}), bf16[16,64,128]{2,1,0:T(8,128)(2,1)S(1)}, u32[]{:S(2)}, u32[]{:S(2)}) %all-to-all-start.2) | async-done | bytes 262176 | tf_op jit(solution)/shard_map/all_to_all | solution.py:102
  98.9 0.9 broadcast_select_fusion.1
  99.7 9.3 %collective-permute-start.10 = (f32[2,64,128]{2,1,0:T(8,128)S(1)}, f32[2,64,128]{2,1,0:T(8,128)S(1)}, u32[]{:S(2)}, u32[]{:S(2)}) collective-permute-start(f32[2,64,128]{2,1,0:T(8,128)S(1)} %get-tuple-element.29), channel_id=1, source_target_pairs={{0,1},{1,0},{2,3},{3,2},{4,5},{5,4},{6,7},{7,6},{8,9},{9,8},{10,11... | collective-permute-start | bytes 196616 | tf_op jit(solution)/shard_map/ppermute | solution.py:25
  109.1 0.1 collective-permute-start.9
  109.2 0.5 convolution_bitcast_fusion.1
  109.7 0.3 collective-permute-done.10
  110.0 0.7 slice_bitcast_fusion
  110.7 0.5 convolution_bitcast_fusion
  111.1 0.1 fusion.7
  111.3 1.0 copy.14
  (28 shorter events, 0.3 us)
Async XLA Ops:
  0.6 4.9 %copy-start = (bf16[512,1024]{1,0:T(8,128)(2,1)S(1)}, bf16[512,1024]{1,0:T(8,128)(2,1)}, u32[]{:S(2)}) copy-start(bf16[512,1024]{1,0:T(8,128)(2,1)} %param.7) | copy-start | bytes 3145732
  0.6 11.0 %collective-permute-start = (bf16[8192,256]{1,0:T(8,128)(2,1)}, bf16[8192,256]{1,0:T(8,128)(2,1)}, u32[]{:S(2)}, u32[]{:S(2)}) collective-permute-start(bf16[8192,256]{1,0:T(8,128)(2,1)} %bitcast.47), channel_id=1, source_target_pairs={{0,1},{1,0},{2,3},{3,2},{4,5},{5,4},{6,7},{7,6},{8,9},{9,8},{10,11... | collective-permute-start | bytes 12582920 | tf_op jit(solution)/shard_map/ppermute | solution.py:25
  5.6 1.8 %copy-start.3 = (f32[64,256]{1,0:T(8,128)S(1)}, f32[64,256]{1,0:T(8,128)}, u32[]{:S(2)}) copy-start(f32[64,256]{1,0:T(8,128)} %param.11) | copy-start | bytes 196612
  5.6 1.8 %copy-start.4 = (f32[64,256]{1,0:T(8,128)S(1)}, f32[64,256]{1,0:T(8,128)}, u32[]{:S(2)}) copy-start(f32[64,256]{1,0:T(8,128)} %param.10) | copy-start | bytes 196612
  7.3 4.0 %collective-permute-start.1 = (f32[512,128]{1,0:T(8,128)}, f32[512,128]{1,0:T(8,128)S(1)}, u32[]{:S(2)}, u32[]{:S(2)}) collective-permute-start(f32[512,128]{1,0:T(8,128)} %fusion.18), channel_id=1, source_target_pairs={{0,1},{1,0},{2,3},{3,2},{4,5},{5,4},{6,7},{7,6},{8,9},{9,8},{10,11... | collective-permute-start | bytes 786440 | tf_op jit(solution)/shard_map/ppermute | solution.py:25
  8.1 8.7 %collective-permute-start.2 = (f32[2,64,256]{2,1,0:T(8,128)}, f32[2,64,256]{2,1,0:T(8,128)S(1)}, u32[]{:S(2)}, u32[]{:S(2)}) collective-permute-start(f32[2,64,256]{2,1,0:T(8,128)} %pad_maximum_fusion.1), channel_id=1, source_target_pairs={{0,0},{2,2},{4,4},{6,6},{8,8},{10,10},{12,12},{14,14},{32,34},{34,... | collective-permute-start | bytes 393224 | tf_op jit(solution)/shard_map/ppermute | solution.py:53
  16.7 5.1 %copy-start.1 = (bf16[512,1024]{1,0:T(8,128)(2,1)S(1)}, bf16[512,1024]{1,0:T(8,128)(2,1)}, u32[]{:S(2)}) copy-start(bf16[512,1024]{1,0:T(8,128)(2,1)} %param.8) | copy-start | bytes 3145732
  16.7 37.8 %all-to-all-start = ((f16[8,1088,128]{2,1,0:T(8,128)(2,1)}), f16[8,1088,128]{2,1,0:T(8,128)(2,1)}, u32[]{:S(2)}, u32[]{:S(2)}) async-start(f16[8,1088,128]{2,1,0:T(8,128)(2,1)} %pad_maximum_fusion), calls=%async_computation | async-start | bytes 4456448 | tf_op jit(solution)/shard_map/all_to_all | solution.py:70
  21.8 35.3 %collective-permute-start.3 = (bf16[512,1024]{1,0:T(8,128)(2,1)S(1)}, bf16[512,1024]{1,0:T(8,128)(2,1)S(1)}, u32[]{:S(2)}, u32[]{:S(2)}) collective-permute-start(bf16[512,1024]{1,0:T(8,128)(2,1)S(1)} %copy-done.1), channel_id=1, source_target_pairs={{0,1},{1,0},{2,3},{3,2},{4,5},{5,4},{6,7},{7,6},{8,9},{9,8},{10,11... | collective-permute-start | bytes 3145736 | tf_op jit(solution)/shard_map/ppermute | solution.py:25
  22.5 2.4 %collective-permute-start.4 = (f32[2,64,128]{2,1,0:T(8,128)S(1)}, f32[2,64,128]{2,1,0:T(8,128)S(1)}, u32[]{:S(2)}, u32[]{:S(2)}) collective-permute-start(f32[2,64,128]{2,1,0:T(8,128)S(1)} %get-tuple-element.31), channel_id=1, source_target_pairs={{0,1},{1,0},{2,3},{3,2},{4,5},{5,4},{6,7},{7,6},{8,9},{9,8},{10,11... | collective-permute-start | bytes 196616 | tf_op jit(solution)/shard_map/ppermute | solution.py:25
  57.6 35.4 %copy-start.2 = (f32[512,256]{1,0:T(8,128)S(1)}, f32[512,256]{1,0:T(8,128)}, u32[]{:S(2)}) copy-start(f32[512,256]{1,0:T(8,128)} %param.9) | copy-start | bytes 1572868
  58.5 10.8 %all-to-all-start.1 = ((f16[16,64,128]{2,1,0:T(8,128)(2,1)}), f16[16,64,128]{2,1,0:T(8,128)(2,1)S(1)}, u32[]{:S(2)}, u32[]{:S(2)}) async-start(f16[16,64,128]{2,1,0:T(8,128)(2,1)} %bitcast.9), calls=%async_computation.1 | async-start | bytes 524288 | tf_op jit(solution)/shard_map/all_to_all | solution.py:83
  69.5 3.6 %collective-permute-start.5 = (f32[3,64,128]{2,1,0:T(8,128)S(1)}, f32[3,64,128]{2,1,0:T(8,128)S(1)}, u32[]{:S(2)}, u32[]{:S(2)}) collective-permute-start(f32[3,64,128]{2,1,0:T(8,128)S(1)} %pad_maximum_fusion.2), channel_id=1, source_target_pairs={{0,32},{32,0},{64,96},{96,64},{128,160},{160,128},{192,224},{224,1... | collective-permute-start | bytes 294920 | tf_op jit(solution)/shard_map/ppermute | solution.py:25
  73.0 5.7 %collective-permute-start.6 = (f32[3,64,128]{2,1,0:T(8,128)S(1)}, f32[3,64,128]{2,1,0:T(8,128)S(1)}, u32[]{:S(2)}, u32[]{:S(2)}) collective-permute-start(f32[3,64,128]{2,1,0:T(8,128)S(1)} %fusion.43), channel_id=1, source_target_pairs={{0,64},{32,96},{64,0},{96,32},{128,192},{160,224},{192,128},{224,1... | collective-permute-start | bytes 294920 | tf_op jit(solution)/shard_map/ppermute | solution.py:25
  78.7 8.0 %collective-permute-start.7 = (f32[3,64,128]{2,1,0:T(8,128)S(1)}, f32[3,64,128]{2,1,0:T(8,128)S(1)}, u32[]{:S(2)}, u32[]{:S(2)}) collective-permute-start(f32[3,64,128]{2,1,0:T(8,128)S(1)} %fusion.55), channel_id=1, source_target_pairs={{0,128},{32,160},{64,192},{96,224},{128,0},{160,32},{192,64},{224,... | collective-permute-start | bytes 294920 | tf_op jit(solution)/shard_map/ppermute | solution.py:25
  87.5 11.4 %all-to-all-start.2 = ((bf16[16,64,128]{2,1,0:T(8,128)(2,1)}), bf16[16,64,128]{2,1,0:T(8,128)(2,1)S(1)}, u32[]{:S(2)}, u32[]{:S(2)}) async-start(bf16[16,64,128]{2,1,0:T(8,128)(2,1)} %broadcast_in_dim.9), calls=%async_computation.2 | async-start | bytes 524288 | tf_op jit(solution)/shard_map/all_to_all | solution.py:102
  91.6 3.7 %collective-permute-start.8 = (f32[2,64,128]{2,1,0:T(8,128)S(1)}, f32[2,64,128]{2,1,0:T(8,128)}, u32[]{:S(2)}, u32[]{:S(2)}) collective-permute-start(f32[2,64,128]{2,1,0:T(8,128)S(1)} %pad_maximum_fusion.3), channel_id=1, source_target_pairs={{0,16},{16,0},{1,17},{17,1},{2,18},{18,2},{3,19},{19,3},{4,20},{20... | collective-permute-start | bytes 196616 | tf_op jit(solution)/shard_map/ppermute | solution.py:25
  99.7 10.2 %collective-permute-start.10 = (f32[2,64,128]{2,1,0:T(8,128)S(1)}, f32[2,64,128]{2,1,0:T(8,128)S(1)}, u32[]{:S(2)}, u32[]{:S(2)}) collective-permute-start(f32[2,64,128]{2,1,0:T(8,128)S(1)} %get-tuple-element.29), channel_id=1, source_target_pairs={{0,1},{1,0},{2,3},{3,2},{4,5},{5,4},{6,7},{7,6},{8,9},{9,8},{10,11... | collective-permute-start | bytes 196616 | tf_op jit(solution)/shard_map/ppermute | solution.py:25
  109.1 1.6 %collective-permute-start.9 = (bf16[1024,128]{1,0:T(8,128)(2,1)S(1)}, bf16[1024,128]{1,0:T(8,128)(2,1)S(1)}, u32[]{:S(2)}, u32[]{:S(2)}) collective-permute-start(bf16[1024,128]{1,0:T(8,128)(2,1)S(1)} %bitcast.48), channel_id=1, source_target_pairs={{0,1},{1,0},{2,3},{3,2},{4,5},{5,4},{6,7},{7,6},{8,9},{9,8},{10,11... | collective-permute-start | bytes 786440 | tf_op jit(solution)/shard_map/ppermute | solution.py:25

commit v5 on v4

--- a/solution.py
+++ b/solution.py
@@ -19,6 +19,10 @@
 SCALE = 4096.0
 MARGIN_SCALE = 8192.0
 PROJECTED_SCALE = 8.0
+SHARE_SCALE = 2.0**-4
+FIRST_SCALE = 2.0**-6
+SECOND_SCALE = 2.0**-15
+LOW_SCALE = 2.0**11
 
 
 def swap(value, axis, bit, size):
@@ -33,6 +37,19 @@
     high = lax.reduce_precision(value, 8, 7)
     rest = value - high
     return jnp.concatenate([high, rest], axis=1).astype(jnp.bfloat16)
+
+
+def packed_shares(projected, first, second):
+    high = (first * FIRST_SCALE).astype(jnp.float16)
+    high = lax.optimization_barrier(high)
+    low = (first * FIRST_SCALE - high.astype(jnp.float32)) * LOW_SCALE
+    rest = jnp.stack([low, projected * SHARE_SCALE, second * SECOND_SCALE])
+    return jnp.concatenate([high[None], rest.astype(jnp.float16)])
+
+
+def unpacked_shares(total):
+    first = (total[0] + total[1] * (1.0 / LOW_SCALE)) * (1.0 / FIRST_SCALE)
+    return total[2] * (1.0 / SHARE_SCALE), first, total[3] * (1.0 / SECOND_SCALE)
 
 
 def on_device(partials, p_old, p_new, weight, m_old, v_old):
@@ -87,10 +104,12 @@
     margin = jnp.sum(rows[:, 1024:].astype(f32), axis=0) * (1.0 / MARGIN_SCALE)
     first = jnp.dot(margin, moments[0], precision=lax.Precision.HIGHEST)
     second = jnp.dot(margin * margin, moments[1], precision=lax.Precision.HIGHEST)
-    shares = jnp.stack([projected, first, second])
+    shares = (projected, first, second)
     for bit in (1, 2, 4):
-        shares = shares + swap(shares, "z", bit, 8)
-    projected, first, second = shares[0], shares[1], shares[2]
+        packed = lax.optimization_barrier(packed_shares(*shares))
+        ours, theirs = packed.astype(f32), swap(packed, "z", bit, 8).astype(f32)
+        shares = unpacked_shares(ours + theirs)
+    projected, first, second = shares
 
     m_new = beta_mean * first + (1.0 - beta_mean) * projected
     v_new = beta_square * second + (1.0 - beta_square) * projected * projected

time: 113 us -> 111 us (0.982)
  starting transfers between devices: 39.7 us -> 38.4 us
    ppermute x10, waiting for transfers between devices: 13.2 us -> 11.6 us  [swap(): return lax.ppermute(value, axis, [(i, i ^ bit) for i in range(size)])]
  transfers between devices with their start and end apart: 14 -> 14, of which waited for: 10 -> 10; matrix products, arithmetic and copies ran while one was open for 13% -> 12% of each run, Pallas kernels for 0% -> 0%
where the time goes in v5:
time: 111 us
  waiting for transfers between devices  51.7 us (47%)
  starting transfers between devices  38.4 us (35%)
  other arithmetic  11.3 us (10%)
  local copies, waits for them, and re-layouts  5.11 us (5%)
  matrix products  2.98 us (3%)
    all_to_all x1, waiting for transfers between devices, on_device(): rows = lax.all_to_all(sent, PAIRS, 0, 0, tiled=True)  29.6 us
    ppermute x10, starting transfers between devices, swap(): return lax.ppermute(value, axis, [(i, i ^ bit) for i in range(size)])  24.6 us
    ppermute x10, waiting for transfers between devices, swap(): return lax.ppermute(value, axis, [(i, i ^ bit) for i in range(size)])  11.6 us
    all_to_all x1, waiting for transfers between devices, on_device(): lax.all_to_all(projected.reshape(16, 64, 128), PLANE, 0, 0, tiled=True)  6.88 us
    all_to_all x1, starting transfers between devices, on_device(): rows = lax.all_to_all(sent, PAIRS, 0, 0, tiled=True)  5.05 us
    all_to_all x1, starting transfers between devices, on_device(): mine = lax.all_to_all(spread, PLANE, 0, 0, tiled=True).reshape(1024, 128)  3.65 us
    all_to_all x1, waiting for transfers between devices, on_device(): mine = lax.all_to_all(spread, PLANE, 0, 0, tiled=True).reshape(1024, 128)  3.64 us
    all_to_all x1, starting transfers between devices, on_device(): lax.all_to_all(projected.reshape(16, 64, 128), PLANE, 0, 0, tiled=True)  3.53 us
  transfers between devices with their start and end apart: 14, of which 10 were waited for; matrix products, arithmetic and copies ran while one was open for 12% of the time, Pallas kernels for 0%

profile of v5, /device:TPU:1, one launch (start us, length us, event | category | flops | bytes accessed | tf_op | source)
XLA Modules:
  0.0 110.5 jit_solution(5562262098184304108)
XLA Ops:
  0.6 3.3 %collective-permute-start = (bf16[8192,256]{1,0:T(8,128)(2,1)}, bf16[8192,256]{1,0:T(8,128)(2,1)}, u32[]{:S(2)}, u32[]{:S(2)}) collective-permute-start(bf16[8192,256]{1,0:T(8,128)(2,1)} %bitcast.68), channel_id=1, source_target_pairs={{0,1},{1,0},{2,3},{3,2},{4,5},{5,4},{6,7},{7,6},{8,9},{9,8},{10,11... | collective-permute-start | bytes 12582920 | tf_op jit(solution)/shard_map/ppermute | solution.py:29
  4.0 1.5 %copy.11 = bf16[512,1024]{0,1:T(8,128)(2,1)S(1)} copy(bf16[512,1024]{1,0:T(8,128)(2,1)} %param.8) | data formatting | bytes 2097152 | tf_op args[2]
  5.6 0.7 fusion.60
  6.3 1.0 fusion.20
  7.3 0.1 collective-permute-start.1
  7.4 0.7 pad_maximum_fusion.1
  8.1 1.6 %collective-permute-start.2 = (f32[2,64,256]{2,1,0:T(8,128)}, f32[2,64,256]{2,1,0:T(8,128)S(1)}, u32[]{:S(2)}, u32[]{:S(2)}) collective-permute-start(f32[2,64,256]{2,1,0:T(8,128)} %pad_maximum_fusion.1), channel_id=1, source_target_pairs={{0,0},{2,2},{4,4},{6,6},{8,8},{10,10},{12,12},{14,14},{32,34},{34,... | collective-permute-start | bytes 393224 | tf_op jit(solution)/shard_map/ppermute | solution.py:70
  9.6 1.7 %collective-permute-done.1 = f32[512,128]{1,0:T(8,128)S(1)} collective-permute-done((f32[512,128]{1,0:T(8,128)}, f32[512,128]{1,0:T(8,128)S(1)}, u32[]{:S(2)}, u32[]{:S(2)}) %collective-permute-start.1) | collective-permute-done | bytes 262176 | tf_op jit(solution)/shard_map/ppermute | solution.py:29
  11.3 0.3 multiply_convert_fusion
  11.6 3.0 %fusion.1 = f16[8192,128]{1,0:T(8,128)(2,1)S(1)} fusion(bf16[8192,256]{1,0:T(8,128)(2,1)} %collective-permute-done, s32[]{:T(128)S(6)} %select_n.82, bf16[1,8192,256]{2,1,0:T(8,128)(2,1)} %param.6), kind=kLoop, calls=%fused_computation.2 | loop fusion | flops 5242880 | bytes 6291460 | tf_op jit(solution)/shard_map/convert_element_type | solution.py:84
  14.7 2.0 %pad_maximum_fusion = f16[8,1088,128]{2,1,0:T(8,128)(2,1)} fusion(f16[8,64,128]{2,1,0:T(8,128)(2,1)S(1)} %bitcast.71, f16[8,1024,128]{2,1,0:T(8,128)(2,1)S(1)} %bitcast.65), kind=kLoop, calls=%fused_computation.4 | loop fusion | flops 1114112 | bytes 4456448 | tf_op jit(solution)/shard_map/concatenate | solution.py:85
  16.7 5.0 %all-to-all-start = ((f16[8,1088,128]{2,1,0:T(8,128)(2,1)}), f16[8,1088,128]{2,1,0:T(8,128)(2,1)}, u32[]{:S(2)}, u32[]{:S(2)}) async-start(f16[8,1088,128]{2,1,0:T(8,128)(2,1)} %pad_maximum_fusion), calls=%async_computation | async-start | bytes 4456448 | tf_op jit(solution)/shard_map/all_to_all | solution.py:87
  21.8 0.7 collective-permute-start.3
  22.5 0.1 collective-permute-start.4
  22.7 2.3 %collective-permute-done.4 = f32[2,64,128]{2,1,0:T(8,128)S(1)} collective-permute-done((f32[2,64,128]{2,1,0:T(8,128)S(1)}, f32[2,64,128]{2,1,0:T(8,128)S(1)}, u32[]{:S(2)}, u32[]{:S(2)}) %collective-permute-start.4) | collective-permute-done | bytes 65568 | tf_op jit(solution)/shard_map/ppermute | solution.py:29
  24.9 29.6 %all-to-all-done = f16[8,1088,128]{2,1,0:T(8,128)(2,1)} async-done(((f16[8,1088,128]{2,1,0:T(8,128)(2,1)}), f16[8,1088,128]{2,1,0:T(8,128)(2,1)}, u32[]{:S(2)}, u32[]{:S(2)}) %all-to-all-start) | async-done | bytes 2228256 | tf_op jit(solution)/shard_map/all_to_all | solution.py:87
  54.6 1.9 %convert_reduce_fusion = f32[1024,128]{1,0:T(8,128)S(1)} fusion(f16[8,1088,128]{2,1,0:T(8,128)(2,1)} %all-to-all-done), kind=kLoop, calls=%fused_computation.3 | loop fusion | flops 1966080 | bytes 2621440 | tf_op jit(solution)/shard_map/reduce_sum | solution.py:89
  56.5 0.1 fusion.5
  56.6 0.5 fusion.13
  57.1 0.5 fusion.2
  57.5 0.1 fusion.7
  57.6 0.9 convert_reduce_fusion.2
  58.6 0.9 copy.12
  59.5 3.5 %all-to-all-start.1 = ((f16[16,64,128]{2,1,0:T(8,128)(2,1)}), f16[16,64,128]{2,1,0:T(8,128)(2,1)S(1)}, u32[]{:S(2)}, u32[]{:S(2)}) async-start(f16[16,64,128]{2,1,0:T(8,128)(2,1)} %bitcast.12), calls=%async_computation.1 | async-start | bytes 524288 | tf_op jit(solution)/shard_map/all_to_all | solution.py:100
  63.0 0.2 fusion.59
  63.2 0.2 fusion.4
  63.4 6.9 %all-to-all-done.1 = f16[16,64,128]{2,1,0:T(8,128)(2,1)S(1)} async-done(((f16[16,64,128]{2,1,0:T(8,128)(2,1)}), f16[16,64,128]{2,1,0:T(8,128)(2,1)S(1)}, u32[]{:S(2)}, u32[]{:S(2)}) %all-to-all-start.1) | async-done | bytes 262176 | tf_op jit(solution)/shard_map/all_to_all | solution.py:100
  70.4 1.4 %collective-permute-start.5 = (f16[4,64,128]{2,1,0:T(8,128)(2,1)S(1)}, f16[4,64,128]{2,1,0:T(8,128)(2,1)S(1)}, u32[]{:S(2)}, u32[]{:S(2)}) collective-permute-start(f16[4,64,128]{2,1,0:T(8,128)(2,1)S(1)} %pad_maximum_fusion.2), channel_id=1, source_target_pairs={{0,32},{32,0},{64,96},{96,64},{128,160},{160,128},{192,224},{224,1... | collective-permute-start | bytes 196616 | tf_op jit(solution)/shard_map/ppermute | solution.py:29
  71.8 1.8 %collective-permute-done.5 = f16[4,64,128]{2,1,0:T(8,128)(2,1)S(1)} collective-permute-done((f16[4,64,128]{2,1,0:T(8,128)(2,1)S(1)}, f16[4,64,128]{2,1,0:T(8,128)(2,1)S(1)}, u32[]{:S(2)}, u32[]{:S(2)}) %collective-permute-start.5) | collective-permute-done | bytes 65568 | tf_op jit(solution)/shard_map/ppermute | solution.py:29
  73.7 3.1 %collective-permute-start.6 = (f16[4,64,128]{2,1,0:T(8,128)(2,1)S(1)}, f16[4,64,128]{2,1,0:T(8,128)(2,1)S(1)}, u32[]{:S(2)}, u32[]{:S(2)}) collective-permute-start(f16[4,64,128]{2,1,0:T(8,128)(2,1)S(1)} %pad_maximum_fusion.3), channel_id=1, source_target_pairs={{0,64},{32,96},{64,0},{96,32},{128,192},{160,224},{192,128},{224,1... | collective-permute-start | bytes 196616 | tf_op jit(solution)/shard_map/ppermute | solution.py:29
  76.8 1.7 %collective-permute-done.6 = f16[4,64,128]{2,1,0:T(8,128)(2,1)S(1)} collective-permute-done((f16[4,64,128]{2,1,0:T(8,128)(2,1)S(1)}, f16[4,64,128]{2,1,0:T(8,128)(2,1)S(1)}, u32[]{:S(2)}, u32[]{:S(2)}) %collective-permute-start.6) | collective-permute-done | bytes 65568 | tf_op jit(solution)/shard_map/ppermute | solution.py:29
  78.6 6.4 %collective-permute-start.7 = (f16[4,64,128]{2,1,0:T(8,128)(2,1)S(1)}, f16[4,64,128]{2,1,0:T(8,128)(2,1)S(1)}, u32[]{:S(2)}, u32[]{:S(2)}) collective-permute-start(f16[4,64,128]{2,1,0:T(8,128)(2,1)S(1)} %pad_maximum_fusion.4), channel_id=1, source_target_pairs={{0,128},{32,160},{64,192},{96,224},{128,0},{160,32},{192,64},{224,... | collective-permute-start | bytes 196616 | tf_op jit(solution)/shard_map/ppermute | solution.py:29
  85.0 1.8 %collective-permute-done.7 = f16[4,64,128]{2,1,0:T(8,128)(2,1)S(1)} collective-permute-done((f16[4,64,128]{2,1,0:T(8,128)(2,1)S(1)}, f16[4,64,128]{2,1,0:T(8,128)(2,1)S(1)}, u32[]{:S(2)}, u32[]{:S(2)}) %collective-permute-start.7) | collective-permute-done | bytes 65568 | tf_op jit(solution)/shard_map/ppermute | solution.py:29
  86.8 0.8 broadcast_in_dim.21
  87.6 3.7 %all-to-all-start.2 = ((bf16[16,64,128]{2,1,0:T(8,128)(2,1)}), bf16[16,64,128]{2,1,0:T(8,128)(2,1)S(1)}, u32[]{:S(2)}, u32[]{:S(2)}) async-start(bf16[16,64,128]{2,1,0:T(8,128)(2,1)} %broadcast_in_dim.21), calls=%async_computation.2 | async-start | bytes 524288 | tf_op jit(solution)/shard_map/all_to_all | solution.py:121
  91.3 1.4 %collective-permute-start.8 = (f32[2,64,128]{2,1,0:T(8,128)S(1)}, f32[2,64,128]{2,1,0:T(8,128)}, u32[]{:S(2)}, u32[]{:S(2)}) collective-permute-start(f32[2,64,128]{2,1,0:T(8,128)S(1)} %pad_maximum_fusion.5), channel_id=1, source_target_pairs={{0,16},{16,0},{1,17},{17,1},{2,18},{18,2},{3,19},{19,3},{4,20},{20... | collective-permute-start | bytes 196616 | tf_op jit(solution)/shard_map/ppermute | solution.py:29
  92.7 0.2 copy.13
  92.9 2.0 %collective-permute-done.8 = f32[2,64,128]{2,1,0:T(8,128)} collective-permute-done((f32[2,64,128]{2,1,0:T(8,128)S(1)}, f32[2,64,128]{2,1,0:T(8,128)}, u32[]{:S(2)}, u32[]{:S(2)}) %collective-permute-start.8) | collective-permute-done | bytes 65568 | tf_op jit(solution)/shard_map/ppermute | solution.py:29
  94.9 3.6 %all-to-all-done.2 = bf16[16,64,128]{2,1,0:T(8,128)(2,1)S(1)} async-done(((bf16[16,64,128]{2,1,0:T(8,128)(2,1)}), bf16[16,64,128]{2,1,0:T(8,128)(2,1)S(1)}, u32[]{:S(2)}, u32[]{:S(2)}) %all-to-all-start.2) | async-done | bytes 262176 | tf_op jit(solution)/shard_map/all_to_all | solution.py:121
  98.6 0.9 broadcast_select_fusion.1
  99.4 7.9 %collective-permute-start.10 = (f32[2,64,128]{2,1,0:T(8,128)S(1)}, f32[2,64,128]{2,1,0:T(8,128)S(1)}, u32[]{:S(2)}, u32[]{:S(2)}) collective-permute-start(f32[2,64,128]{2,1,0:T(8,128)S(1)} %get-tuple-element.29), channel_id=1, source_target_pairs={{0,1},{1,0},{2,3},{3,2},{4,5},{5,4},{6,7},{7,6},{8,9},{9,8},{10,11... | collective-permute-start | bytes 196616 | tf_op jit(solution)/shard_map/ppermute | solution.py:29
  107.3 0.1 collective-permute-start.9
  107.4 0.5 convolution_bitcast_fusion.1
  107.9 0.3 collective-permute-done.10
  108.3 0.7 slice_bitcast_fusion
  108.9 0.5 convolution_bitcast_fusion
  109.4 0.1 fusion.9
  109.5 1.0 copy.14
  (37 shorter events, 0.4 us)
Async XLA Ops:
  0.6 4.9 %copy-start = (bf16[512,1024]{1,0:T(8,128)(2,1)S(1)}, bf16[512,1024]{1,0:T(8,128)(2,1)}, u32[]{:S(2)}) copy-start(bf16[512,1024]{1,0:T(8,128)(2,1)} %param.7) | copy-start | bytes 3145732
  0.6 11.0 %collective-permute-start = (bf16[8192,256]{1,0:T(8,128)(2,1)}, bf16[8192,256]{1,0:T(8,128)(2,1)}, u32[]{:S(2)}, u32[]{:S(2)}) collective-permute-start(bf16[8192,256]{1,0:T(8,128)(2,1)} %bitcast.68), channel_id=1, source_target_pairs={{0,1},{1,0},{2,3},{3,2},{4,5},{5,4},{6,7},{7,6},{8,9},{9,8},{10,11... | collective-permute-start | bytes 12582920 | tf_op jit(solution)/shard_map/ppermute | solution.py:29
  5.6 1.8 %copy-start.3 = (f32[64,256]{1,0:T(8,128)S(1)}, f32[64,256]{1,0:T(8,128)}, u32[]{:S(2)}) copy-start(f32[64,256]{1,0:T(8,128)} %param.11) | copy-start | bytes 196612
  5.6 1.8 %copy-start.4 = (f32[64,256]{1,0:T(8,128)S(1)}, f32[64,256]{1,0:T(8,128)}, u32[]{:S(2)}) copy-start(f32[64,256]{1,0:T(8,128)} %param.10) | copy-start | bytes 196612
  7.3 4.0 %collective-permute-start.1 = (f32[512,128]{1,0:T(8,128)}, f32[512,128]{1,0:T(8,128)S(1)}, u32[]{:S(2)}, u32[]{:S(2)}) collective-permute-start(f32[512,128]{1,0:T(8,128)} %fusion.20), channel_id=1, source_target_pairs={{0,1},{1,0},{2,3},{3,2},{4,5},{5,4},{6,7},{7,6},{8,9},{9,8},{10,11... | collective-permute-start | bytes 786440 | tf_op jit(solution)/shard_map/ppermute | solution.py:29
  8.1 8.7 %collective-permute-start.2 = (f32[2,64,256]{2,1,0:T(8,128)}, f32[2,64,256]{2,1,0:T(8,128)S(1)}, u32[]{:S(2)}, u32[]{:S(2)}) collective-permute-start(f32[2,64,256]{2,1,0:T(8,128)} %pad_maximum_fusion.1), channel_id=1, source_target_pairs={{0,0},{2,2},{4,4},{6,6},{8,8},{10,10},{12,12},{14,14},{32,34},{34,... | collective-permute-start | bytes 393224 | tf_op jit(solution)/shard_map/ppermute | solution.py:70
  16.7 5.1 %copy-start.1 = (bf16[512,1024]{1,0:T(8,128)(2,1)S(1)}, bf16[512,1024]{1,0:T(8,128)(2,1)}, u32[]{:S(2)}) copy-start(bf16[512,1024]{1,0:T(8,128)(2,1)} %param.8) | copy-start | bytes 3145732
  16.7 37.8 %all-to-all-start = ((f16[8,1088,128]{2,1,0:T(8,128)(2,1)}), f16[8,1088,128]{2,1,0:T(8,128)(2,1)}, u32[]{:S(2)}, u32[]{:S(2)}) async-start(f16[8,1088,128]{2,1,0:T(8,128)(2,1)} %pad_maximum_fusion), calls=%async_computation | async-start | bytes 4456448 | tf_op jit(solution)/shard_map/all_to_all | solution.py:87
  21.8 35.3 %collective-permute-start.3 = (bf16[512,1024]{1,0:T(8,128)(2,1)S(1)}, bf16[512,1024]{1,0:T(8,128)(2,1)S(1)}, u32[]{:S(2)}, u32[]{:S(2)}) collective-permute-start(bf16[512,1024]{1,0:T(8,128)(2,1)S(1)} %copy-done.1), channel_id=1, source_target_pairs={{0,1},{1,0},{2,3},{3,2},{4,5},{5,4},{6,7},{7,6},{8,9},{9,8},{10,11... | collective-permute-start | bytes 3145736 | tf_op jit(solution)/shard_map/ppermute | solution.py:29
  22.5 2.4 %collective-permute-start.4 = (f32[2,64,128]{2,1,0:T(8,128)S(1)}, f32[2,64,128]{2,1,0:T(8,128)S(1)}, u32[]{:S(2)}, u32[]{:S(2)}) collective-permute-start(f32[2,64,128]{2,1,0:T(8,128)S(1)} %get-tuple-element.31), channel_id=1, source_target_pairs={{0,1},{1,0},{2,3},{3,2},{4,5},{5,4},{6,7},{7,6},{8,9},{9,8},{10,11... | collective-permute-start | bytes 196616 | tf_op jit(solution)/shard_map/ppermute | solution.py:29
  58.6 34.1 %copy-start.2 = (f32[512,256]{1,0:T(8,128)S(1)}, f32[512,256]{1,0:T(8,128)}, u32[]{:S(2)}) copy-start(f32[512,256]{1,0:T(8,128)} %param.9) | copy-start | bytes 1572868
  59.5 10.8 %all-to-all-start.1 = ((f16[16,64,128]{2,1,0:T(8,128)(2,1)}), f16[16,64,128]{2,1,0:T(8,128)(2,1)S(1)}, u32[]{:S(2)}, u32[]{:S(2)}) async-start(f16[16,64,128]{2,1,0:T(8,128)(2,1)} %bitcast.12), calls=%async_computation.1 | async-start | bytes 524288 | tf_op jit(solution)/shard_map/all_to_all | solution.py:100
  70.4 3.2 %collective-permute-start.5 = (f16[4,64,128]{2,1,0:T(8,128)(2,1)S(1)}, f16[4,64,128]{2,1,0:T(8,128)(2,1)S(1)}, u32[]{:S(2)}, u32[]{:S(2)}) collective-permute-start(f16[4,64,128]{2,1,0:T(8,128)(2,1)S(1)} %pad_maximum_fusion.2), channel_id=1, source_target_pairs={{0,32},{32,0},{64,96},{96,64},{128,160},{160,128},{192,224},{224,1... | collective-permute-start | bytes 196616 | tf_op jit(solution)/shard_map/ppermute | solution.py:29
  73.7 4.7 %collective-permute-start.6 = (f16[4,64,128]{2,1,0:T(8,128)(2,1)S(1)}, f16[4,64,128]{2,1,0:T(8,128)(2,1)S(1)}, u32[]{:S(2)}, u32[]{:S(2)}) collective-permute-start(f16[4,64,128]{2,1,0:T(8,128)(2,1)S(1)} %pad_maximum_fusion.3), channel_id=1, source_target_pairs={{0,64},{32,96},{64,0},{96,32},{128,192},{160,224},{192,128},{224,1... | collective-permute-start | bytes 196616 | tf_op jit(solution)/shard_map/ppermute | solution.py:29
  78.6 8.2 %collective-permute-start.7 = (f16[4,64,128]{2,1,0:T(8,128)(2,1)S(1)}, f16[4,64,128]{2,1,0:T(8,128)(2,1)S(1)}, u32[]{:S(2)}, u32[]{:S(2)}) collective-permute-start(f16[4,64,128]{2,1,0:T(8,128)(2,1)S(1)} %pad_maximum_fusion.4), channel_id=1, source_target_pairs={{0,128},{32,160},{64,192},{96,224},{128,0},{160,32},{192,64},{224,... | collective-permute-start | bytes 196616 | tf_op jit(solution)/shard_map/ppermute | solution.py:29
  87.6 11.0 %all-to-all-start.2 = ((bf16[16,64,128]{2,1,0:T(8,128)(2,1)}), bf16[16,64,128]{2,1,0:T(8,128)(2,1)S(1)}, u32[]{:S(2)}, u32[]{:S(2)}) async-start(bf16[16,64,128]{2,1,0:T(8,128)(2,1)} %broadcast_in_dim.21), calls=%async_computation.2 | async-start | bytes 524288 | tf_op jit(solution)/shard_map/all_to_all | solution.py:121
  91.3 3.7 %collective-permute-start.8 = (f32[2,64,128]{2,1,0:T(8,128)S(1)}, f32[2,64,128]{2,1,0:T(8,128)}, u32[]{:S(2)}, u32[]{:S(2)}) collective-permute-start(f32[2,64,128]{2,1,0:T(8,128)S(1)} %pad_maximum_fusion.5), channel_id=1, source_target_pairs={{0,16},{16,0},{1,17},{17,1},{2,18},{18,2},{3,19},{19,3},{4,20},{20... | collective-permute-start | bytes 196616 | tf_op jit(solution)/shard_map/ppermute | solution.py:29
  99.4 8.8 %collective-permute-start.10 = (f32[2,64,128]{2,1,0:T(8,128)S(1)}, f32[2,64,128]{2,1,0:T(8,128)S(1)}, u32[]{:S(2)}, u32[]{:S(2)}) collective-permute-start(f32[2,64,128]{2,1,0:T(8,128)S(1)} %get-tuple-element.29), channel_id=1, source_target_pairs={{0,1},{1,0},{2,3},{3,2},{4,5},{5,4},{6,7},{7,6},{8,9},{9,8},{10,11... | collective-permute-start | bytes 196616 | tf_op jit(solution)/shard_map/ppermute | solution.py:29
  107.3 1.6 %collective-permute-start.9 = (bf16[1024,128]{1,0:T(8,128)(2,1)S(1)}, bf16[1024,128]{1,0:T(8,128)(2,1)S(1)}, u32[]{:S(2)}, u32[]{:S(2)}) collective-permute-start(bf16[1024,128]{1,0:T(8,128)(2,1)S(1)} %bitcast.69), channel_id=1, source_target_pairs={{0,1},{1,0},{2,3},{3,2},{4,5},{5,4},{6,7},{7,6},{8,9},{9,8},{10,11... | collective-permute-start | bytes 786440 | tf_op jit(solution)/shard_map/ppermute | solution.py:29

commit v6 on v5

--- a/solution.py
+++ b/solution.py
@@ -86,7 +86,8 @@
     sent, turned = lax.optimization_barrier((sent, turned))
     rows = lax.all_to_all(sent, PAIRS, 0, 0, tiled=True)
 
-    grad_rows = jnp.sum(rows[:, :1024].astype(f32), axis=0) * (1.0 / SCALE)
+    sums = lax.optimization_barrier(jnp.sum(rows.astype(f32), axis=0))
+    grad_rows = sums[:1024] * (1.0 / SCALE)
     split = pieces(grad_rows)
     across = (((0,), (0,)), ((), ()))
     terms = lax.dot_general(
@@ -96,12 +97,12 @@
     )
     projected = terms[:, :128] + terms[:, 128:]
     projected = (projected * PROJECTED_SCALE).astype(jnp.float16)
-    projected, rows = lax.optimization_barrier((projected, rows))
+    projected, sums = lax.optimization_barrier((projected, sums))
     projected = lax.all_to_all(projected.reshape(16, 64, 128), PLANE, 0, 0, tiled=True)
     projected = jnp.sum(projected.astype(f32), axis=0) * (1.0 / PROJECTED_SCALE)
     moments_in = swap(cut(turned, 1 - core, 128, 2), "core", 1, 2)
     moments = sides(cut(turned, core, 128, 2), moments_in, 1)
-    margin = jnp.sum(rows[:, 1024:].astype(f32), axis=0) * (1.0 / MARGIN_SCALE)
+    margin = sums[1024:] * (1.0 / MARGIN_SCALE)
     first = jnp.dot(margin, moments[0], precision=lax.Precision.HIGHEST)
     second = jnp.dot(margin * margin, moments[1], precision=lax.Precision.HIGHEST)
     shares = (projected, first, second)
@@ -123,11 +124,7 @@
     near = swap(made, "yl", 1, 2)
     near, mine = lax.optimization_barrier((near, mine))
     other = swap(mine, "core", 1, 2)
-    update = sides(
-        jnp.dot(p_new, mine, preferred_element_type=f32),
-        jnp.dot(p_new, other, preferred_element_type=f32),
-        1,
-    )
+    update = jnp.dot(p_new, sides(mine, other, 1), preferred_element_type=f32)
     new_weight = weight - step_scale * update
 
     kept = jnp.where(core == yl, made, near)

time: 111 us -> 111 us (level)
  other arithmetic: 11.3 us -> 8.76 us
  matrix products: 2.98 us -> 5.26 us
  waiting for transfers between devices: 51.7 us -> 50 us
  local copies, waits for them, and re-layouts: 5.11 us -> 6.78 us
    reduce_sum x2 -> x1, other arithmetic: 2.86 us -> 0.32 us  [on_device(): sums = lax.optimization_barrier(jnp.sum(rows.astype(f32), axis=0))]
    all_to_all x1, waiting for transfers between devices: 6.88 us -> 5.37 us  [on_device(): lax.all_to_all(projected.reshape(16, 64, 128), PLANE, 0, 0, tiled=True)]
    dot_general x1, matrix products: 0.47 us -> 1.71 us  [on_device(): lax.dot_general(p_other, cut(split, 1 - core, 512, 0), across, preferred_...]
    unnamed x13 -> x19, local copies, waits for them, and re-layouts: 2.72 us -> 3.52 us
  transfers between devices with their start and end apart: 14 -> 14, of which waited for: 10 -> 10; matrix products, arithmetic and copies ran while one was open for 12% -> 13% of each run, Pallas kernels for 0% -> 0%
where the time goes in v6:
time: 111 us; the launch traced here: 110 us
  waiting for transfers between devices  50 us (45%)
  starting transfers between devices  38.4 us (35%)
  other arithmetic  8.76 us (8%)
  local copies, waits for them, and re-layouts  6.78 us (6%)
  matrix products  5.26 us (5%)
    all_to_all x1, waiting for transfers between devices, on_device(): rows = lax.all_to_all(sent, PAIRS, 0, 0, tiled=True)  29.6 us
    ppermute x10, starting transfers between devices, swap(): return lax.ppermute(value, axis, [(i, i ^ bit) for i in range(size)])  24.5 us
    ppermute x10, waiting for transfers between devices, swap(): return lax.ppermute(value, axis, [(i, i ^ bit) for i in range(size)])  11.3 us
    all_to_all x1, waiting for transfers between devices, on_device(): lax.all_to_all(projected.reshape(16, 64, 128), PLANE, 0, 0, tiled=True)  5.37 us
    all_to_all x1, starting transfers between devices, on_device(): rows = lax.all_to_all(sent, PAIRS, 0, 0, tiled=True)  4.92 us
    all_to_all x1, waiting for transfers between devices, on_device(): mine = lax.all_to_all(spread, PLANE, 0, 0, tiled=True).reshape(1024, 128)  3.74 us
    all_to_all x1, starting transfers between devices, on_device(): mine = lax.all_to_all(spread, PLANE, 0, 0, tiled=True).reshape(1024, 128)  3.68 us
    all_to_all x1, starting transfers between devices, on_device(): lax.all_to_all(projected.reshape(16, 64, 128), PLANE, 0, 0, tiled=True)  3.66 us
  transfers between devices with their start and end apart: 14, of which 10 were waited for; matrix products, arithmetic and copies ran while one was open for 13% of the time, Pallas kernels for 0%

profile of v6, /device:TPU:1, one launch (start us, length us, event | category | flops | bytes accessed | tf_op | source)
XLA Modules:
  0.0 110.1 jit_solution(8328865789476462876)
XLA Ops:
  0.6 3.3 %collective-permute-start = (bf16[8192,256]{1,0:T(8,128)(2,1)}, bf16[8192,256]{1,0:T(8,128)(2,1)}, u32[]{:S(2)}, u32[]{:S(2)}) collective-permute-start(bf16[8192,256]{1,0:T(8,128)(2,1)} %bitcast.65), channel_id=1, source_target_pairs={{0,1},{1,0},{2,3},{3,2},{4,5},{5,4},{6,7},{7,6},{8,9},{9,8},{10,11... | collective-permute-start | bytes 12582920 | tf_op jit(solution)/shard_map/ppermute | solution.py:29
  4.0 1.5 %copy.11 = bf16[512,1024]{0,1:T(8,128)(2,1)S(1)} copy(bf16[512,1024]{1,0:T(8,128)(2,1)} %param.8) | data formatting | bytes 2097152 | tf_op args[2]
  5.5 0.1 constant_dynamic-slice_fusion.2
  5.6 0.7 fusion.65
  6.3 1.0 fusion.26
  7.3 0.1 collective-permute-start.1
  7.4 0.7 pad_maximum_fusion.1
  8.1 1.6 %collective-permute-start.2 = (f32[2,64,256]{2,1,0:T(8,128)}, f32[2,64,256]{2,1,0:T(8,128)S(1)}, u32[]{:S(2)}, u32[]{:S(2)}) collective-permute-start(f32[2,64,256]{2,1,0:T(8,128)} %pad_maximum_fusion.1), channel_id=1, source_target_pairs={{0,0},{2,2},{4,4},{6,6},{8,8},{10,10},{12,12},{14,14},{32,34},{34,... | collective-permute-start | bytes 393224 | tf_op jit(solution)/shard_map/ppermute | solution.py:70
  9.6 1.7 %collective-permute-done.1 = f32[512,128]{1,0:T(8,128)S(1)} collective-permute-done((f32[512,128]{1,0:T(8,128)}, f32[512,128]{1,0:T(8,128)S(1)}, u32[]{:S(2)}, u32[]{:S(2)}) %collective-permute-start.1) | collective-permute-done | bytes 262176 | tf_op jit(solution)/shard_map/ppermute | solution.py:29
  11.3 0.3 multiply_convert_fusion
  11.6 3.0 %fusion.1 = f16[8192,128]{1,0:T(8,128)(2,1)S(1)} fusion(bf16[8192,256]{1,0:T(8,128)(2,1)} %collective-permute-done, s32[]{:T(128)S(6)} %select_n.82, bf16[1,8192,256]{2,1,0:T(8,128)(2,1)} %param.6), kind=kLoop, calls=%fused_computation.3 | loop fusion | flops 5242880 | bytes 6291460 | tf_op jit(solution)/shard_map/convert_element_type | solution.py:84
  14.7 2.0 %pad_maximum_fusion = f16[8,1088,128]{2,1,0:T(8,128)(2,1)} fusion(f16[8,64,128]{2,1,0:T(8,128)(2,1)S(1)} %bitcast.66, f16[8,1024,128]{2,1,0:T(8,128)(2,1)S(1)} %bitcast.62), kind=kLoop, calls=%fused_computation.4 | loop fusion | flops 1114112 | bytes 4456448 | tf_op jit(solution)/shard_map/concatenate | solution.py:85
  16.7 4.9 %all-to-all-start = ((f16[8,1088,128]{2,1,0:T(8,128)(2,1)}), f16[8,1088,128]{2,1,0:T(8,128)(2,1)S(1)}, u32[]{:S(2)}, u32[]{:S(2)}) async-start(f16[8,1088,128]{2,1,0:T(8,128)(2,1)} %pad_maximum_fusion), calls=%async_computation | async-start | bytes 4456448 | tf_op jit(solution)/shard_map/all_to_all | solution.py:87
  21.7 0.7 collective-permute-start.3
  22.3 0.9 constant_dynamic-slice_fusion
  23.2 0.1 collective-permute-start.4
  23.3 1.4 %collective-permute-done.4 = f32[2,64,128]{2,1,0:T(8,128)S(1)} collective-permute-done((f32[2,64,128]{2,1,0:T(8,128)S(1)}, f32[2,64,128]{2,1,0:T(8,128)S(1)}, u32[]{:S(2)}, u32[]{:S(2)}) %collective-permute-start.4) | collective-permute-done | bytes 65568 | tf_op jit(solution)/shard_map/ppermute | solution.py:29
  24.7 29.6 %all-to-all-done = f16[8,1088,128]{2,1,0:T(8,128)(2,1)S(1)} async-done(((f16[8,1088,128]{2,1,0:T(8,128)(2,1)}), f16[8,1088,128]{2,1,0:T(8,128)(2,1)S(1)}, u32[]{:S(2)}, u32[]{:S(2)}) %all-to-all-start) | async-done | bytes 2228256 | tf_op jit(solution)/shard_map/all_to_all | solution.py:87
  54.3 0.3 convert_reduce_fusion
  54.7 0.1 fusion.7
  54.8 0.8 copy-done.1
  55.6 0.5 fusion.19
  56.0 1.7 %fusion.2 = f32[1024,256]{0,1:T(8,128)S(1)} fusion(f32[256,1024]{1,0:T(8,128)S(1)} %fusion.19, bf16[512,1024]{1,0:T(8,128)(2,1)} %collective-permute-done.3, s32[]{:T(128)S(6)} %select_n.93, bf16[1024,128]{1,0:T(8,128)(2,1)S(1)} %get-tuple-element.25, bf16[1024,128]{1,0:T(8,128)(2,1)S(1)} %get-tuple-element.24), kind=kOutput, calls=%fused_computation.6 | convolution fusion | flops 269221888 | bytes 3670020 | tf_op jit(solution)/shard_map/dot_general | solution.py:95
  57.8 0.1 fusion.9
  57.8 0.9 copy.12
  58.8 3.7 %all-to-all-start.1 = ((f16[16,64,128]{2,1,0:T(8,128)(2,1)}), f16[16,64,128]{2,1,0:T(8,128)(2,1)S(1)}, u32[]{:S(2)}, u32[]{:S(2)}) async-start(f16[16,64,128]{2,1,0:T(8,128)(2,1)} %bitcast.12), calls=%async_computation.1 | async-start | bytes 524288 | tf_op jit(solution)/shard_map/all_to_all | solution.py:101
  62.4 0.9 fusion.64
  63.4 0.9 fusion.6
  64.4 5.4 %all-to-all-done.1 = f16[16,64,128]{2,1,0:T(8,128)(2,1)S(1)} async-done(((f16[16,64,128]{2,1,0:T(8,128)(2,1)}), f16[16,64,128]{2,1,0:T(8,128)(2,1)S(1)}, u32[]{:S(2)}, u32[]{:S(2)}) %all-to-all-start.1) | async-done | bytes 262176 | tf_op jit(solution)/shard_map/all_to_all | solution.py:101
  69.8 1.2 %collective-permute-start.5 = (f16[4,64,128]{2,1,0:T(8,128)(2,1)S(1)}, f16[4,64,128]{2,1,0:T(8,128)(2,1)S(1)}, u32[]{:S(2)}, u32[]{:S(2)}) collective-permute-start(f16[4,64,128]{2,1,0:T(8,128)(2,1)S(1)} %pad_maximum_fusion.2), channel_id=1, source_target_pairs={{0,32},{32,0},{64,96},{96,64},{128,160},{160,128},{192,224},{224,1... | collective-permute-start | bytes 196616 | tf_op jit(solution)/shard_map/ppermute | solution.py:29
  71.0 2.0 %collective-permute-done.5 = f16[4,64,128]{2,1,0:T(8,128)(2,1)S(1)} collective-permute-done((f16[4,64,128]{2,1,0:T(8,128)(2,1)S(1)}, f16[4,64,128]{2,1,0:T(8,128)(2,1)S(1)}, u32[]{:S(2)}, u32[]{:S(2)}) %collective-permute-start.5) | collective-permute-done | bytes 65568 | tf_op jit(solution)/shard_map/ppermute | solution.py:29
  73.1 3.1 %collective-permute-start.6 = (f16[4,64,128]{2,1,0:T(8,128)(2,1)S(1)}, f16[4,64,128]{2,1,0:T(8,128)(2,1)S(1)}, u32[]{:S(2)}, u32[]{:S(2)}) collective-permute-start(f16[4,64,128]{2,1,0:T(8,128)(2,1)S(1)} %pad_maximum_fusion.3), channel_id=1, source_target_pairs={{0,64},{32,96},{64,0},{96,32},{128,192},{160,224},{192,128},{224,1... | collective-permute-start | bytes 196616 | tf_op jit(solution)/shard_map/ppermute | solution.py:29
  76.2 1.7 %collective-permute-done.6 = f16[4,64,128]{2,1,0:T(8,128)(2,1)S(1)} collective-permute-done((f16[4,64,128]{2,1,0:T(8,128)(2,1)S(1)}, f16[4,64,128]{2,1,0:T(8,128)(2,1)S(1)}, u32[]{:S(2)}, u32[]{:S(2)}) %collective-permute-start.6) | collective-permute-done | bytes 65568 | tf_op jit(solution)/shard_map/ppermute | solution.py:29
  78.0 6.6 %collective-permute-start.7 = (f16[4,64,128]{2,1,0:T(8,128)(2,1)S(1)}, f16[4,64,128]{2,1,0:T(8,128)(2,1)S(1)}, u32[]{:S(2)}, u32[]{:S(2)}) collective-permute-start(f16[4,64,128]{2,1,0:T(8,128)(2,1)S(1)} %pad_maximum_fusion.4), channel_id=1, source_target_pairs={{0,128},{32,160},{64,192},{96,224},{128,0},{160,32},{192,64},{224,... | collective-permute-start | bytes 196616 | tf_op jit(solution)/shard_map/ppermute | solution.py:29
  84.5 1.7 %collective-permute-done.7 = f16[4,64,128]{2,1,0:T(8,128)(2,1)S(1)} collective-permute-done((f16[4,64,128]{2,1,0:T(8,128)(2,1)S(1)}, f16[4,64,128]{2,1,0:T(8,128)(2,1)S(1)}, u32[]{:S(2)}, u32[]{:S(2)}) %collective-permute-start.7) | collective-permute-done | bytes 65568 | tf_op jit(solution)/shard_map/ppermute | solution.py:29
  86.3 0.8 broadcast_in_dim.21
  87.0 3.7 %all-to-all-start.2 = ((bf16[16,64,128]{2,1,0:T(8,128)(2,1)}), bf16[16,64,128]{2,1,0:T(8,128)(2,1)S(1)}, u32[]{:S(2)}, u32[]{:S(2)}) async-start(bf16[16,64,128]{2,1,0:T(8,128)(2,1)} %broadcast_in_dim.21), calls=%async_computation.2 | async-start | bytes 524288 | tf_op jit(solution)/shard_map/all_to_all | solution.py:122
  90.7 1.4 %collective-permute-start.8 = (f32[2,64,128]{2,1,0:T(8,128)S(1)}, f32[2,64,128]{2,1,0:T(8,128)S(1)}, u32[]{:S(2)}, u32[]{:S(2)}) collective-permute-start(f32[2,64,128]{2,1,0:T(8,128)S(1)} %pad_maximum_fusion.5), channel_id=1, source_target_pairs={{0,16},{16,0},{1,17},{17,1},{2,18},{18,2},{3,19},{19,3},{4,20},{20... | collective-permute-start | bytes 196616 | tf_op jit(solution)/shard_map/ppermute | solution.py:29
  92.2 2.1 %collective-permute-done.8 = f32[2,64,128]{2,1,0:T(8,128)S(1)} collective-permute-done((f32[2,64,128]{2,1,0:T(8,128)S(1)}, f32[2,64,128]{2,1,0:T(8,128)S(1)}, u32[]{:S(2)}, u32[]{:S(2)}) %collective-permute-start.8) | collective-permute-done | bytes 65568 | tf_op jit(solution)/shard_map/ppermute | solution.py:29
  94.3 3.7 %all-to-all-done.2 = bf16[16,64,128]{2,1,0:T(8,128)(2,1)S(1)} async-done(((bf16[16,64,128]{2,1,0:T(8,128)(2,1)}), bf16[16,64,128]{2,1,0:T(8,128)(2,1)S(1)}, u32[]{:S(2)}, u32[]{:S(2)}) %all-to-all-start.2) | async-done | bytes 262176 | tf_op jit(solution)/shard_map/all_to_all | solution.py:122
  98.1 8.0 %collective-permute-start.10 = (f32[2,64,128]{2,1,0:T(8,128)S(1)}, f32[2,64,128]{2,1,0:T(8,128)}, u32[]{:S(2)}, u32[]{:S(2)}) collective-permute-start(f32[2,64,128]{2,1,0:T(8,128)S(1)} %get-tuple-element.29), channel_id=1, source_target_pairs={{0,1},{1,0},{2,3},{3,2},{4,5},{5,4},{6,7},{7,6},{8,9},{9,8},{10,11... | collective-permute-start | bytes 196616 | tf_op jit(solution)/shard_map/ppermute | solution.py:29
  106.0 0.2 copy.13
  106.2 0.1 collective-permute-start.9
  106.3 0.7 collective-permute-done.10
  107.1 0.9 maximum_select_fusion.3
  108.0 0.7 slice_bitcast_fusion
  108.7 0.5 fusion.4
  109.1 1.0 copy.14
  (40 shorter events, 0.4 us)
Async XLA Ops:
  0.6 4.9 %copy-start = (bf16[512,1024]{1,0:T(8,128)(2,1)S(1)}, bf16[512,1024]{1,0:T(8,128)(2,1)}, u32[]{:S(2)}) copy-start(bf16[512,1024]{1,0:T(8,128)(2,1)} %param.7) | copy-start | bytes 3145732
  0.6 11.0 %collective-permute-start = (bf16[8192,256]{1,0:T(8,128)(2,1)}, bf16[8192,256]{1,0:T(8,128)(2,1)}, u32[]{:S(2)}, u32[]{:S(2)}) collective-permute-start(bf16[8192,256]{1,0:T(8,128)(2,1)} %bitcast.65), channel_id=1, source_target_pairs={{0,1},{1,0},{2,3},{3,2},{4,5},{5,4},{6,7},{7,6},{8,9},{9,8},{10,11... | collective-permute-start | bytes 12582920 | tf_op jit(solution)/shard_map/ppermute | solution.py:29
  5.6 1.8 %copy-start.6 = (f32[64,256]{1,0:T(8,128)S(1)}, f32[64,256]{1,0:T(8,128)}, u32[]{:S(2)}) copy-start(f32[64,256]{1,0:T(8,128)} %param.11) | copy-start | bytes 196612
  5.6 1.8 %copy-start.7 = (f32[64,256]{1,0:T(8,128)S(1)}, f32[64,256]{1,0:T(8,128)}, u32[]{:S(2)}) copy-start(f32[64,256]{1,0:T(8,128)} %param.10) | copy-start | bytes 196612
  7.3 4.0 %collective-permute-start.1 = (f32[512,128]{1,0:T(8,128)}, f32[512,128]{1,0:T(8,128)S(1)}, u32[]{:S(2)}, u32[]{:S(2)}) collective-permute-start(f32[512,128]{1,0:T(8,128)} %fusion.26), channel_id=1, source_target_pairs={{0,1},{1,0},{2,3},{3,2},{4,5},{5,4},{6,7},{7,6},{8,9},{9,8},{10,11... | collective-permute-start | bytes 786440 | tf_op jit(solution)/shard_map/ppermute | solution.py:29
  8.1 8.7 %collective-permute-start.2 = (f32[2,64,256]{2,1,0:T(8,128)}, f32[2,64,256]{2,1,0:T(8,128)S(1)}, u32[]{:S(2)}, u32[]{:S(2)}) collective-permute-start(f32[2,64,256]{2,1,0:T(8,128)} %pad_maximum_fusion.1), channel_id=1, source_target_pairs={{0,0},{2,2},{4,4},{6,6},{8,8},{10,10},{12,12},{14,14},{32,34},{34,... | collective-permute-start | bytes 393224 | tf_op jit(solution)/shard_map/ppermute | solution.py:70
  16.7 5.6 %copy-start.5 = (f32[2,64,256]{2,1,0:T(8,128)}, f32[2,64,256]{2,1,0:T(8,128)S(1)}, u32[]{:S(2)}) copy-start(f32[2,64,256]{2,1,0:T(8,128)S(1)} %collective-permute-done.2) | copy-start | bytes 393220
  16.7 37.6 %all-to-all-start = ((f16[8,1088,128]{2,1,0:T(8,128)(2,1)}), f16[8,1088,128]{2,1,0:T(8,128)(2,1)S(1)}, u32[]{:S(2)}, u32[]{:S(2)}) async-start(f16[8,1088,128]{2,1,0:T(8,128)(2,1)} %pad_maximum_fusion), calls=%async_computation | async-start | bytes 4456448 | tf_op jit(solution)/shard_map/all_to_all | solution.py:87
  21.7 34.4 %collective-permute-start.3 = (bf16[512,1024]{1,0:T(8,128)(2,1)}, bf16[512,1024]{1,0:T(8,128)(2,1)}, u32[]{:S(2)}, u32[]{:S(2)}) collective-permute-start(bf16[512,1024]{1,0:T(8,128)(2,1)} %param.8), channel_id=1, source_target_pairs={{0,1},{1,0},{2,3},{3,2},{4,5},{5,4},{6,7},{7,6},{8,9},{9,8},{10,11... | collective-permute-start | bytes 3145736 | tf_op jit(solution)/shard_map/ppermute | solution.py:29
  23.2 1.5 %collective-permute-start.4 = (f32[2,64,128]{2,1,0:T(8,128)S(1)}, f32[2,64,128]{2,1,0:T(8,128)S(1)}, u32[]{:S(2)}, u32[]{:S(2)}) collective-permute-start(f32[2,64,128]{2,1,0:T(8,128)S(1)} %get-tuple-element.31), channel_id=1, source_target_pairs={{0,1},{1,0},{2,3},{3,2},{4,5},{5,4},{6,7},{7,6},{8,9},{9,8},{10,11... | collective-permute-start | bytes 196616 | tf_op jit(solution)/shard_map/ppermute | solution.py:29
  54.3 1.2 %copy-start.1 = (bf16[512,1024]{1,0:T(8,128)(2,1)S(1)}, bf16[512,1024]{1,0:T(8,128)(2,1)}, u32[]{:S(2)}) copy-start(bf16[512,1024]{1,0:T(8,128)(2,1)} %param.8) | copy-start | bytes 3145732
  54.7 3.1 %copy-start.3 = (f32[1088,128]{1,0:T(8,128)}, f32[1088,128]{1,0:T(8,128)S(1)}, u32[]{:S(2)}) copy-start(f32[1088,128]{1,0:T(8,128)S(1)} %convert_reduce_fusion) | copy-start | bytes 1671172
  58.8 47.3 %copy-start.4 = (f32[512,256]{1,0:T(8,128)S(1)}, f32[512,256]{1,0:T(8,128)}, u32[]{:S(2)}) copy-start(f32[512,256]{1,0:T(8,128)} %param.9) | copy-start | bytes 1572868
  58.8 11.0 %all-to-all-start.1 = ((f16[16,64,128]{2,1,0:T(8,128)(2,1)}), f16[16,64,128]{2,1,0:T(8,128)(2,1)S(1)}, u32[]{:S(2)}, u32[]{:S(2)}) async-start(f16[16,64,128]{2,1,0:T(8,128)(2,1)} %bitcast.12), calls=%async_computation.1 | async-start | bytes 524288 | tf_op jit(solution)/shard_map/all_to_all | solution.py:101
  69.8 3.2 %collective-permute-start.5 = (f16[4,64,128]{2,1,0:T(8,128)(2,1)S(1)}, f16[4,64,128]{2,1,0:T(8,128)(2,1)S(1)}, u32[]{:S(2)}, u32[]{:S(2)}) collective-permute-start(f16[4,64,128]{2,1,0:T(8,128)(2,1)S(1)} %pad_maximum_fusion.2), channel_id=1, source_target_pairs={{0,32},{32,0},{64,96},{96,64},{128,160},{160,128},{192,224},{224,1... | collective-permute-start | bytes 196616 | tf_op jit(solution)/shard_map/ppermute | solution.py:29
  73.0 35.6 %copy-start.2 = (bf16[512,1024]{1,0:T(8,128)(2,1)S(1)}, bf16[512,1024]{1,0:T(8,128)(2,1)}, u32[]{:S(2)}) copy-start(bf16[512,1024]{1,0:T(8,128)(2,1)} %param.8) | copy-start | bytes 3145732
  73.1 4.7 %collective-permute-start.6 = (f16[4,64,128]{2,1,0:T(8,128)(2,1)S(1)}, f16[4,64,128]{2,1,0:T(8,128)(2,1)S(1)}, u32[]{:S(2)}, u32[]{:S(2)}) collective-permute-start(f16[4,64,128]{2,1,0:T(8,128)(2,1)S(1)} %pad_maximum_fusion.3), channel_id=1, source_target_pairs={{0,64},{32,96},{64,0},{96,32},{128,192},{160,224},{192,128},{224,1... | collective-permute-start | bytes 196616 | tf_op jit(solution)/shard_map/ppermute | solution.py:29
  78.0 8.2 %collective-permute-start.7 = (f16[4,64,128]{2,1,0:T(8,128)(2,1)S(1)}, f16[4,64,128]{2,1,0:T(8,128)(2,1)S(1)}, u32[]{:S(2)}, u32[]{:S(2)}) collective-permute-start(f16[4,64,128]{2,1,0:T(8,128)(2,1)S(1)} %pad_maximum_fusion.4), channel_id=1, source_target_pairs={{0,128},{32,160},{64,192},{96,224},{128,0},{160,32},{192,64},{224,... | collective-permute-start | bytes 196616 | tf_op jit(solution)/shard_map/ppermute | solution.py:29
  87.0 11.0 %all-to-all-start.2 = ((bf16[16,64,128]{2,1,0:T(8,128)(2,1)}), bf16[16,64,128]{2,1,0:T(8,128)(2,1)S(1)}, u32[]{:S(2)}, u32[]{:S(2)}) async-start(bf16[16,64,128]{2,1,0:T(8,128)(2,1)} %broadcast_in_dim.21), calls=%async_computation.2 | async-start | bytes 524288 | tf_op jit(solution)/shard_map/all_to_all | solution.py:122
  90.7 3.6 %collective-permute-start.8 = (f32[2,64,128]{2,1,0:T(8,128)S(1)}, f32[2,64,128]{2,1,0:T(8,128)S(1)}, u32[]{:S(2)}, u32[]{:S(2)}) collective-permute-start(f32[2,64,128]{2,1,0:T(8,128)S(1)} %pad_maximum_fusion.5), channel_id=1, source_target_pairs={{0,16},{16,0},{1,17},{17,1},{2,18},{18,2},{3,19},{19,3},{4,20},{20... | collective-permute-start | bytes 196616 | tf_op jit(solution)/shard_map/ppermute | solution.py:29
  98.1 9.0 %collective-permute-start.10 = (f32[2,64,128]{2,1,0:T(8,128)S(1)}, f32[2,64,128]{2,1,0:T(8,128)}, u32[]{:S(2)}, u32[]{:S(2)}) collective-permute-start(f32[2,64,128]{2,1,0:T(8,128)S(1)} %get-tuple-element.29), channel_id=1, source_target_pairs={{0,1},{1,0},{2,3},{3,2},{4,5},{5,4},{6,7},{7,6},{8,9},{9,8},{10,11... | collective-permute-start | bytes 196616 | tf_op jit(solution)/shard_map/ppermute | solution.py:29
  106.2 2.4 %collective-permute-start.9 = (bf16[1024,128]{1,0:T(8,128)(2,1)S(1)}, bf16[1024,128]{1,0:T(8,128)(2,1)S(1)}, u32[]{:S(2)}, u32[]{:S(2)}) collective-permute-start(bf16[1024,128]{1,0:T(8,128)(2,1)S(1)} %bitcast.67), channel_id=1, source_target_pairs={{0,1},{1,0},{2,3},{3,2},{4,5},{5,4},{6,7},{7,6},{8,9},{9,8},{10,11... | collective-permute-start | bytes 786440 | tf_op jit(solution)/shard_map/ppermute | solution.py:29

commit v7 on v6

--- a/solution.py
+++ b/solution.py
@@ -1,6 +1,7 @@
 import jax
 import jax.numpy as jnp
 from jax import lax
+from jax.experimental.layout import Layout, with_layout_constraint
 from jax.sharding import Mesh, PartitionSpec as P
 
 beta_mean = 0.9
@@ -106,7 +107,7 @@
     first = jnp.dot(margin, moments[0], precision=lax.Precision.HIGHEST)
     second = jnp.dot(margin * margin, moments[1], precision=lax.Precision.HIGHEST)
     shares = (projected, first, second)
-    for bit in (1, 2, 4):
+    for bit in (2, 4, 1):
         packed = lax.optimization_barrier(packed_shares(*shares))
         ours, theirs = packed.astype(f32), swap(packed, "z", bit, 8).astype(f32)
         shares = unpacked_shares(ours + theirs)
@@ -125,6 +126,7 @@
     near, mine = lax.optimization_barrier((near, mine))
     other = swap(mine, "core", 1, 2)
     update = jnp.dot(p_new, sides(mine, other, 1), preferred_element_type=f32)
+    update = with_layout_constraint(update, Layout((0, 1)))
     new_weight = weight - step_scale * update
 
     kept = jnp.where(core == yl, made, near)

time: 111 us -> 109 us (0.982)
  local copies, waits for them, and re-layouts: 6.78 us -> 5.59 us
    unnamed x19 -> x17, local copies, waits for them, and re-layouts: 3.52 us -> 2.33 us
where the time goes in v7:
time: 109 us
  waiting for transfers between devices  50.2 us (46%)
  starting transfers between devices  37.9 us (35%)
  other arithmetic  7.85 us (7%)
  matrix products  6.14 us (6%)
  local copies, waits for them, and re-layouts  5.59 us (5%)
    all_to_all x1, waiting for transfers between devices, on_device(): rows = lax.all_to_all(sent, PAIRS, 0, 0, tiled=True)  29.6 us
    ppermute x10, starting transfers between devices, swap(): return lax.ppermute(value, axis, [(i, i ^ bit) for i in range(size)])  23.9 us
    ppermute x10, waiting for transfers between devices, swap(): return lax.ppermute(value, axis, [(i, i ^ bit) for i in range(size)])  11.6 us
    all_to_all x1, waiting for transfers between devices, on_device(): lax.all_to_all(projected.reshape(16, 64, 128), PLANE, 0, 0, tiled=True)  5.23 us
    all_to_all x1, starting transfers between devices, on_device(): rows = lax.all_to_all(sent, PAIRS, 0, 0, tiled=True)  4.92 us
    all_to_all x1, starting transfers between devices, on_device(): mine = lax.all_to_all(spread, PLANE, 0, 0, tiled=True).reshape(1024, 128)  3.98 us
    all_to_all x1, waiting for transfers between devices, on_device(): mine = lax.all_to_all(spread, PLANE, 0, 0, tiled=True).reshape(1024, 128)  3.74 us
    all_to_all x1, starting transfers between devices, on_device(): lax.all_to_all(projected.reshape(16, 64, 128), PLANE, 0, 0, tiled=True)  3.53 us
  transfers between devices with their start and end apart: 14, of which 10 were waited for; matrix products, arithmetic and copies ran while one was open for 13% of the time, Pallas kernels for 0%

profile of v7, /device:TPU:1, one launch (start us, length us, event | category | flops | bytes accessed | tf_op | source)
XLA Modules:
  0.0 108.6 jit_solution(824322156356400123)
XLA Ops:
  0.6 0.0 copy-start
  0.6 3.3 %collective-permute-start = (bf16[8192,256]{1,0:T(8,128)(2,1)}, bf16[8192,256]{1,0:T(8,128)(2,1)}, u32[]{:S(2)}, u32[]{:S(2)}) collective-permute-start(bf16[8192,256]{1,0:T(8,128)(2,1)} %bitcast.67), channel_id=1, source_target_pairs={{0,1},{1,0},{2,3},{3,2},{4,5},{5,4},{6,7},{7,6},{8,9},{9,8},{10,11... | collective-permute-start | bytes 12582920 | tf_op jit(solution)/shard_map/ppermute | solution.py:30
  4.0 1.5 %copy.9 = bf16[512,1024]{0,1:T(8,128)(2,1)S(1)} copy(bf16[512,1024]{1,0:T(8,128)(2,1)} %param.8) | data formatting | bytes 2097152 | tf_op args[2]
  5.5 0.1 constant_dynamic-slice_fusion.2
  5.6 0.0 copy-start.5
  5.6 0.7 fusion.65
  6.3 1.0 fusion.26
  7.3 0.1 collective-permute-start.1
  7.4 0.7 pad_maximum_fusion.1
  8.1 1.6 %collective-permute-start.2 = (f32[2,64,256]{2,1,0:T(8,128)}, f32[2,64,256]{2,1,0:T(8,128)S(1)}, u32[]{:S(2)}, u32[]{:S(2)}) collective-permute-start(f32[2,64,256]{2,1,0:T(8,128)} %pad_maximum_fusion.1), channel_id=1, source_target_pairs={{0,0},{2,2},{4,4},{6,6},{8,8},{10,10},{12,12},{14,14},{32,34},{34,... | collective-permute-start | bytes 393224 | tf_op jit(solution)/shard_map/ppermute | solution.py:71
  9.6 1.7 %collective-permute-done.1 = f32[512,128]{1,0:T(8,128)S(1)} collective-permute-done((f32[512,128]{1,0:T(8,128)}, f32[512,128]{1,0:T(8,128)S(1)}, u32[]{:S(2)}, u32[]{:S(2)}) %collective-permute-start.1) | collective-permute-done | bytes 262176 | tf_op jit(solution)/shard_map/ppermute | solution.py:30
  11.3 0.3 multiply_convert_fusion
  11.6 3.0 %fusion.1 = f16[8192,128]{1,0:T(8,128)(2,1)S(1)} fusion(bf16[8192,256]{1,0:T(8,128)(2,1)} %collective-permute-done, s32[]{:T(128)S(6)} %select_n.82, bf16[1,8192,256]{2,1,0:T(8,128)(2,1)} %param.6), kind=kLoop, calls=%fused_computation.3 | loop fusion | flops 5242880 | bytes 6291460 | tf_op jit(solution)/shard_map/convert_element_type | solution.py:85
  14.7 2.0 %pad_maximum_fusion = f16[8,1088,128]{2,1,0:T(8,128)(2,1)} fusion(f16[8,64,128]{2,1,0:T(8,128)(2,1)S(1)} %bitcast.68, f16[8,1024,128]{2,1,0:T(8,128)(2,1)S(1)} %bitcast.64), kind=kLoop, calls=%fused_computation.4 | loop fusion | flops 1114112 | bytes 4456448 | tf_op jit(solution)/shard_map/concatenate | solution.py:86
  16.7 4.9 %all-to-all-start = ((f16[8,1088,128]{2,1,0:T(8,128)(2,1)}), f16[8,1088,128]{2,1,0:T(8,128)(2,1)S(1)}, u32[]{:S(2)}, u32[]{:S(2)}) async-start(f16[8,1088,128]{2,1,0:T(8,128)(2,1)} %pad_maximum_fusion), calls=%async_computation | async-start | bytes 4456448 | tf_op jit(solution)/shard_map/all_to_all | solution.py:88
  21.7 0.7 collective-permute-start.3
  22.3 0.9 constant_dynamic-slice_fusion
  23.2 0.1 collective-permute-start.4
  23.3 1.4 %collective-permute-done.4 = f32[2,64,128]{2,1,0:T(8,128)S(1)} collective-permute-done((f32[2,64,128]{2,1,0:T(8,128)S(1)}, f32[2,64,128]{2,1,0:T(8,128)S(1)}, u32[]{:S(2)}, u32[]{:S(2)}) %collective-permute-start.4) | collective-permute-done | bytes 65568 | tf_op jit(solution)/shard_map/ppermute | solution.py:30
  24.7 29.6 %all-to-all-done = f16[8,1088,128]{2,1,0:T(8,128)(2,1)S(1)} async-done(((f16[8,1088,128]{2,1,0:T(8,128)(2,1)}), f16[8,1088,128]{2,1,0:T(8,128)(2,1)S(1)}, u32[]{:S(2)}, u32[]{:S(2)}) %all-to-all-start) | async-done | bytes 2228256 | tf_op jit(solution)/shard_map/all_to_all | solution.py:88
  54.3 0.3 convert_reduce_fusion
  54.7 0.1 fusion.7
  54.8 0.8 copy-done.1
  55.6 0.5 fusion.19
  56.0 1.7 %fusion.2 = f32[1024,256]{0,1:T(8,128)S(1)} fusion(f32[256,1024]{1,0:T(8,128)S(1)} %fusion.19, bf16[512,1024]{1,0:T(8,128)(2,1)} %collective-permute-done.3, s32[]{:T(128)S(6)} %select_n.93, bf16[1024,128]{1,0:T(8,128)(2,1)S(1)} %get-tuple-element.19, bf16[1024,128]{1,0:T(8,128)(2,1)S(1)} %get-tuple-element.18), kind=kOutput, calls=%fused_computation.6 | convolution fusion | flops 269221888 | bytes 3670020 | tf_op jit(solution)/shard_map/dot_general | solution.py:96
  57.8 0.1 fusion.9
  57.8 0.9 copy.10
  58.8 3.5 %all-to-all-start.1 = ((f16[16,64,128]{2,1,0:T(8,128)(2,1)}), f16[16,64,128]{2,1,0:T(8,128)(2,1)S(1)}, u32[]{:S(2)}, u32[]{:S(2)}) async-start(f16[16,64,128]{2,1,0:T(8,128)(2,1)} %bitcast.12), calls=%async_computation.1 | async-start | bytes 524288 | tf_op jit(solution)/shard_map/all_to_all | solution.py:102
  62.3 0.0 copy-start.7
  62.3 1.1 fusion.64
  63.4 0.9 fusion.6
  64.4 5.2 %all-to-all-done.1 = f16[16,64,128]{2,1,0:T(8,128)(2,1)S(1)} async-done(((f16[16,64,128]{2,1,0:T(8,128)(2,1)}), f16[16,64,128]{2,1,0:T(8,128)(2,1)S(1)}, u32[]{:S(2)}, u32[]{:S(2)}) %all-to-all-start.1) | async-done | bytes 262176 | tf_op jit(solution)/shard_map/all_to_all | solution.py:102
  69.7 3.1 %collective-permute-start.5 = (f16[4,64,128]{2,1,0:T(8,128)(2,1)S(1)}, f16[4,64,128]{2,1,0:T(8,128)(2,1)S(1)}, u32[]{:S(2)}, u32[]{:S(2)}) collective-permute-start(f16[4,64,128]{2,1,0:T(8,128)(2,1)S(1)} %pad_maximum_fusion.2), channel_id=1, source_target_pairs={{0,64},{32,96},{64,0},{96,32},{128,192},{160,224},{192,128},{224,1... | collective-permute-start | bytes 196616 | tf_op jit(solution)/shard_map/ppermute | solution.py:30
  72.8 1.7 %collective-permute-done.5 = f16[4,64,128]{2,1,0:T(8,128)(2,1)S(1)} collective-permute-done((f16[4,64,128]{2,1,0:T(8,128)(2,1)S(1)}, f16[4,64,128]{2,1,0:T(8,128)(2,1)S(1)}, u32[]{:S(2)}, u32[]{:S(2)}) %collective-permute-start.5) | collective-permute-done | bytes 65568 | tf_op jit(solution)/shard_map/ppermute | solution.py:30
  74.5 5.8 %collective-permute-start.6 = (f16[4,64,128]{2,1,0:T(8,128)(2,1)S(1)}, f16[4,64,128]{2,1,0:T(8,128)(2,1)S(1)}, u32[]{:S(2)}, u32[]{:S(2)}) collective-permute-start(f16[4,64,128]{2,1,0:T(8,128)(2,1)S(1)} %pad_maximum_fusion.3), channel_id=1, source_target_pairs={{0,128},{32,160},{64,192},{96,224},{128,0},{160,32},{192,64},{224,... | collective-permute-start | bytes 196616 | tf_op jit(solution)/shard_map/ppermute | solution.py:30
  80.4 1.8 %collective-permute-done.6 = f16[4,64,128]{2,1,0:T(8,128)(2,1)S(1)} collective-permute-done((f16[4,64,128]{2,1,0:T(8,128)(2,1)S(1)}, f16[4,64,128]{2,1,0:T(8,128)(2,1)S(1)}, u32[]{:S(2)}, u32[]{:S(2)}) %collective-permute-start.6) | collective-permute-done | bytes 65568 | tf_op jit(solution)/shard_map/ppermute | solution.py:30
  82.2 2.2 %collective-permute-start.7 = (f16[4,64,128]{2,1,0:T(8,128)(2,1)S(1)}, f16[4,64,128]{2,1,0:T(8,128)(2,1)S(1)}, u32[]{:S(2)}, u32[]{:S(2)}) collective-permute-start(f16[4,64,128]{2,1,0:T(8,128)(2,1)S(1)} %pad_maximum_fusion.4), channel_id=1, source_target_pairs={{0,32},{32,0},{64,96},{96,64},{128,160},{160,128},{192,224},{224,1... | collective-permute-start | bytes 196616 | tf_op jit(solution)/shard_map/ppermute | solution.py:30
  84.4 2.1 %collective-permute-done.7 = f16[4,64,128]{2,1,0:T(8,128)(2,1)S(1)} collective-permute-done((f16[4,64,128]{2,1,0:T(8,128)(2,1)S(1)}, f16[4,64,128]{2,1,0:T(8,128)(2,1)S(1)}, u32[]{:S(2)}, u32[]{:S(2)}) %collective-permute-start.7) | collective-permute-done | bytes 65568 | tf_op jit(solution)/shard_map/ppermute | solution.py:30
  86.6 0.8 broadcast_in_dim.21
  87.4 4.0 %all-to-all-start.2 = ((bf16[16,64,128]{2,1,0:T(8,128)(2,1)}), bf16[16,64,128]{2,1,0:T(8,128)(2,1)S(1)}, u32[]{:S(2)}, u32[]{:S(2)}) async-start(bf16[16,64,128]{2,1,0:T(8,128)(2,1)} %broadcast_in_dim.21), calls=%async_computation.2 | async-start | bytes 524288 | tf_op jit(solution)/shard_map/all_to_all | solution.py:123
  91.4 1.4 %collective-permute-start.8 = (f32[2,64,128]{2,1,0:T(8,128)S(1)}, f32[2,64,128]{2,1,0:T(8,128)S(1)}, u32[]{:S(2)}, u32[]{:S(2)}) collective-permute-start(f32[2,64,128]{2,1,0:T(8,128)S(1)} %pad_maximum_fusion.5), channel_id=1, source_target_pairs={{0,16},{16,0},{1,17},{17,1},{2,18},{18,2},{3,19},{19,3},{4,20},{20... | collective-permute-start | bytes 196616 | tf_op jit(solution)/shard_map/ppermute | solution.py:30
  92.8 2.1 %collective-permute-done.8 = f32[2,64,128]{2,1,0:T(8,128)S(1)} collective-permute-done((f32[2,64,128]{2,1,0:T(8,128)S(1)}, f32[2,64,128]{2,1,0:T(8,128)S(1)}, u32[]{:S(2)}, u32[]{:S(2)}) %collective-permute-start.8) | collective-permute-done | bytes 65568 | tf_op jit(solution)/shard_map/ppermute | solution.py:30
  94.9 3.7 %all-to-all-done.2 = bf16[16,64,128]{2,1,0:T(8,128)(2,1)S(1)} async-done(((bf16[16,64,128]{2,1,0:T(8,128)(2,1)}), bf16[16,64,128]{2,1,0:T(8,128)(2,1)S(1)}, u32[]{:S(2)}, u32[]{:S(2)}) %all-to-all-start.2) | async-done | bytes 262176 | tf_op jit(solution)/shard_map/all_to_all | solution.py:123
  98.7 7.1 %collective-permute-start.10 = (f32[2,64,128]{2,1,0:T(8,128)S(1)}, f32[2,64,128]{2,1,0:T(8,128)S(1)}, u32[]{:S(2)}, u32[]{:S(2)}) collective-permute-start(f32[2,64,128]{2,1,0:T(8,128)S(1)} %get-tuple-element.23), channel_id=1, source_target_pairs={{0,1},{1,0},{2,3},{3,2},{4,5},{5,4},{6,7},{7,6},{8,9},{9,8},{10,11... | collective-permute-start | bytes 196616 | tf_op jit(solution)/shard_map/ppermute | solution.py:30
  105.8 0.1 collective-permute-start.9
  105.9 0.8 collective-permute-done.10
  106.7 0.7 slice_bitcast_fusion
  107.4 1.3 %fusion.4 = f32[512,256]{1,0:T(8,128)} fusion(f32[512,256]{1,0:T(8,128)S(1)} %copy-done.7, bf16[512,1024]{1,0:T(8,128)(2,1)S(1)} %copy-done.2, bf16[1024,128]{1,0:T(8,128)(2,1)S(1)} %collective-permute-done.9, bf16[1024,128]{1,0:T(8,128)(2,1)S(1)} %bitcast.70, pred[]{:T(512)S(6)} %eq.49), kind=kOutput, calls=%fused_computation.9 | convolution fusion | flops 271056896 | bytes 2621441 | tf_op jit(solution)/shard_map/dot_general | solution.py:128
  (38 shorter events, 0.4 us)
Async XLA Ops:
  0.6 4.9 %copy-start = (bf16[512,1024]{1,0:T(8,128)(2,1)S(1)}, bf16[512,1024]{1,0:T(8,128)(2,1)}, u32[]{:S(2)}) copy-start(bf16[512,1024]{1,0:T(8,128)(2,1)} %param.7) | copy-start | bytes 3145732
  0.6 11.0 %collective-permute-start = (bf16[8192,256]{1,0:T(8,128)(2,1)}, bf16[8192,256]{1,0:T(8,128)(2,1)}, u32[]{:S(2)}, u32[]{:S(2)}) collective-permute-start(bf16[8192,256]{1,0:T(8,128)(2,1)} %bitcast.67), channel_id=1, source_target_pairs={{0,1},{1,0},{2,3},{3,2},{4,5},{5,4},{6,7},{7,6},{8,9},{9,8},{10,11... | collective-permute-start | bytes 12582920 | tf_op jit(solution)/shard_map/ppermute | solution.py:30
  5.6 1.8 %copy-start.5 = (f32[64,256]{1,0:T(8,128)S(1)}, f32[64,256]{1,0:T(8,128)}, u32[]{:S(2)}) copy-start(f32[64,256]{1,0:T(8,128)} %param.11) | copy-start | bytes 196612
  5.6 1.8 %copy-start.6 = (f32[64,256]{1,0:T(8,128)S(1)}, f32[64,256]{1,0:T(8,128)}, u32[]{:S(2)}) copy-start(f32[64,256]{1,0:T(8,128)} %param.10) | copy-start | bytes 196612
  7.3 4.0 %collective-permute-start.1 = (f32[512,128]{1,0:T(8,128)}, f32[512,128]{1,0:T(8,128)S(1)}, u32[]{:S(2)}, u32[]{:S(2)}) collective-permute-start(f32[512,128]{1,0:T(8,128)} %fusion.26), channel_id=1, source_target_pairs={{0,1},{1,0},{2,3},{3,2},{4,5},{5,4},{6,7},{7,6},{8,9},{9,8},{10,11... | collective-permute-start | bytes 786440 | tf_op jit(solution)/shard_map/ppermute | solution.py:30
  8.1 8.7 %collective-permute-start.2 = (f32[2,64,256]{2,1,0:T(8,128)}, f32[2,64,256]{2,1,0:T(8,128)S(1)}, u32[]{:S(2)}, u32[]{:S(2)}) collective-permute-start(f32[2,64,256]{2,1,0:T(8,128)} %pad_maximum_fusion.1), channel_id=1, source_target_pairs={{0,0},{2,2},{4,4},{6,6},{8,8},{10,10},{12,12},{14,14},{32,34},{34,... | collective-permute-start | bytes 393224 | tf_op jit(solution)/shard_map/ppermute | solution.py:71
  16.7 5.6 %copy-start.4 = (f32[2,64,256]{2,1,0:T(8,128)}, f32[2,64,256]{2,1,0:T(8,128)S(1)}, u32[]{:S(2)}) copy-start(f32[2,64,256]{2,1,0:T(8,128)S(1)} %collective-permute-done.2) | copy-start | bytes 393220
  16.7 37.6 %all-to-all-start = ((f16[8,1088,128]{2,1,0:T(8,128)(2,1)}), f16[8,1088,128]{2,1,0:T(8,128)(2,1)S(1)}, u32[]{:S(2)}, u32[]{:S(2)}) async-start(f16[8,1088,128]{2,1,0:T(8,128)(2,1)} %pad_maximum_fusion), calls=%async_computation | async-start | bytes 4456448 | tf_op jit(solution)/shard_map/all_to_all | solution.py:88
  21.7 34.4 %collective-permute-start.3 = (bf16[512,1024]{1,0:T(8,128)(2,1)}, bf16[512,1024]{1,0:T(8,128)(2,1)}, u32[]{:S(2)}, u32[]{:S(2)}) collective-permute-start(bf16[512,1024]{1,0:T(8,128)(2,1)} %param.8), channel_id=1, source_target_pairs={{0,1},{1,0},{2,3},{3,2},{4,5},{5,4},{6,7},{7,6},{8,9},{9,8},{10,11... | collective-permute-start | bytes 3145736 | tf_op jit(solution)/shard_map/ppermute | solution.py:30
  23.2 1.5 %collective-permute-start.4 = (f32[2,64,128]{2,1,0:T(8,128)S(1)}, f32[2,64,128]{2,1,0:T(8,128)S(1)}, u32[]{:S(2)}, u32[]{:S(2)}) collective-permute-start(f32[2,64,128]{2,1,0:T(8,128)S(1)} %get-tuple-element.25), channel_id=1, source_target_pairs={{0,1},{1,0},{2,3},{3,2},{4,5},{5,4},{6,7},{7,6},{8,9},{9,8},{10,11... | collective-permute-start | bytes 196616 | tf_op jit(solution)/shard_map/ppermute | solution.py:30
  54.3 1.2 %copy-start.1 = (bf16[512,1024]{1,0:T(8,128)(2,1)S(1)}, bf16[512,1024]{1,0:T(8,128)(2,1)}, u32[]{:S(2)}) copy-start(bf16[512,1024]{1,0:T(8,128)(2,1)} %param.8) | copy-start | bytes 3145732
  54.7 3.1 %copy-start.3 = (f32[1088,128]{1,0:T(8,128)}, f32[1088,128]{1,0:T(8,128)S(1)}, u32[]{:S(2)}) copy-start(f32[1088,128]{1,0:T(8,128)S(1)} %convert_reduce_fusion) | copy-start | bytes 1671172
  58.8 10.8 %all-to-all-start.1 = ((f16[16,64,128]{2,1,0:T(8,128)(2,1)}), f16[16,64,128]{2,1,0:T(8,128)(2,1)S(1)}, u32[]{:S(2)}, u32[]{:S(2)}) async-start(f16[16,64,128]{2,1,0:T(8,128)(2,1)} %bitcast.12), calls=%async_computation.1 | async-start | bytes 524288 | tf_op jit(solution)/shard_map/all_to_all | solution.py:102
  62.3 45.0 %copy-start.2 = (bf16[512,1024]{1,0:T(8,128)(2,1)S(1)}, bf16[512,1024]{1,0:T(8,128)(2,1)}, u32[]{:S(2)}) copy-start(bf16[512,1024]{1,0:T(8,128)(2,1)} %param.8) | copy-start | bytes 3145732
  62.3 45.0 %copy-start.7 = (f32[512,256]{1,0:T(8,128)S(1)}, f32[512,256]{1,0:T(8,128)}, u32[]{:S(2)}) copy-start(f32[512,256]{1,0:T(8,128)} %param.9) | copy-start | bytes 1572868
  69.7 4.7 %collective-permute-start.5 = (f16[4,64,128]{2,1,0:T(8,128)(2,1)S(1)}, f16[4,64,128]{2,1,0:T(8,128)(2,1)S(1)}, u32[]{:S(2)}, u32[]{:S(2)}) collective-permute-start(f16[4,64,128]{2,1,0:T(8,128)(2,1)S(1)} %pad_maximum_fusion.2), channel_id=1, source_target_pairs={{0,64},{32,96},{64,0},{96,32},{128,192},{160,224},{192,128},{224,1... | collective-permute-start | bytes 196616 | tf_op jit(solution)/shard_map/ppermute | solution.py:30
  74.5 7.6 %collective-permute-start.6 = (f16[4,64,128]{2,1,0:T(8,128)(2,1)S(1)}, f16[4,64,128]{2,1,0:T(8,128)(2,1)S(1)}, u32[]{:S(2)}, u32[]{:S(2)}) collective-permute-start(f16[4,64,128]{2,1,0:T(8,128)(2,1)S(1)} %pad_maximum_fusion.3), channel_id=1, source_target_pairs={{0,128},{32,160},{64,192},{96,224},{128,0},{160,32},{192,64},{224,... | collective-permute-start | bytes 196616 | tf_op jit(solution)/shard_map/ppermute | solution.py:30
  82.2 4.3 %collective-permute-start.7 = (f16[4,64,128]{2,1,0:T(8,128)(2,1)S(1)}, f16[4,64,128]{2,1,0:T(8,128)(2,1)S(1)}, u32[]{:S(2)}, u32[]{:S(2)}) collective-permute-start(f16[4,64,128]{2,1,0:T(8,128)(2,1)S(1)} %pad_maximum_fusion.4), channel_id=1, source_target_pairs={{0,32},{32,0},{64,96},{96,64},{128,160},{160,128},{192,224},{224,1... | collective-permute-start | bytes 196616 | tf_op jit(solution)/shard_map/ppermute | solution.py:30
  87.4 11.3 %all-to-all-start.2 = ((bf16[16,64,128]{2,1,0:T(8,128)(2,1)}), bf16[16,64,128]{2,1,0:T(8,128)(2,1)S(1)}, u32[]{:S(2)}, u32[]{:S(2)}) async-start(bf16[16,64,128]{2,1,0:T(8,128)(2,1)} %broadcast_in_dim.21), calls=%async_computation.2 | async-start | bytes 524288 | tf_op jit(solution)/shard_map/all_to_all | solution.py:123
  91.4 3.6 %collective-permute-start.8 = (f32[2,64,128]{2,1,0:T(8,128)S(1)}, f32[2,64,128]{2,1,0:T(8,128)S(1)}, u32[]{:S(2)}, u32[]{:S(2)}) collective-permute-start(f32[2,64,128]{2,1,0:T(8,128)S(1)} %pad_maximum_fusion.5), channel_id=1, source_target_pairs={{0,16},{16,0},{1,17},{17,1},{2,18},{18,2},{3,19},{19,3},{4,20},{20... | collective-permute-start | bytes 196616 | tf_op jit(solution)/shard_map/ppermute | solution.py:30
  98.7 8.0 %collective-permute-start.10 = (f32[2,64,128]{2,1,0:T(8,128)S(1)}, f32[2,64,128]{2,1,0:T(8,128)S(1)}, u32[]{:S(2)}, u32[]{:S(2)}) collective-permute-start(f32[2,64,128]{2,1,0:T(8,128)S(1)} %get-tuple-element.23), channel_id=1, source_target_pairs={{0,1},{1,0},{2,3},{3,2},{4,5},{5,4},{6,7},{7,6},{8,9},{9,8},{10,11... | collective-permute-start | bytes 196616 | tf_op jit(solution)/shard_map/ppermute | solution.py:30
  105.8 1.6 %collective-permute-start.9 = (bf16[1024,128]{1,0:T(8,128)(2,1)S(1)}, bf16[1024,128]{1,0:T(8,128)(2,1)S(1)}, u32[]{:S(2)}, u32[]{:S(2)}) collective-permute-start(bf16[1024,128]{1,0:T(8,128)(2,1)S(1)} %bitcast.69), channel_id=1, source_target_pairs={{0,1},{1,0},{2,3},{3,2},{4,5},{5,4},{6,7},{7,6},{8,9},{9,8},{10,11... | collective-permute-start | bytes 786440 | tf_op jit(solution)/shard_map/ppermute | solution.py:30
